TPU v7x, 256 devices: a whole 4x4x8 slice. The times are simulated.
256 devices in a mesh: replica: 32 (over y, x, core), fsdp: 8 (over z).
Axes of the slice: x: 4, y: 4, z: 8, core: 2. Of those that a mesh axis runs over, the one named last changes fastest.
Arguments:
- global_weights: float32 [1024, 8192], P('fsdp')
- replica_weights: bfloat16 [32, 1024, 8192], P('replica', 'fsdp')
- exponents: int32 [32, 1024, 64], P('replica', 'fsdp'), may hold values from -14 to -6, as said below
- momentum: float32 [1024, 8192], P('fsdp', 'replica'), may hold values from -0.4375 to 0.4375
Outputs:
- new_weights: float32 [1024, 8192], P('fsdp')
- new_momentum: float32 [1024, 8192], P('fsdp', 'replica')
Inputs may be any that keep to these rules, and one draw needn't show every extreme that they name: `exponents`: one exponent for each 128 consecutive columns of each replica's row, set by the block's largest magnitude so that most of its entries fit the code range.
All inputs are finite; a program needn't handle non-finite values.
Results may differ from a plain program's by a relative error of at most 0.0003.
Values sent between devices are 32-bit elements; how exact they have to be, the bound alone decides.
No kernel may reach another device: no remote copies, remote signals or barrier semaphores. Data moves between devices by JAX's collectives and lax.ppermute only.
A program may use at most 64 MiB of HBM per device.

v0:
```python
import math

import jax
import jax.numpy as jnp
from jax import lax
from jax.sharding import PartitionSpec as P

BLOCK = 128


FP8_LIMIT = 448.0
CLIP_SCALE = 0.03
OUTER_RATE = 0.7
OUTER_MOMENTUM = 0.9


def per_device(global_weights, replica_weights, exponents, momentum):
    replica_count = lax.axis_size("replica")
    row_count, col_count = global_weights.shape
    block_count = col_count // BLOCK
    own_width = col_count // replica_count
    scaled = exponents[0].astype(jnp.float32)
    powers = jnp.exp2(scaled)
    difference = (global_weights - replica_weights[0].astype(jnp.float32)).reshape(
        row_count, block_count, BLOCK
    )
    encoded = jnp.clip(difference * jnp.exp2(-scaled)[..., None], -FP8_LIMIT, FP8_LIMIT)
    decoded = (encoded * powers[..., None]).reshape(row_count, col_count)
    summed = lax.psum_scatter(decoded, "replica", scatter_dimension=1, tiled=True)
    average = summed / replica_count
    squares = lax.psum(jnp.sum(average * average), ("replica", "fsdp"))
    magnitude = jnp.sqrt(squares)
    threshold = CLIP_SCALE * math.sqrt(row_count * lax.axis_size("fsdp") * col_count)
    factor = jnp.minimum(1.0, threshold / (magnitude + 1e-06))
    outer_grad = average * factor
    new_momentum = OUTER_MOMENTUM * momentum + outer_grad
    own_columns = lax.dynamic_slice_in_dim(
        global_weights, lax.axis_index("replica") * own_width, own_width, 1
    )
    updated = own_columns - OUTER_RATE * (outer_grad + OUTER_MOMENTUM * new_momentum)
    new_weights = lax.all_gather(updated, "replica", axis=1, tiled=True)
    return (new_weights, new_momentum)


def solution(mesh):
    in_specs = (
        P("fsdp", None),
        P("replica", "fsdp", None),
        P("replica", "fsdp", None),
        P("fsdp", "replica"),
    )
    out_specs = (P("fsdp", None), P("fsdp", "replica"))
    return jax.shard_map(
        per_device, mesh=mesh, in_specs=in_specs, out_specs=out_specs, check_vma=False
    )
```

profile of v0, /device:TPU:1, one launch (start us, length us, event | category | flops | bytes accessed | tf_op | source)
XLA Modules:
  0.0 257.1 jit_solution(5180536153711107905)
XLA Ops:
  7.2 0.0 reduce-scatter.2.cloned.1.call-start
  7.2 0.8 exponential_bitcast_fusion.1
  8.0 0.1 copy.6
  8.1 0.1 copy.7
  8.2 0.0 copy-start
  8.2 0.0 copy-start.1
  8.2 1.1 mul.52
  9.4 1.1 mul.49
  10.5 0.0 copy-done
  10.5 0.6 copy-done.1
  11.1 10.0 %bitcast_multiply_fusion = f32[128,8192]{1,0:T(8,128)} fusion(f32[16,8,64,128]{3,2,1,0:T(8,128)S(1)} %bitcast.17, f32[16,8,64,128]{3,2,1,0:T(8,128)S(1)} %bitcast.18, f32[128,8192]{1,0:T(8,128)S(1)} %copy-done, bf16[1,128,8192]{2,1,0:T(8,128)(2,1)S(1)} %copy-done.1), kind=kLoop, calls=%fused_computation | loop fusion | flops 5242880 | bytes 18874368 | tf_op jit(solution)/shard_map/mul | solution.py:28
  21.1 0.0 copy-start.2
  21.1 0.0 reduce-scatter.2.cloned.1.call-update
  21.1 0.0 all-gather.2.cloned.1.call-start
  21.2 91.8 %reduce-scatter.2.cloned.1.call-done = f32[128,256]{1,0:T(8,128)} async-done(((f32[128,8192]{1,0:T(8,128)}), f32[128,256]{1,0:T(8,128)}) %reduce-scatter.2.cloned.1.call-update) | async-done | bytes 131088 | tf_op jit(solution)/shard_map/reduce_scatter | solution.py:29
  113.0 1.5 multiply_reduce_fusion
  114.5 77.2 %psum.7 = f32[]{:T(128)} all-reduce(f32[]{:T(128)} %multiply_reduce_fusion), channel_id=1, replica_groups=mesh['replica'=32,'fsdp'=8] {'replica','fsdp'}, use_global_device_ids=true, to_apply=%region_2.3 | all-reduce | flops 1 | bytes 8 | tf_op jit(solution)/shard_map/psum | solution.py:31
  192.4 0.0 copy-done.2
  192.4 1.7 multiply_subtract_fusion
  194.2 0.0 all-gather.2.cloned.1.call-update
  194.2 51.5 %all-gather.2.cloned.1.call-done = f32[128,8192]{1,0:T(8,128)} async-done(((f32[128,256]{1,0:T(8,128)}), f32[128,8192]{1,0:T(8,128)}) %all-gather.2.cloned.1.call-update) | async-done | bytes 4194320 | tf_op jit(solution)/shard_map/all_gather | solution.py:41
  245.6 4.6 %copy.13 = f32[128,8192]{1,0:T(8,128)} copy(f32[128,8192]{1,0:T(8,128)} %all-gather.2.cloned.1.call-done) | data formatting | bytes 8388608
Async XLA Ops:
  7.2 105.8 %reduce-scatter.2.cloned.1.call-start = ((), (), s32[]{:S(2)}) async-start(), calls=%async_computation.1 | async-start | bytes 4325376 | tf_op jit(solution)/shard_map/reduce_scatter | solution.py:29
  8.2 2.3 copy-start
  8.2 2.9 %copy-start.1 = (bf16[1,128,8192]{2,1,0:T(8,128)(2,1)S(1)}, bf16[1,128,8192]{2,1,0:T(8,128)(2,1)}, u32[]{:S(2)}) copy-start(bf16[1,128,8192]{2,1,0:T(8,128)(2,1)} %param.5) | copy-start | bytes 6291460
  21.1 171.3 %copy-start.2 = (f32[128,256]{1,0:T(8,128)S(1)}, f32[128,256]{1,0:T(8,128)}, u32[]{:S(2)}) copy-start(f32[128,256]{1,0:T(8,128)} %param.7) | copy-start | bytes 393220
  21.1 224.5 %all-gather.2.cloned.1.call-start = ((), (), s32[]{:S(2)}) async-start(), calls=%async_computation.2 | async-start | bytes 4325376 | tf_op jit(solution)/shard_map/all_gather | solution.py:41
Sparse Core Ops, SparseCore 0:
  21.3 91.6 reduce-scatter.1
  194.3 51.3 all-gather.1
where the time goes:
time: 257 us
  waiting for transfers between devices  143 us (56%)
  blocking collectives  77.2 us (30%)
  between operations  14.8 us (6%)
  other arithmetic  14.1 us (5%)
  local copies, waits for them, and re-layouts  7.64 us (3%)
    reduce_scatter x1, waiting for transfers between devices, per_device(): lax.psum_scatter(decoded, 'replica', scatter_dimension=1, tiled=True)  91.8 us
    psum x1, blocking collectives, per_device(): squares = lax.psum(jnp.sum(average * average), ('replica', 'fsdp'))  77.2 us
    all_gather x1, waiting for transfers between devices, per_device(): new_weights = lax.all_gather(updated, 'replica', axis=1, tiled=True)  51.5 us
    mul x1, other arithmetic, per_device(): decoded = (encoded * powers[..., None]).reshape(row_count, col_count)  10 us
    unnamed x7, local copies, waits for them, and re-layouts  5.17 us
  transfers between devices with their start and end apart: 2, of which 2 were waited for; matrix products, arithmetic and copies ran while one was open for 0% of the time, Pallas kernels for 0%

commit v1 on v0

v1 whole, which is shorter than its diff:
```python
import functools
import math

import jax
import jax.numpy as jnp
from jax import lax
from jax.experimental import pallas as pl
from jax.experimental.pallas import tpu as pltpu
from jax.sharding import PartitionSpec as P

BLOCK = 128
SIDE = 4
WIDTH = 256
LOADS = 8
STEPS = (2, 1, 3)

FP8_LIMIT = 448.0
CLIP_SCALE = 0.03
OUTER_RATE = 0.7
OUTER_MOMENTUM = 0.9

VMEM = pl.BlockSpec(memory_space=pltpu.VMEM)
HBM = pl.BlockSpec(memory_space=pltpu.HBM)
SCOPED = 12 * 1024 * 1024


def index_of(y, x, core):
    return (y % SIDE) * 8 + (x % SIDE) * 2 + core


def replica_perm(move):
    return [
        (index_of(y, x, core), index_of(*move(y, x, core)))
        for y in range(SIDE)
        for x in range(SIDE)
        for core in range(2)
    ]


def along_major(move):
    return replica_perm(lambda y, x, c: (y, move(x), c) if c == 0 else (move(y), x, c))


def along_minor(move):
    return replica_perm(lambda y, x, c: (move(y), x, c) if c == 0 else (y, move(x), c))


def major_shift(step):
    return along_major(lambda at: at + step)


def minor_shift(step):
    return along_minor(lambda at: at + step)


CORE_SWAP = replica_perm(lambda y, x, c: (y, x, 1 - c))
EVEN_PAIRS = along_minor(lambda at: at ^ 1)
ODD_PAIRS = along_minor(lambda at: ((at + 3) % 4 ^ 1) + 1)
Z_ROUNDS = [
    [(z, z ^ 1) for z in range(8)],
    [(z, z ^ 2) for z in range(8)],
    [(z, 7 - z) for z in range(8)],
]


def axes_of(me, core):
    x, y = lax.rem(me // 2, SIDE), me // 8
    return jnp.where(core == 0, x, y), jnp.where(core == 0, y, x)


def owner_of(core, major, minor):
    x, y = jnp.where(core == 0, major, minor), jnp.where(core == 0, minor, major)
    return y * 8 + x * 2 + core


def columns_of(owner):
    return pl.ds(pl.multiple_of(owner * WIDTH, WIDTH), WIDTH)


def encode_kernel(weights, local, exponents, momentum, *refs):
    outs, scratch = refs[: 2 * SIDE], refs[2 * SIDE :]
    base, wbuf, lbuf, ebuf, mbuf, limits, wsem, lsem, sem = scratch
    rows = weights.shape[0] // LOADS
    me = lax.axis_index("replica")
    core = lax.rem(me, 2)
    load_exponents = pltpu.make_async_copy(exponents, ebuf, sem.at[0])
    load_exponents.start()
    loads = []
    for n in range(LOADS):
        part = pl.ds(n * rows, rows)
        pair = (
            pltpu.make_async_copy(weights.at[part], wbuf.at[part], wsem.at[n]),
            pltpu.make_async_copy(local.at[part], lbuf.at[part], lsem.at[n]),
        )
        for copy in pair:
            copy.start()
        loads.append(pair)
    load_momentum = pltpu.make_async_copy(momentum, mbuf, sem.at[1])
    load_momentum.start()
    load_exponents.wait()
    tops = (FP8_LIMIT * jnp.exp2(ebuf[...].astype(jnp.float32))).astype(jnp.bfloat16)
    blocks = tops.shape[0]
    row = lax.broadcasted_iota(jnp.int32, (blocks, WIDTH), 0)
    col = lax.broadcasted_iota(jnp.int32, (blocks, WIDTH), 1) // BLOCK
    work = []
    for n, k in enumerate((*STEPS, 0)):
        for keep in range(2):
            for j in range(SIDE):
                target = core if keep else 1 - core
                owner = owner_of(target, lax.rem(axes_of(me, target)[0] + k, SIDE), j)
                pick = jnp.where(row == 2 * owner + col, 1.0, 0.0).astype(jnp.bfloat16)
                limits[len(work)] = lax.dot_general(
                    tops, pick, (((0,), (0,)), ((), ())), preferred_element_type=jnp.float32
                )
                work.append((outs[SIDE * keep + n], j, columns_of(owner)))
    for n in range(LOADS):
        for copy in loads[n]:
            copy.wait()
        part = pl.ds(n * rows, rows)
        for at, (out, slot, columns) in enumerate(work):
            limit = limits[at, part, :]
            difference = wbuf[part, columns] - lbuf[part, columns].astype(jnp.float32)
            out[slot, part, :] = jnp.clip(difference, -limit, limit)
    decay = OUTER_RATE * OUTER_MOMENTUM * OUTER_MOMENTUM
    load_momentum.wait()
    base[...] = wbuf[:, columns_of(me)] - decay * mbuf[...]


def encode(weights, local, exponents, momentum):
    rows, cols = weights.shape
    blocks = [jax.ShapeDtypeStruct((SIDE, rows, WIDTH), jnp.float32)] * SIDE
    outs = pl.pallas_call(
        encode_kernel,
        out_shape=[*blocks, *blocks, jax.ShapeDtypeStruct((rows, WIDTH), jnp.float32)],
        in_specs=[HBM] * 4,
        out_specs=[VMEM] * (2 * SIDE + 1),
        scratch_shapes=[
            pltpu.VMEM((rows, cols), jnp.float32),
            pltpu.VMEM((rows, cols), jnp.bfloat16),
            pltpu.VMEM(exponents.shape, jnp.int32),
            pltpu.VMEM(momentum.shape, jnp.float32),
            pltpu.VMEM((2 * SIDE * SIDE, rows, WIDTH), jnp.float32),
            pltpu.SemaphoreType.DMA((LOADS,)),
            pltpu.SemaphoreType.DMA((LOADS,)),
            pltpu.SemaphoreType.DMA((2,)),
        ],
        compiler_params=pltpu.CompilerParams(vmem_limit_bytes=SCOPED),
        cost_estimate=pl.CostEstimate(flops=2**22, bytes_accessed=6 * 2**20, transcendentals=0),
        name="encode",
    )(*(pltpu.with_memory_space_constraint(x, pltpu.HBM) for x in (weights, local, exponents, momentum)))
    return outs[:SIDE], outs[SIDE : 2 * SIDE], outs[2 * SIDE]


def squares_kernel(values, out):
    total = None
    for r in range(0, values.shape[0], 8):
        value = values[r : r + 8, :]
        total = value * value if total is None else total + value * value
    out[...] = total


def sum_squares(values):
    return pl.pallas_call(
        squares_kernel,
        out_shape=jax.ShapeDtypeStruct((8, WIDTH), jnp.float32),
        in_specs=[VMEM],
        out_specs=VMEM,
        compiler_params=pltpu.CompilerParams(vmem_limit_bytes=SCOPED),
        cost_estimate=pl.CostEstimate(flops=2**18, bytes_accessed=2**12, transcendentals=0),
        name="squares",
    )(values)


def update_kernel(threshold, *refs):
    mine, handed, (momentum, new_momentum, out, buf, sem) = refs[:5], refs[5:13], refs[13:]
    rows = momentum.shape[0]
    size, half = SIDE * rows, rows // 2
    me = lax.axis_index("replica")
    core = lax.rem(me, 2)
    squares = mine[-1][size:, :] + handed[-1][size:, :]
    magnitude = jnp.sqrt(jnp.sum(squares, axis=(0, 1), keepdims=True))
    factor = jnp.minimum(1.0, threshold / (magnitude + 1e-06))
    rate = OUTER_RATE * (1.0 + OUTER_MOMENTUM) * factor
    own = [(k, mine[n], 0, mine[n], size) for n, k in enumerate((0, 1, 3))]
    own.append((2, mine[3], 0, mine[4], 0))
    other = [(k, handed[2 * n], 0, handed[2 * n + 1], 0) for n, k in enumerate((0, 1, 3, 2))]
    copies = []
    for side, sources in ((core, own), (1 - core, other)):
        major, minor = axes_of(me, side)
        for k, averages, first, bases, offset in sources:
            place = lax.rem(major + SIDE - k, SIDE)
            for j in range(SIDE):
                apart = minor ^ j
                low = jnp.where(apart < 2, apart, 5 - apart)
                high = jnp.where(apart == 0, 0, lax.rem(apart, SIDE - 1) + 1)
                at = len(copies)
                for n, slot in enumerate((low, SIDE + high)):
                    base = pl.ds(pl.multiple_of(offset + slot * half, half), half)
                    average = averages[first + j * rows + n * half : first + j * rows + (n + 1) * half, :]
                    buf[at, n * half : (n + 1) * half, :] = bases[base, :] - rate * average
                columns = columns_of(owner_of(side, place, j))
                copy = pltpu.make_async_copy(buf.at[at], out.at[:, columns], sem.at[at])
                copy.start()
                copies.append(copy)
    here = pl.ds(pl.multiple_of(axes_of(me, core)[1] * rows, rows), rows)
    new_momentum[...] = OUTER_MOMENTUM * momentum[...] + factor * mine[0][here, :]
    for copy in copies:
        copy.wait()


def update(cols, threshold, mine, handed, momentum):
    rows = momentum.shape[0]
    chunks = 2 * SIDE * SIDE
    return pl.pallas_call(
        functools.partial(update_kernel, threshold),
        out_shape=[
            jax.ShapeDtypeStruct((rows, WIDTH), jnp.float32),
            jax.ShapeDtypeStruct((rows, cols), jnp.float32),
        ],
        in_specs=[VMEM] * (len(mine) + len(handed) + 1),
        out_specs=[VMEM, HBM],
        scratch_shapes=[
            pltpu.VMEM((chunks, rows, WIDTH), jnp.float32),
            pltpu.SemaphoreType.DMA((chunks,)),
        ],
        compiler_params=pltpu.CompilerParams(vmem_limit_bytes=SCOPED),
        cost_estimate=pl.CostEstimate(flops=2**21, bytes_accessed=2**22, transcendentals=0),
        name="update",
    )(*mine, *handed, momentum)


def tie(*values):
    return lax.optimization_barrier(values)


def per_device(global_weights, replica_weights, exponents, momentum):
    replica_count = lax.axis_size("replica")
    row_count, col_count = global_weights.shape
    threshold = CLIP_SCALE * math.sqrt(row_count * lax.axis_size("fsdp") * col_count)
    up, down = major_shift(1), major_shift(-1)

    def move(value, perm):
        return lax.ppermute(value, "replica", perm)

    with jax.named_scope("core_sum"):
        send, keep, base = encode(global_weights, replica_weights[0], exponents[0].T, momentum)
        parts = [kept + move(sent, CORE_SWAP) for sent, kept in zip(send, keep)]

    with jax.named_scope("major_sum"):
        arrived = [move(part, major_shift(k)) for part, k in zip(parts, STEPS)]
        total = parts[SIDE - 1] + arrived[0] + arrived[1] + arrived[2]
        low, high = total[:2], total[2:]

    with jax.named_scope("minor_sum"):
        size = low.shape[0] * row_count
        low, high = low.reshape(size, WIDTH), high.reshape(size, WIDTH)
        low_base, high_base = base[: row_count // 2], base[row_count // 2 :]
        for low_perm, high_perm in ((EVEN_PAIRS, ODD_PAIRS), (ODD_PAIRS, EVEN_PAIRS)):
            low_moved = move(jnp.concatenate([low, low_base]), low_perm)
            high_moved = move(jnp.concatenate([high, high_base]), high_perm)
            low, low_base = low + low_moved[:size], jnp.concatenate([low_base, low_moved[size:]])
            high, high_base = high + high_moved[:size], jnp.concatenate([high_base, high_moved[size:]])
        averages = jnp.concatenate([low, high]) / replica_count
        mine = jnp.concatenate([averages, low_base, high_base])
        middle = averages.shape[0]

    with jax.named_scope("square_sum"):
        squares = sum_squares(averages)
        squares = squares + lax.ppermute(squares, "fsdp", Z_ROUNDS[0])
        for perm in Z_ROUNDS[1:]:
            squares = squares + lax.ppermute(squares, "fsdp", perm)

    with jax.named_scope("major_gather"):
        below, above = move(mine, up), move(mine, down)

    with jax.named_scope("major_forward"):
        below, above, squares = tie(below, above, squares)
        far_low = move(jnp.concatenate([below[:middle], squares]), up)
        far_high = move(jnp.concatenate([above[middle:], squares]), down)

    with jax.named_scope("core_gather"):
        whole = tie(mine, squares)[0], below, above
        near = [move(part, CORE_SWAP) for x in whole for part in (x[:middle], x[middle:])]

    with jax.named_scope("square_sum"):
        across = move(squares, major_shift(2))
        far_low, far_high, near = tie(far_low, far_high, near)
        squares = squares + across + far_low[middle:] + far_high[middle:]

    with jax.named_scope("update"):
        (far_low,) = tie(far_low[:middle])
        far_high = jnp.concatenate([far_high[:middle], squares])
        handed = [*near, move(far_low, CORE_SWAP), move(far_high, CORE_SWAP)]
        new_momentum, new_weights = update(
            col_count, threshold, [mine, below, above, far_low, far_high], handed, momentum
        )
    return (new_weights, new_momentum)


def solution(mesh):
    in_specs = (
        P("fsdp", None),
        P("replica", "fsdp", None),
        P("replica", "fsdp", None),
        P("fsdp", "replica"),
    )
    out_specs = (P("fsdp", None), P("fsdp", "replica"))
    return jax.shard_map(
        per_device, mesh=mesh, in_specs=in_specs, out_specs=out_specs, check_vma=False
    )
```

time: 257 us -> 84 us (0.33)
  waiting for transfers between devices: 143 us -> 38.6 us
  blocking collectives: 77.2 us -> 0 us
  starting transfers between devices: 0.08 us -> 35.9 us
  between operations: 14.8 us -> 1.04 us
  other arithmetic: 14.1 us -> 0.86 us
  local copies, waits for them, and re-layouts: 7.64 us -> 0.39 us
  Pallas kernels: 0 us -> 7.12 us
    reduce_scatter x1 -> x0, waiting for transfers between devices: 91.8 us -> none  [per_device(): lax.psum_scatter(decoded, 'replica', scatter_dimension=1, tiled=True)]
    psum x1 -> x0, blocking collectives: 77.2 us -> none  [per_device(): squares = lax.psum(jnp.sum(average * average), ('replica', 'fsdp'))]
    all_gather x1 -> x0, waiting for transfers between devices: 51.5 us -> none  [per_device(): new_weights = lax.all_gather(updated, 'replica', axis=1, tiled=True)]
    ppermute x0 -> x27, waiting for transfers between devices: none -> 38.6 us  [the longest x24 35.2 us: move(): return lax.ppermute(value, 'replica', perm)]
    ppermute x0 -> x27, starting transfers between devices: none -> 35.9 us  [the longest x24 26.4 us: move(): return lax.ppermute(value, 'replica', perm)]
    mul x1 -> x0, other arithmetic: 10 us -> none  [per_device(): decoded = (encoded * powers[..., None]).reshape(row_count, col_count)]
    pallas_call x0 -> x3, Pallas kernels: none -> 7.12 us  [the longest x1 3.98 us: encode(): pl.pallas_call(encode_kernel, out_shape=[*blocks, *blocks, jax.ShapeDtype...]
    unnamed x7, local copies, waits for them, and re-layouts: 5.17 us -> 0.05 us
  transfers between devices with their start and end apart: 2 -> 27, of which waited for: 2 -> 15; matrix products, arithmetic and copies ran while one was open for 0% -> 1% of each run, Pallas kernels for 0% -> 0%
where the time goes in v1:
time: 84 us; the launch traced here: 83.9 us
  waiting for transfers between devices  38.6 us (46%)
  starting transfers between devices  35.9 us (43%)
  Pallas kernels  7.12 us (8%)
  between operations  1.04 us (1%)
  other arithmetic  0.86 us (1%)
    ppermute x24, waiting for transfers between devices, move(): return lax.ppermute(value, 'replica', perm)  35.2 us
    ppermute x24, starting transfers between devices, move(): return lax.ppermute(value, 'replica', perm)  26.4 us
    ppermute x2, starting transfers between devices, per_device(): squares = squares + lax.ppermute(squares, 'fsdp', perm)  7.76 us
    pallas_call x1, Pallas kernels, encode(): pl.pallas_call(encode_kernel, out_shape=[*blocks, *blocks, jax.ShapeDtype...  3.98 us
    pallas_call x1, Pallas kernels, update(): pl.pallas_call(functools.partial(update_kernel, threshold), out_shape=[ja...  3.07 us
    ppermute x2, waiting for transfers between devices, per_device(): squares = squares + lax.ppermute(squares, 'fsdp', perm)  2.37 us
    ppermute x1, starting transfers between devices, per_device(): squares = squares + lax.ppermute(squares, 'fsdp', Z_ROUNDS[0])  1.72 us
  transfers between devices with their start and end apart: 27, of which 15 were waited for; matrix products, arithmetic and copies ran while one was open for 1% of the time, Pallas kernels for 0%

profile of v1, /device:TPU:1, one launch (start us, length us, event | category | flops | bytes accessed | tf_op | source)
XLA Modules:
  0.0 83.9 jit_solution(17536612659145553221)
XLA Ops:
  0.6 4.0 %encode.1 = (f32[4,128,256]{2,1,0:T(8,128)S(1)}, f32[4,128,256]{2,1,0:T(8,128)S(1)}, f32[4,128,256]{2,1,0:T(8,128)S(1)}, f32[4,128,256]{2,1,0:T(8,128)S(1)}, f32...) custom-call(f32[128,8192]{1,0:T(8,128)} %weights.1, ...), custom_call_target="tpu_custom_call" | custom-call | flops 4194304 | bytes 6291456 | tf_op jit(solution)/shard_map/core_sum/encode/pallas_call | solution.py:132
  4.6 3.3 %collective-permute-start.1 = (f32[4,128,256]{2,1,0:T(8,128)S(1)}, f32[4,128,256]{2,1,0:T(8,128)S(1)}, u32[]{:S(2)}, u32[]{:S(2)}) collective-permute-start(f32[4,128,256]{2,1,0:T(8,128)S(1)} %get-tuple-element.28), channel_id=1, source_target_pairs={{0,8},{8,0},{16,24},{24,16},{32,40},{40,32},{48,56},{56,48},{64,72... | collective-permute-start | bytes 1572872 | tf_op jit(solution)/shard_map/core_sum/ppermute | solution.py:243
  7.9 0.1 collective-permute-start.3
  8.0 0.4 collective-permute-start.5
  8.5 0.1 collective-permute-start
  8.6 0.9 %collective-permute-done.1 = f32[4,128,256]{2,1,0:T(8,128)S(1)} collective-permute-done((f32[4,128,256]{2,1,0:T(8,128)S(1)}, f32[4,128,256]{2,1,0:T(8,128)S(1)}, u32[]{:S(2)}, u32[]{:S(2)}) %collective-permute-start.1) | collective-permute-done | bytes 524320 | tf_op jit(solution)/shard_map/core_sum/ppermute | solution.py:243
  9.5 0.1 add.52
  9.5 1.3 %collective-permute-start.2 = (f32[4,128,256]{2,1,0:T(8,128)S(1)}, f32[4,128,256]{2,1,0:T(8,128)S(1)}, u32[]{:S(2)}, u32[]{:S(2)}) collective-permute-start(f32[4,128,256]{2,1,0:T(8,128)S(1)} %add.52), channel_id=1, source_target_pairs={{0,32},{8,136},{16,48},{24,152},{32,0},{40,168},{48,16},{56,184},{... | collective-permute-start | bytes 1572872 | tf_op jit(solution)/shard_map/major_sum/ppermute | solution.py:243
  10.8 0.0 collective-permute-done.3
  10.8 0.1 add.54
  10.9 0.5 collective-permute-start.4
  11.4 0.0 collective-permute-done.5
  11.4 0.1 add.56
  11.4 2.4 %collective-permute-start.6 = (f32[4,128,256]{2,1,0:T(8,128)S(1)}, f32[4,128,256]{2,1,0:T(8,128)S(1)}, u32[]{:S(2)}, u32[]{:S(2)}) collective-permute-start(f32[4,128,256]{2,1,0:T(8,128)S(1)} %add.56), channel_id=1, source_target_pairs={{0,48},{8,200},{16,0},{24,216},{32,16},{40,232},{48,32},{56,248},{... | collective-permute-start | bytes 1572872 | tf_op jit(solution)/shard_map/major_sum/ppermute | solution.py:243
  13.8 0.0 collective-permute-done
  13.8 5.7 %collective-permute-done.2 = f32[4,128,256]{2,1,0:T(8,128)S(1)} collective-permute-done((f32[4,128,256]{2,1,0:T(8,128)S(1)}, f32[4,128,256]{2,1,0:T(8,128)S(1)}, u32[]{:S(2)}, u32[]{:S(2)}) %collective-permute-start.2) | collective-permute-done | bytes 524320 | tf_op jit(solution)/shard_map/major_sum/ppermute | solution.py:243
  19.5 5.6 %collective-permute-done.4 = f32[4,128,256]{2,1,0:T(8,128)S(1)} collective-permute-done((f32[4,128,256]{2,1,0:T(8,128)S(1)}, f32[4,128,256]{2,1,0:T(8,128)S(1)}, u32[]{:S(2)}, u32[]{:S(2)}) %collective-permute-start.4) | collective-permute-done | bytes 524320 | tf_op jit(solution)/shard_map/major_sum/ppermute | solution.py:243
  25.1 0.0 collective-permute-done.6
  25.1 0.2 add_add_fusion
  25.3 1.2 %collective-permute-start.9 = (f32[320,256]{1,0:T(8,128)S(1)}, f32[320,256]{1,0:T(8,128)S(1)}, u32[]{:S(2)}, u32[]{:S(2)}) collective-permute-start(f32[320,256]{1,0:T(8,128)S(1)} %pad_maximum_fusion.6), channel_id=1, source_target_pairs={{0,192},{8,56},{16,208},{24,40},{32,224},{40,24},{48,240},{56,8},{... | collective-permute-start | bytes 983048 | tf_op jit(solution)/shard_map/minor_sum/ppermute | solution.py:243
  26.6 0.1 collective-permute-start.7
  26.7 6.2 %collective-permute-done.9 = f32[320,256]{1,0:T(8,128)S(1)} collective-permute-done((f32[320,256]{1,0:T(8,128)S(1)}, f32[320,256]{1,0:T(8,128)S(1)}, u32[]{:S(2)}, u32[]{:S(2)}) %collective-permute-start.9) | collective-permute-done | bytes 327712 | tf_op jit(solution)/shard_map/minor_sum/ppermute | solution.py:243
  32.9 0.1 collective-permute-start.10
  33.0 0.0 collective-permute-done.7
  33.1 1.5 %collective-permute-start.8 = (f32[384,256]{1,0:T(8,128)S(1)}, f32[384,256]{1,0:T(8,128)S(1)}, u32[]{:S(2)}, u32[]{:S(2)}) collective-permute-start(f32[384,256]{1,0:T(8,128)S(1)} %pad_maximum_fusion.3), channel_id=1, source_target_pairs={{0,192},{8,56},{16,208},{24,40},{32,224},{40,24},{48,240},{56,8},{... | collective-permute-start | bytes 1179656 | tf_op jit(solution)/shard_map/minor_sum/ppermute | solution.py:243
  34.6 5.3 %collective-permute-done.10 = f32[384,256]{1,0:T(8,128)S(1)} collective-permute-done((f32[384,256]{1,0:T(8,128)S(1)}, f32[384,256]{1,0:T(8,128)S(1)}, u32[]{:S(2)}, u32[]{:S(2)}) %collective-permute-start.10) | collective-permute-done | bytes 393248 | tf_op jit(solution)/shard_map/minor_sum/ppermute | solution.py:243
  40.0 1.4 %collective-permute-done.8 = f32[384,256]{1,0:T(8,128)S(1)} collective-permute-done((f32[384,256]{1,0:T(8,128)S(1)}, f32[384,256]{1,0:T(8,128)S(1)}, u32[]{:S(2)}, u32[]{:S(2)}) %collective-permute-start.8) | collective-permute-done | bytes 393248 | tf_op jit(solution)/shard_map/minor_sum/ppermute | solution.py:243
  41.4 0.1 maximum_multiply_fusion
  41.6 2.2 %collective-permute-start.12 = (f32[1024,256]{1,0:T(8,128)S(1)}, f32[1024,256]{1,0:T(8,128)S(1)}, u32[]{:S(2)}, u32[]{:S(2)}) collective-permute-start(f32[1024,256]{1,0:T(8,128)S(1)} %slice_dynamic-update-slice_fusion.refs_0_), channel_id=1, source_target_pairs={{0,48},{8,200},{16,0},{24,216},{32,16},{40,232},{48,32},{56,248},{... | collective-permute-start | bytes 3145736 | tf_op jit(solution)/shard_map/major_gather/ppermute | solution.py:243
  43.8 0.0 collective-permute-start.11
  43.8 0.1 squares.1
  43.9 1.7 %collective-permute-start.13 = (f32[8,256]{1,0:T(8,128)S(1)}, f32[8,256]{1,0:T(8,128)S(1)}, u32[]{:S(2)}, u32[]{:S(2)}) collective-permute-start(f32[8,256]{1,0:T(8,128)S(1)} %squares.1), channel_id=1, source_target_pairs={{0,1},{1,0},{2,3},{3,2},{4,5},{5,4},{6,7},{7,6},{8,9},{9,8},{10,11... | collective-permute-start | bytes 24584 | tf_op jit(solution)/shard_map/square_sum/ppermute | solution.py:269
  45.6 1.0 %collective-permute-done.13 = f32[8,256]{1,0:T(8,128)S(1)} collective-permute-done((f32[8,256]{1,0:T(8,128)S(1)}, f32[8,256]{1,0:T(8,128)S(1)}, u32[]{:S(2)}, u32[]{:S(2)}) %collective-permute-start.13) | collective-permute-done | bytes 8224 | tf_op jit(solution)/shard_map/square_sum/ppermute | solution.py:269
  46.7 3.0 %collective-permute-start.14 = (f32[8,256]{1,0:T(8,128)S(1)}, f32[8,256]{1,0:T(8,128)S(1)}, u32[]{:S(2)}, u32[]{:S(2)}) collective-permute-start(f32[8,256]{1,0:T(8,128)S(1)} %add.62), channel_id=1, source_target_pairs={{0,2},{1,3},{2,0},{3,1},{4,6},{5,7},{6,4},{7,5},{8,10},{9,11},{10,... | collective-permute-start | bytes 24584 | tf_op jit(solution)/shard_map/square_sum/ppermute | solution.py:271
  49.7 1.0 %collective-permute-done.14 = f32[8,256]{1,0:T(8,128)S(1)} collective-permute-done((f32[8,256]{1,0:T(8,128)S(1)}, f32[8,256]{1,0:T(8,128)S(1)}, u32[]{:S(2)}, u32[]{:S(2)}) %collective-permute-start.14) | collective-permute-done | bytes 8224 | tf_op jit(solution)/shard_map/square_sum/ppermute | solution.py:271
  50.7 4.8 %collective-permute-start.15 = (f32[8,256]{1,0:T(8,128)S(1)}, f32[8,256]{1,0:T(8,128)S(1)}, u32[]{:S(2)}, u32[]{:S(2)}) collective-permute-start(f32[8,256]{1,0:T(8,128)S(1)} %add.63), channel_id=1, source_target_pairs={{0,7},{1,6},{2,5},{3,4},{4,3},{5,2},{6,1},{7,0},{8,15},{9,14},{10,... | collective-permute-start | bytes 24584 | tf_op jit(solution)/shard_map/square_sum/ppermute | solution.py:271
  55.5 1.3 %collective-permute-done.15 = f32[8,256]{1,0:T(8,128)S(1)} collective-permute-done((f32[8,256]{1,0:T(8,128)S(1)}, f32[8,256]{1,0:T(8,128)S(1)}, u32[]{:S(2)}, u32[]{:S(2)}) %collective-permute-start.15) | collective-permute-done | bytes 8224 | tf_op jit(solution)/shard_map/square_sum/ppermute | solution.py:271
  56.8 0.0 collective-permute-done.12.refs_2_
  56.8 2.2 %collective-permute-done.11.refs_1_ = f32[1024,256]{1,0:T(8,128)S(1)} collective-permute-done((f32[1024,256]{1,0:T(8,128)S(1)}, f32[1024,256]{1,0:T(8,128)S(1)}, u32[]{:S(2)}, u32[]{:S(2)}) %collective-permute-start.11) | collective-permute-done | bytes 1048608 | tf_op jit(solution)/shard_map/major_gather/ppermute | solution.py:243
  59.0 0.1 fusion.2
  59.1 4.4 %collective-permute-start.19 = (f32[512,256]{1,0:T(8,128)S(1)}, f32[512,256]{1,0:T(8,128)S(1)}, u32[]{:S(2)}, u32[]{:S(2)}) collective-permute-start(f32[512,256]{1,0:T(8,128)S(1)} %get-tuple-element.52), channel_id=1, source_target_pairs={{0,8},{8,0},{16,24},{24,16},{32,40},{40,32},{48,56},{56,48},{64,72... | collective-permute-start | bytes 1572872 | tf_op jit(solution)/shard_map/core_gather/ppermute | solution.py:243
  63.5 0.1 collective-permute-start.18
  63.6 0.1 fusion.1
  63.7 0.0 copy-start
  63.7 0.5 collective-permute-start.21
  64.2 0.1 fusion
  64.2 0.1 pad_maximum_fusion
  64.4 1.1 %collective-permute-start.17 = (f32[520,256]{1,0:T(8,128)S(1)}, f32[520,256]{1,0:T(8,128)S(1)}, u32[]{:S(2)}, u32[]{:S(2)}) collective-permute-start(f32[520,256]{1,0:T(8,128)S(1)} %get-tuple-element.60), channel_id=1, source_target_pairs={{0,48},{8,200},{16,0},{24,216},{32,16},{40,232},{48,32},{56,248},{... | collective-permute-start | bytes 1597448 | tf_op jit(solution)/shard_map/major_forward/ppermute | solution.py:243
  65.5 0.5 collective-permute-start.16
  65.9 0.0 collective-permute-done.19.refs_6_
  65.9 1.7 %collective-permute-start.20 = (f32[512,256]{1,0:T(8,128)S(1)}, f32[512,256]{1,0:T(8,128)S(1)}, u32[]{:S(2)}, u32[]{:S(2)}) collective-permute-start(f32[512,256]{1,0:T(8,128)S(1)} %get-tuple-element.51), channel_id=1, source_target_pairs={{0,8},{8,0},{16,24},{24,16},{32,40},{40,32},{48,56},{56,48},{64,72... | collective-permute-start | bytes 1572872 | tf_op jit(solution)/shard_map/core_gather/ppermute | solution.py:243
  67.6 0.1 collective-permute-start.22
  67.7 0.4 collective-permute-start.23
  68.2 1.0 %collective-permute-done.20.refs_7_ = f32[512,256]{1,0:T(8,128)S(1)} collective-permute-done((f32[512,256]{1,0:T(8,128)S(1)}, f32[512,256]{1,0:T(8,128)S(1)}, u32[]{:S(2)}, u32[]{:S(2)}) %collective-permute-start.20) | collective-permute-done | bytes 524320 | tf_op jit(solution)/shard_map/core_gather/ppermute | solution.py:243
  69.2 1.2 %collective-permute-start.24 = (f32[8,256]{1,0:T(8,128)S(1)}, f32[8,256]{1,0:T(8,128)S(1)}, u32[]{:S(2)}, u32[]{:S(2)}) collective-permute-start(f32[8,256]{1,0:T(8,128)S(1)} %add.64), channel_id=1, source_target_pairs={{0,32},{8,136},{16,48},{24,152},{32,0},{40,168},{48,16},{56,184},{... | collective-permute-start | bytes 24584 | tf_op jit(solution)/shard_map/square_sum/ppermute | solution.py:243
  70.4 0.3 collective-permute-done.23.refs_10_
  70.7 2.2 %collective-permute-done.17 = f32[520,256]{1,0:T(8,128)S(1)} collective-permute-done((f32[520,256]{1,0:T(8,128)S(1)}, f32[520,256]{1,0:T(8,128)S(1)}, u32[]{:S(2)}, u32[]{:S(2)}) %collective-permute-start.17) | collective-permute-done | bytes 532512 | tf_op jit(solution)/shard_map/major_forward/ppermute | solution.py:243
  72.8 2.3 %collective-permute-done.16 = f32[520,256]{1,0:T(8,128)S(1)} collective-permute-done((f32[520,256]{1,0:T(8,128)S(1)}, f32[520,256]{1,0:T(8,128)S(1)}, u32[]{:S(2)}, u32[]{:S(2)}) %collective-permute-start.16) | collective-permute-done | bytes 532512 | tf_op jit(solution)/shard_map/major_forward/ppermute | solution.py:243
  75.2 0.0 collective-permute-done.24
  75.3 3.1 %collective-permute-start.26 = (f32[520,256]{1,0:T(8,128)S(1)}, f32[520,256]{1,0:T(8,128)S(1)}, u32[]{:S(2)}, u32[]{:S(2)}) collective-permute-start(f32[520,256]{1,0:T(8,128)S(1)} %pad_maximum_fusion.2.refs_4_), channel_id=1, source_target_pairs={{0,8},{8,0},{16,24},{24,16},{32,40},{40,32},{48,56},{56,48},{64,72... | collective-permute-start | bytes 1597448 | tf_op jit(solution)/shard_map/update/ppermute | solution.py:243
  78.4 0.1 collective-permute-start.25
  78.5 2.2 %collective-permute-done.25.refs_11_ = f32[512,256]{1,0:T(8,128)S(1)} collective-permute-done((f32[512,256]{1,0:T(8,128)S(1)}, f32[512,256]{1,0:T(8,128)S(1)}, u32[]{:S(2)}, u32[]{:S(2)}) %collective-permute-start.25) | collective-permute-done | bytes 524320 | tf_op jit(solution)/shard_map/update/ppermute | solution.py:243
  80.7 0.0 collective-permute-done.26.refs_12_
  80.7 3.1 %update.1 = (f32[128,256]{1,0:T(8,128)}, f32[128,8192]{1,0:T(8,128)}) custom-call(f32[1024,256]{1,0:T(8,128)S(1)} %slice_dynamic-update-slice_fusion.refs_0_, f32[1024,256]{1,0:T(8,128)S(1)} %collective-permute-done.11.refs_1_, f32[1024,256]{1,0:T(8,128)S(1)} %collective-permute-done.12.refs_2_, f32[512,256]{1,0:T(8,128)S(1)} %slice.86.refs_3_, ...), custom_call_target="tpu_custom_call" | custom-call | flops 2097152 | bytes 4194304 | tf_op jit(solution)/shard_map/update/update/pallas_call | solution.py:214
  (29 shorter events, 0.5 us)
Async XLA Ops:
  4.6 4.9 %collective-permute-start.1 = (f32[4,128,256]{2,1,0:T(8,128)S(1)}, f32[4,128,256]{2,1,0:T(8,128)S(1)}, u32[]{:S(2)}, u32[]{:S(2)}) collective-permute-start(f32[4,128,256]{2,1,0:T(8,128)S(1)} %get-tuple-element.28), channel_id=1, source_target_pairs={{0,8},{8,0},{16,24},{24,16},{32,40},{40,32},{48,56},{56,48},{64,72... | collective-permute-start | bytes 1572872 | tf_op jit(solution)/shard_map/core_sum/ppermute | solution.py:243
  7.9 2.9 %collective-permute-start.3 = (f32[4,128,256]{2,1,0:T(8,128)S(1)}, f32[4,128,256]{2,1,0:T(8,128)S(1)}, u32[]{:S(2)}, u32[]{:S(2)}) collective-permute-start(f32[4,128,256]{2,1,0:T(8,128)S(1)} %get-tuple-element.30), channel_id=1, source_target_pairs={{0,8},{8,0},{16,24},{24,16},{32,40},{40,32},{48,56},{56,48},{64,72... | collective-permute-start | bytes 1572872 | tf_op jit(solution)/shard_map/core_sum/ppermute | solution.py:243
  8.0 3.3 %collective-permute-start.5 = (f32[4,128,256]{2,1,0:T(8,128)S(1)}, f32[4,128,256]{2,1,0:T(8,128)S(1)}, u32[]{:S(2)}, u32[]{:S(2)}) collective-permute-start(f32[4,128,256]{2,1,0:T(8,128)S(1)} %get-tuple-element.32), channel_id=1, source_target_pairs={{0,8},{8,0},{16,24},{24,16},{32,40},{40,32},{48,56},{56,48},{64,72... | collective-permute-start | bytes 1572872 | tf_op jit(solution)/shard_map/core_sum/ppermute | solution.py:243
  8.5 5.4 %collective-permute-start = (f32[4,128,256]{2,1,0:T(8,128)S(1)}, f32[4,128,256]{2,1,0:T(8,128)S(1)}, u32[]{:S(2)}, u32[]{:S(2)}) collective-permute-start(f32[4,128,256]{2,1,0:T(8,128)S(1)} %get-tuple-element.26), channel_id=1, source_target_pairs={{0,8},{8,0},{16,24},{24,16},{32,40},{40,32},{48,56},{56,48},{64,72... | collective-permute-start | bytes 1572872 | tf_op jit(solution)/shard_map/core_sum/ppermute | solution.py:243
  9.5 10.0 %collective-permute-start.2 = (f32[4,128,256]{2,1,0:T(8,128)S(1)}, f32[4,128,256]{2,1,0:T(8,128)S(1)}, u32[]{:S(2)}, u32[]{:S(2)}) collective-permute-start(f32[4,128,256]{2,1,0:T(8,128)S(1)} %add.52), channel_id=1, source_target_pairs={{0,32},{8,136},{16,48},{24,152},{32,0},{40,168},{48,16},{56,184},{... | collective-permute-start | bytes 1572872 | tf_op jit(solution)/shard_map/major_sum/ppermute | solution.py:243
  10.9 14.2 %collective-permute-start.4 = (f32[4,128,256]{2,1,0:T(8,128)S(1)}, f32[4,128,256]{2,1,0:T(8,128)S(1)}, u32[]{:S(2)}, u32[]{:S(2)}) collective-permute-start(f32[4,128,256]{2,1,0:T(8,128)S(1)} %add.54), channel_id=1, source_target_pairs={{0,16},{8,72},{16,32},{24,88},{32,48},{40,104},{48,0},{56,120},{64... | collective-permute-start | bytes 1572872 | tf_op jit(solution)/shard_map/major_sum/ppermute | solution.py:243
  11.4 13.6 %collective-permute-start.6 = (f32[4,128,256]{2,1,0:T(8,128)S(1)}, f32[4,128,256]{2,1,0:T(8,128)S(1)}, u32[]{:S(2)}, u32[]{:S(2)}) collective-permute-start(f32[4,128,256]{2,1,0:T(8,128)S(1)} %add.56), channel_id=1, source_target_pairs={{0,48},{8,200},{16,0},{24,216},{32,16},{40,232},{48,32},{56,248},{... | collective-permute-start | bytes 1572872 | tf_op jit(solution)/shard_map/major_sum/ppermute | solution.py:243
  25.3 7.5 %collective-permute-start.9 = (f32[320,256]{1,0:T(8,128)S(1)}, f32[320,256]{1,0:T(8,128)S(1)}, u32[]{:S(2)}, u32[]{:S(2)}) collective-permute-start(f32[320,256]{1,0:T(8,128)S(1)} %pad_maximum_fusion.6), channel_id=1, source_target_pairs={{0,192},{8,56},{16,208},{24,40},{32,224},{40,24},{48,240},{56,8},{... | collective-permute-start | bytes 983048 | tf_op jit(solution)/shard_map/minor_sum/ppermute | solution.py:243
  26.6 6.5 %collective-permute-start.7 = (f32[320,256]{1,0:T(8,128)S(1)}, f32[320,256]{1,0:T(8,128)S(1)}, u32[]{:S(2)}, u32[]{:S(2)}) collective-permute-start(f32[320,256]{1,0:T(8,128)S(1)} %pad_maximum_fusion.5), channel_id=1, source_target_pairs={{0,64},{8,24},{16,80},{24,8},{32,96},{40,56},{48,112},{56,40},{64,... | collective-permute-start | bytes 983048 | tf_op jit(solution)/shard_map/minor_sum/ppermute | solution.py:243
  32.9 7.0 %collective-permute-start.10 = (f32[384,256]{1,0:T(8,128)S(1)}, f32[384,256]{1,0:T(8,128)S(1)}, u32[]{:S(2)}, u32[]{:S(2)}) collective-permute-start(f32[384,256]{1,0:T(8,128)S(1)} %pad_maximum_fusion.4), channel_id=1, source_target_pairs={{0,64},{8,24},{16,80},{24,8},{32,96},{40,56},{48,112},{56,40},{64,... | collective-permute-start | bytes 1179656 | tf_op jit(solution)/shard_map/minor_sum/ppermute | solution.py:243
  33.1 8.2 %collective-permute-start.8 = (f32[384,256]{1,0:T(8,128)S(1)}, f32[384,256]{1,0:T(8,128)S(1)}, u32[]{:S(2)}, u32[]{:S(2)}) collective-permute-start(f32[384,256]{1,0:T(8,128)S(1)} %pad_maximum_fusion.3), channel_id=1, source_target_pairs={{0,192},{8,56},{16,208},{24,40},{32,224},{40,24},{48,240},{56,8},{... | collective-permute-start | bytes 1179656 | tf_op jit(solution)/shard_map/minor_sum/ppermute | solution.py:243
  41.6 15.2 %collective-permute-start.12 = (f32[1024,256]{1,0:T(8,128)S(1)}, f32[1024,256]{1,0:T(8,128)S(1)}, u32[]{:S(2)}, u32[]{:S(2)}) collective-permute-start(f32[1024,256]{1,0:T(8,128)S(1)} %slice_dynamic-update-slice_fusion.refs_0_), channel_id=1, source_target_pairs={{0,48},{8,200},{16,0},{24,216},{32,16},{40,232},{48,32},{56,248},{... | collective-permute-start | bytes 3145736 | tf_op jit(solution)/shard_map/major_gather/ppermute | solution.py:243
  43.8 15.2 %collective-permute-start.11 = (f32[1024,256]{1,0:T(8,128)S(1)}, f32[1024,256]{1,0:T(8,128)S(1)}, u32[]{:S(2)}, u32[]{:S(2)}) collective-permute-start(f32[1024,256]{1,0:T(8,128)S(1)} %slice_dynamic-update-slice_fusion.refs_0_), channel_id=1, source_target_pairs={{0,16},{8,72},{16,32},{24,88},{32,48},{40,104},{48,0},{56,120},{64... | collective-permute-start | bytes 3145736 | tf_op jit(solution)/shard_map/major_gather/ppermute | solution.py:243
  43.9 2.8 %collective-permute-start.13 = (f32[8,256]{1,0:T(8,128)S(1)}, f32[8,256]{1,0:T(8,128)S(1)}, u32[]{:S(2)}, u32[]{:S(2)}) collective-permute-start(f32[8,256]{1,0:T(8,128)S(1)} %squares.1), channel_id=1, source_target_pairs={{0,1},{1,0},{2,3},{3,2},{4,5},{5,4},{6,7},{7,6},{8,9},{9,8},{10,11... | collective-permute-start | bytes 24584 | tf_op jit(solution)/shard_map/square_sum/ppermute | solution.py:269
  46.7 4.0 %collective-permute-start.14 = (f32[8,256]{1,0:T(8,128)S(1)}, f32[8,256]{1,0:T(8,128)S(1)}, u32[]{:S(2)}, u32[]{:S(2)}) collective-permute-start(f32[8,256]{1,0:T(8,128)S(1)} %add.62), channel_id=1, source_target_pairs={{0,2},{1,3},{2,0},{3,1},{4,6},{5,7},{6,4},{7,5},{8,10},{9,11},{10,... | collective-permute-start | bytes 24584 | tf_op jit(solution)/shard_map/square_sum/ppermute | solution.py:271
  50.7 6.1 %collective-permute-start.15 = (f32[8,256]{1,0:T(8,128)S(1)}, f32[8,256]{1,0:T(8,128)S(1)}, u32[]{:S(2)}, u32[]{:S(2)}) collective-permute-start(f32[8,256]{1,0:T(8,128)S(1)} %add.63), channel_id=1, source_target_pairs={{0,7},{1,6},{2,5},{3,4},{4,3},{5,2},{6,1},{7,0},{8,15},{9,14},{10,... | collective-permute-start | bytes 24584 | tf_op jit(solution)/shard_map/square_sum/ppermute | solution.py:271
  59.1 6.8 %collective-permute-start.19 = (f32[512,256]{1,0:T(8,128)S(1)}, f32[512,256]{1,0:T(8,128)S(1)}, u32[]{:S(2)}, u32[]{:S(2)}) collective-permute-start(f32[512,256]{1,0:T(8,128)S(1)} %get-tuple-element.52), channel_id=1, source_target_pairs={{0,8},{8,0},{16,24},{24,16},{32,40},{40,32},{48,56},{56,48},{64,72... | collective-permute-start | bytes 1572872 | tf_op jit(solution)/shard_map/core_gather/ppermute | solution.py:243
  63.5 4.1 %collective-permute-start.18 = (f32[512,256]{1,0:T(8,128)S(1)}, f32[512,256]{1,0:T(8,128)S(1)}, u32[]{:S(2)}, u32[]{:S(2)}) collective-permute-start(f32[512,256]{1,0:T(8,128)S(1)} %get-tuple-element.53), channel_id=1, source_target_pairs={{0,8},{8,0},{16,24},{24,16},{32,40},{40,32},{48,56},{56,48},{64,72... | collective-permute-start | bytes 1572872 | tf_op jit(solution)/shard_map/core_gather/ppermute | solution.py:243
  63.7 17.0 %copy-start = (f32[128,256]{1,0:T(8,128)S(1)}, f32[128,256]{1,0:T(8,128)}, u32[]{:S(2)}) copy-start(f32[128,256]{1,0:T(8,128)} %refs_13_.1) | copy-start | bytes 393220
  63.7 4.1 %collective-permute-start.21 = (f32[512,256]{1,0:T(8,128)S(1)}, f32[512,256]{1,0:T(8,128)S(1)}, u32[]{:S(2)}, u32[]{:S(2)}) collective-permute-start(f32[512,256]{1,0:T(8,128)S(1)} %get-tuple-element.50), channel_id=1, source_target_pairs={{0,8},{8,0},{16,24},{24,16},{32,40},{40,32},{48,56},{56,48},{64,72... | collective-permute-start | bytes 1572872 | tf_op jit(solution)/shard_map/core_gather/ppermute | solution.py:243
  64.4 8.5 %collective-permute-start.17 = (f32[520,256]{1,0:T(8,128)S(1)}, f32[520,256]{1,0:T(8,128)S(1)}, u32[]{:S(2)}, u32[]{:S(2)}) collective-permute-start(f32[520,256]{1,0:T(8,128)S(1)} %get-tuple-element.60), channel_id=1, source_target_pairs={{0,48},{8,200},{16,0},{24,216},{32,16},{40,232},{48,32},{56,248},{... | collective-permute-start | bytes 1597448 | tf_op jit(solution)/shard_map/major_forward/ppermute | solution.py:243
  65.5 9.7 %collective-permute-start.16 = (f32[520,256]{1,0:T(8,128)S(1)}, f32[520,256]{1,0:T(8,128)S(1)}, u32[]{:S(2)}, u32[]{:S(2)}) collective-permute-start(f32[520,256]{1,0:T(8,128)S(1)} %get-tuple-element.61), channel_id=1, source_target_pairs={{0,16},{8,72},{16,32},{24,88},{32,48},{40,104},{48,0},{56,120},{64... | collective-permute-start | bytes 1597448 | tf_op jit(solution)/shard_map/major_forward/ppermute | solution.py:243
  65.9 3.3 %collective-permute-start.20 = (f32[512,256]{1,0:T(8,128)S(1)}, f32[512,256]{1,0:T(8,128)S(1)}, u32[]{:S(2)}, u32[]{:S(2)}) collective-permute-start(f32[512,256]{1,0:T(8,128)S(1)} %get-tuple-element.51), channel_id=1, source_target_pairs={{0,8},{8,0},{16,24},{24,16},{32,40},{40,32},{48,56},{56,48},{64,72... | collective-permute-start | bytes 1572872 | tf_op jit(solution)/shard_map/core_gather/ppermute | solution.py:243
  67.6 2.8 %collective-permute-start.22 = (f32[512,256]{1,0:T(8,128)S(1)}, f32[512,256]{1,0:T(8,128)S(1)}, u32[]{:S(2)}, u32[]{:S(2)}) collective-permute-start(f32[512,256]{1,0:T(8,128)S(1)} %get-tuple-element.48), channel_id=1, source_target_pairs={{0,8},{8,0},{16,24},{24,16},{32,40},{40,32},{48,56},{56,48},{64,72... | collective-permute-start | bytes 1572872 | tf_op jit(solution)/shard_map/core_gather/ppermute | solution.py:243
  67.7 2.9 %collective-permute-start.23 = (f32[512,256]{1,0:T(8,128)S(1)}, f32[512,256]{1,0:T(8,128)S(1)}, u32[]{:S(2)}, u32[]{:S(2)}) collective-permute-start(f32[512,256]{1,0:T(8,128)S(1)} %get-tuple-element.49), channel_id=1, source_target_pairs={{0,8},{8,0},{16,24},{24,16},{32,40},{40,32},{48,56},{56,48},{64,72... | collective-permute-start | bytes 1572872 | tf_op jit(solution)/shard_map/core_gather/ppermute | solution.py:243
  69.2 6.0 %collective-permute-start.24 = (f32[8,256]{1,0:T(8,128)S(1)}, f32[8,256]{1,0:T(8,128)S(1)}, u32[]{:S(2)}, u32[]{:S(2)}) collective-permute-start(f32[8,256]{1,0:T(8,128)S(1)} %add.64), channel_id=1, source_target_pairs={{0,32},{8,136},{16,48},{24,152},{32,0},{40,168},{48,16},{56,184},{... | collective-permute-start | bytes 24584 | tf_op jit(solution)/shard_map/square_sum/ppermute | solution.py:243
  75.3 5.4 %collective-permute-start.26 = (f32[520,256]{1,0:T(8,128)S(1)}, f32[520,256]{1,0:T(8,128)S(1)}, u32[]{:S(2)}, u32[]{:S(2)}) collective-permute-start(f32[520,256]{1,0:T(8,128)S(1)} %pad_maximum_fusion.2.refs_4_), channel_id=1, source_target_pairs={{0,8},{8,0},{16,24},{24,16},{32,40},{40,32},{48,56},{56,48},{64,72... | collective-permute-start | bytes 1597448 | tf_op jit(solution)/shard_map/update/ppermute | solution.py:243
  78.4 2.3 %collective-permute-start.25 = (f32[512,256]{1,0:T(8,128)S(1)}, f32[512,256]{1,0:T(8,128)S(1)}, u32[]{:S(2)}, u32[]{:S(2)}) collective-permute-start(f32[512,256]{1,0:T(8,128)S(1)} %slice.86.refs_3_), channel_id=1, source_target_pairs={{0,8},{8,0},{16,24},{24,16},{32,40},{40,32},{48,56},{56,48},{64,72... | collective-permute-start | bytes 1572872 | tf_op jit(solution)/shard_map/update/ppermute | solution.py:243

commit v2 on v1

--- a/solution.py
+++ b/solution.py
@@ -171,23 +171,27 @@
     )(values)
 
 
-def update_kernel(threshold, *refs):
-    mine, handed, (momentum, new_momentum, out, buf, sem) = refs[:5], refs[5:13], refs[13:]
-    rows = momentum.shape[0]
+def update_kernel(threshold, steps, first, *refs):
+    own_count, other_count = (5, 2 * len(steps)) if first else (0, 2)
+    mine, handed = refs[:own_count], refs[own_count : own_count + other_count]
+    own_squares, other_squares, last = refs[own_count + other_count :][:3]
+    out, buf, sem = refs[-3:]
+    rows = buf.shape[1]
     size, half = SIDE * rows, rows // 2
     me = lax.axis_index("replica")
     core = lax.rem(me, 2)
-    squares = mine[-1][size:, :] + handed[-1][size:, :]
+    squares = own_squares[...] + other_squares[...]
     magnitude = jnp.sqrt(jnp.sum(squares, axis=(0, 1), keepdims=True))
     factor = jnp.minimum(1.0, threshold / (magnitude + 1e-06))
     rate = OUTER_RATE * (1.0 + OUTER_MOMENTUM) * factor
-    own = [(k, mine[n], 0, mine[n], size) for n, k in enumerate((0, 1, 3))]
-    own.append((2, mine[3], 0, mine[4], 0))
-    other = [(k, handed[2 * n], 0, handed[2 * n + 1], 0) for n, k in enumerate((0, 1, 3, 2))]
+    own = []
+    if first:
+        own = [(k, mine[n], mine[n], size) for n, k in enumerate((0, 1, 3))] + [(2, mine[3], mine[4], 0)]
+    other = [(k, handed[2 * n], handed[2 * n + 1], 0) for n, k in enumerate(steps)]
     copies = []
     for side, sources in ((core, own), (1 - core, other)):
         major, minor = axes_of(me, side)
-        for k, averages, first, bases, offset in sources:
+        for k, averages, bases, offset in sources:
             place = lax.rem(major + SIDE - k, SIDE)
             for j in range(SIDE):
                 apart = minor ^ j
@@ -196,37 +200,39 @@
                 at = len(copies)
                 for n, slot in enumerate((low, SIDE + high)):
                     base = pl.ds(pl.multiple_of(offset + slot * half, half), half)
-                    average = averages[first + j * rows + n * half : first + j * rows + (n + 1) * half, :]
+                    average = averages[j * rows + n * half : j * rows + (n + 1) * half, :]
                     buf[at, n * half : (n + 1) * half, :] = bases[base, :] - rate * average
                 columns = columns_of(owner_of(side, place, j))
                 copy = pltpu.make_async_copy(buf.at[at], out.at[:, columns], sem.at[at])
                 copy.start()
                 copies.append(copy)
-    here = pl.ds(pl.multiple_of(axes_of(me, core)[1] * rows, rows), rows)
-    new_momentum[...] = OUTER_MOMENTUM * momentum[...] + factor * mine[0][here, :]
+    if first:
+        momentum, new_momentum = last, refs[-4]
+        here = pl.ds(pl.multiple_of(axes_of(me, core)[1] * rows, rows), rows)
+        new_momentum[...] = OUTER_MOMENTUM * momentum[...] + factor * mine[0][here, :]
     for copy in copies:
         copy.wait()
 
 
-def update(cols, threshold, mine, handed, momentum):
-    rows = momentum.shape[0]
-    chunks = 2 * SIDE * SIDE
+def update(rows, cols, threshold, steps, mine, handed, squares, momentum=None, out=None):
+    first = out is None
+    chunks = SIDE * ((SIDE if first else 0) + len(steps))
+    arrays = [*mine, *handed, *squares]
+    out_shape = [jax.ShapeDtypeStruct((rows, WIDTH), jnp.float32)] if first else []
     return pl.pallas_call(
-        functools.partial(update_kernel, threshold),
-        out_shape=[
-            jax.ShapeDtypeStruct((rows, WIDTH), jnp.float32),
-            jax.ShapeDtypeStruct((rows, cols), jnp.float32),
-        ],
-        in_specs=[VMEM] * (len(mine) + len(handed) + 1),
-        out_specs=[VMEM, HBM],
+        functools.partial(update_kernel, threshold, steps, first),
+        out_shape=[*out_shape, jax.ShapeDtypeStruct((rows, cols), jnp.float32)],
+        in_specs=[VMEM] * len(arrays) + [VMEM if first else HBM],
+        out_specs=([VMEM] if first else []) + [HBM],
         scratch_shapes=[
             pltpu.VMEM((chunks, rows, WIDTH), jnp.float32),
             pltpu.SemaphoreType.DMA((chunks,)),
         ],
+        input_output_aliases={} if first else {len(arrays): 0},
         compiler_params=pltpu.CompilerParams(vmem_limit_bytes=SCOPED),
-        cost_estimate=pl.CostEstimate(flops=2**21, bytes_accessed=2**22, transcendentals=0),
+        cost_estimate=pl.CostEstimate(flops=2**16 * chunks, bytes_accessed=2**17 * chunks, transcendentals=0),
         name="update",
-    )(*mine, *handed, momentum)
+    )(*arrays, momentum if first else out)
 
 
 def tie(*values):
@@ -283,16 +289,20 @@
         near = [move(part, CORE_SWAP) for x in whole for part in (x[:middle], x[middle:])]
 
     with jax.named_scope("square_sum"):
-        across = move(squares, major_shift(2))
-        far_low, far_high, near = tie(far_low, far_high, near)
+        across = move(tie(squares, near[1])[0], major_shift(2))
+        far_low, far_high, near, across = tie(far_low, far_high, near, across)
         squares = squares + across + far_low[middle:] + far_high[middle:]
 
     with jax.named_scope("update"):
-        (far_low,) = tie(far_low[:middle])
-        far_high = jnp.concatenate([far_high[:middle], squares])
-        handed = [*near, move(far_low, CORE_SWAP), move(far_high, CORE_SWAP)]
+        squares = squares, move(squares, CORE_SWAP)
+        far = tie(far_low[:middle], far_high[:middle])
+        ready = tie(*far, *squares)[:2]
+        handed = [move(x, CORE_SWAP) for x in ready]
         new_momentum, new_weights = update(
-            col_count, threshold, [mine, below, above, far_low, far_high], handed, momentum
+            row_count, col_count, threshold, (0, 1, 3), [mine, below, above, *far], near, squares, momentum
+        )
+        (new_weights,) = update(
+            row_count, col_count, threshold, (2,), [], handed, squares, None, new_weights
         )
     return (new_weights, new_momentum)
 

time: 84 us -> 84 us (level)
  waiting for transfers between devices: 38.6 us -> 37.2 us
    ppermute x24 -> x25, waiting for transfers between devices: 35.2 us -> 33.8 us  [move(): return lax.ppermute(value, 'replica', perm)]
    pallas_call x1 -> x2, Pallas kernels: 3.07 us -> 3.83 us  [update(): pl.pallas_call(functools.partial(update_kernel, threshold, steps, first),...]
    ppermute x24 -> x25, starting transfers between devices: 26.4 us -> 27.1 us  [move(): return lax.ppermute(value, 'replica', perm)]
  transfers between devices with their start and end apart: 27 -> 28, of which waited for: 15 -> 15; matrix products, arithmetic and copies ran while one was open for 1% -> 1% of each run, Pallas kernels for 0% -> 3%
where the time goes in v2:
time: 84 us; the launch traced here: 83.9 us
  waiting for transfers between devices  37.2 us (44%)
  starting transfers between devices  36.6 us (44%)
  Pallas kernels  7.88 us (9%)
  between operations  1.04 us (1%)
    ppermute x25, waiting for transfers between devices, move(): return lax.ppermute(value, 'replica', perm)  33.8 us
    ppermute x25, starting transfers between devices, move(): return lax.ppermute(value, 'replica', perm)  27.1 us
    ppermute x2, starting transfers between devices, per_device(): squares = squares + lax.ppermute(squares, 'fsdp', perm)  7.76 us
    pallas_call x1, Pallas kernels, encode(): pl.pallas_call(encode_kernel, out_shape=[*blocks, *blocks, jax.ShapeDtype...  3.98 us
    pallas_call x2, Pallas kernels, update(): pl.pallas_call(functools.partial(update_kernel, threshold, steps, first),...  3.83 us
    ppermute x2, waiting for transfers between devices, per_device(): squares = squares + lax.ppermute(squares, 'fsdp', perm)  2.37 us
    ppermute x1, starting transfers between devices, per_device(): squares = squares + lax.ppermute(squares, 'fsdp', Z_ROUNDS[0])  1.72 us
  transfers between devices with their start and end apart: 28, of which 15 were waited for; matrix products, arithmetic and copies ran while one was open for 1% of the time, Pallas kernels for 3%

profile of v2, /device:TPU:1, one launch (start us, length us, event | category | flops | bytes accessed | tf_op | source)
XLA Modules:
  0.0 83.9 jit_solution(14154263621781369204)
XLA Ops:
  0.6 4.0 %encode.1 = (f32[4,128,256]{2,1,0:T(8,128)S(1)}, f32[4,128,256]{2,1,0:T(8,128)S(1)}, f32[4,128,256]{2,1,0:T(8,128)S(1)}, f32[4,128,256]{2,1,0:T(8,128)S(1)}, f32...) custom-call(f32[128,8192]{1,0:T(8,128)} %weights.1, ...), custom_call_target="tpu_custom_call" | custom-call | flops 4194304 | bytes 6291456 | tf_op jit(solution)/shard_map/core_sum/encode/pallas_call | solution.py:132
  4.6 3.3 %collective-permute-start.1 = (f32[4,128,256]{2,1,0:T(8,128)S(1)}, f32[4,128,256]{2,1,0:T(8,128)S(1)}, u32[]{:S(2)}, u32[]{:S(2)}) collective-permute-start(f32[4,128,256]{2,1,0:T(8,128)S(1)} %get-tuple-element.34), channel_id=1, source_target_pairs={{0,8},{8,0},{16,24},{24,16},{32,40},{40,32},{48,56},{56,48},{64,72... | collective-permute-start | bytes 1572872 | tf_op jit(solution)/shard_map/core_sum/ppermute | solution.py:249
  7.9 0.1 collective-permute-start.3
  8.0 0.4 collective-permute-start.5
  8.5 0.1 collective-permute-start
  8.6 0.9 %collective-permute-done.1 = f32[4,128,256]{2,1,0:T(8,128)S(1)} collective-permute-done((f32[4,128,256]{2,1,0:T(8,128)S(1)}, f32[4,128,256]{2,1,0:T(8,128)S(1)}, u32[]{:S(2)}, u32[]{:S(2)}) %collective-permute-start.1) | collective-permute-done | bytes 524320 | tf_op jit(solution)/shard_map/core_sum/ppermute | solution.py:249
  9.5 0.1 add.52
  9.5 1.3 %collective-permute-start.2 = (f32[4,128,256]{2,1,0:T(8,128)S(1)}, f32[4,128,256]{2,1,0:T(8,128)S(1)}, u32[]{:S(2)}, u32[]{:S(2)}) collective-permute-start(f32[4,128,256]{2,1,0:T(8,128)S(1)} %add.52), channel_id=1, source_target_pairs={{0,32},{8,136},{16,48},{24,152},{32,0},{40,168},{48,16},{56,184},{... | collective-permute-start | bytes 1572872 | tf_op jit(solution)/shard_map/major_sum/ppermute | solution.py:249
  10.8 0.0 collective-permute-done.3
  10.8 0.1 add.54
  10.9 0.5 collective-permute-start.4
  11.4 0.0 collective-permute-done.5
  11.4 0.1 add.56
  11.4 2.4 %collective-permute-start.6 = (f32[4,128,256]{2,1,0:T(8,128)S(1)}, f32[4,128,256]{2,1,0:T(8,128)S(1)}, u32[]{:S(2)}, u32[]{:S(2)}) collective-permute-start(f32[4,128,256]{2,1,0:T(8,128)S(1)} %add.56), channel_id=1, source_target_pairs={{0,48},{8,200},{16,0},{24,216},{32,16},{40,232},{48,32},{56,248},{... | collective-permute-start | bytes 1572872 | tf_op jit(solution)/shard_map/major_sum/ppermute | solution.py:249
  13.8 0.0 collective-permute-done
  13.8 5.7 %collective-permute-done.2 = f32[4,128,256]{2,1,0:T(8,128)S(1)} collective-permute-done((f32[4,128,256]{2,1,0:T(8,128)S(1)}, f32[4,128,256]{2,1,0:T(8,128)S(1)}, u32[]{:S(2)}, u32[]{:S(2)}) %collective-permute-start.2) | collective-permute-done | bytes 524320 | tf_op jit(solution)/shard_map/major_sum/ppermute | solution.py:249
  19.5 5.6 %collective-permute-done.4 = f32[4,128,256]{2,1,0:T(8,128)S(1)} collective-permute-done((f32[4,128,256]{2,1,0:T(8,128)S(1)}, f32[4,128,256]{2,1,0:T(8,128)S(1)}, u32[]{:S(2)}, u32[]{:S(2)}) %collective-permute-start.4) | collective-permute-done | bytes 524320 | tf_op jit(solution)/shard_map/major_sum/ppermute | solution.py:249
  25.1 0.0 collective-permute-done.6
  25.1 0.2 add_add_fusion
  25.3 1.2 %collective-permute-start.9 = (f32[320,256]{1,0:T(8,128)S(1)}, f32[320,256]{1,0:T(8,128)S(1)}, u32[]{:S(2)}, u32[]{:S(2)}) collective-permute-start(f32[320,256]{1,0:T(8,128)S(1)} %pad_maximum_fusion.5), channel_id=1, source_target_pairs={{0,192},{8,56},{16,208},{24,40},{32,224},{40,24},{48,240},{56,8},{... | collective-permute-start | bytes 983048 | tf_op jit(solution)/shard_map/minor_sum/ppermute | solution.py:249
  26.6 0.1 collective-permute-start.7
  26.7 6.2 %collective-permute-done.9 = f32[320,256]{1,0:T(8,128)S(1)} collective-permute-done((f32[320,256]{1,0:T(8,128)S(1)}, f32[320,256]{1,0:T(8,128)S(1)}, u32[]{:S(2)}, u32[]{:S(2)}) %collective-permute-start.9) | collective-permute-done | bytes 327712 | tf_op jit(solution)/shard_map/minor_sum/ppermute | solution.py:249
  32.9 0.1 collective-permute-start.10
  33.1 1.5 %collective-permute-start.8 = (f32[384,256]{1,0:T(8,128)S(1)}, f32[384,256]{1,0:T(8,128)S(1)}, u32[]{:S(2)}, u32[]{:S(2)}) collective-permute-start(f32[384,256]{1,0:T(8,128)S(1)} %pad_maximum_fusion.2), channel_id=1, source_target_pairs={{0,192},{8,56},{16,208},{24,40},{32,224},{40,24},{48,240},{56,8},{... | collective-permute-start | bytes 1179656 | tf_op jit(solution)/shard_map/minor_sum/ppermute | solution.py:249
  34.6 5.3 %collective-permute-done.10 = f32[384,256]{1,0:T(8,128)S(1)} collective-permute-done((f32[384,256]{1,0:T(8,128)S(1)}, f32[384,256]{1,0:T(8,128)S(1)}, u32[]{:S(2)}, u32[]{:S(2)}) %collective-permute-start.10) | collective-permute-done | bytes 393248 | tf_op jit(solution)/shard_map/minor_sum/ppermute | solution.py:249
  40.0 1.4 %collective-permute-done.8 = f32[384,256]{1,0:T(8,128)S(1)} collective-permute-done((f32[384,256]{1,0:T(8,128)S(1)}, f32[384,256]{1,0:T(8,128)S(1)}, u32[]{:S(2)}, u32[]{:S(2)}) %collective-permute-start.8) | collective-permute-done | bytes 393248 | tf_op jit(solution)/shard_map/minor_sum/ppermute | solution.py:249
  41.4 0.1 maximum_multiply_fusion
  41.6 2.2 %collective-permute-start.12 = (f32[1024,256]{1,0:T(8,128)S(1)}, f32[1024,256]{1,0:T(8,128)S(1)}, u32[]{:S(2)}, u32[]{:S(2)}) collective-permute-start(f32[1024,256]{1,0:T(8,128)S(1)} %slice_dynamic-update-slice_fusion.refs_0_), channel_id=1, source_target_pairs={{0,48},{8,200},{16,0},{24,216},{32,16},{40,232},{48,32},{56,248},{... | collective-permute-start | bytes 3145736 | tf_op jit(solution)/shard_map/major_gather/ppermute | solution.py:249
  43.8 0.0 collective-permute-start.11
  43.8 0.1 squares.1
  43.9 1.7 %collective-permute-start.13 = (f32[8,256]{1,0:T(8,128)S(1)}, f32[8,256]{1,0:T(8,128)S(1)}, u32[]{:S(2)}, u32[]{:S(2)}) collective-permute-start(f32[8,256]{1,0:T(8,128)S(1)} %squares.1), channel_id=1, source_target_pairs={{0,1},{1,0},{2,3},{3,2},{4,5},{5,4},{6,7},{7,6},{8,9},{9,8},{10,11... | collective-permute-start | bytes 24584 | tf_op jit(solution)/shard_map/square_sum/ppermute | solution.py:275
  45.6 1.0 %collective-permute-done.13 = f32[8,256]{1,0:T(8,128)S(1)} collective-permute-done((f32[8,256]{1,0:T(8,128)S(1)}, f32[8,256]{1,0:T(8,128)S(1)}, u32[]{:S(2)}, u32[]{:S(2)}) %collective-permute-start.13) | collective-permute-done | bytes 8224 | tf_op jit(solution)/shard_map/square_sum/ppermute | solution.py:275
  46.7 3.0 %collective-permute-start.14 = (f32[8,256]{1,0:T(8,128)S(1)}, f32[8,256]{1,0:T(8,128)S(1)}, u32[]{:S(2)}, u32[]{:S(2)}) collective-permute-start(f32[8,256]{1,0:T(8,128)S(1)} %add.62), channel_id=1, source_target_pairs={{0,2},{1,3},{2,0},{3,1},{4,6},{5,7},{6,4},{7,5},{8,10},{9,11},{10,... | collective-permute-start | bytes 24584 | tf_op jit(solution)/shard_map/square_sum/ppermute | solution.py:277
  49.7 1.0 %collective-permute-done.14 = f32[8,256]{1,0:T(8,128)S(1)} collective-permute-done((f32[8,256]{1,0:T(8,128)S(1)}, f32[8,256]{1,0:T(8,128)S(1)}, u32[]{:S(2)}, u32[]{:S(2)}) %collective-permute-start.14) | collective-permute-done | bytes 8224 | tf_op jit(solution)/shard_map/square_sum/ppermute | solution.py:277
  50.7 4.8 %collective-permute-start.15 = (f32[8,256]{1,0:T(8,128)S(1)}, f32[8,256]{1,0:T(8,128)S(1)}, u32[]{:S(2)}, u32[]{:S(2)}) collective-permute-start(f32[8,256]{1,0:T(8,128)S(1)} %add.63), channel_id=1, source_target_pairs={{0,7},{1,6},{2,5},{3,4},{4,3},{5,2},{6,1},{7,0},{8,15},{9,14},{10,... | collective-permute-start | bytes 24584 | tf_op jit(solution)/shard_map/square_sum/ppermute | solution.py:277
  55.5 1.3 %collective-permute-done.15 = f32[8,256]{1,0:T(8,128)S(1)} collective-permute-done((f32[8,256]{1,0:T(8,128)S(1)}, f32[8,256]{1,0:T(8,128)S(1)}, u32[]{:S(2)}, u32[]{:S(2)}) %collective-permute-start.15) | collective-permute-done | bytes 8224 | tf_op jit(solution)/shard_map/square_sum/ppermute | solution.py:277
  56.8 2.2 %collective-permute-done.11.refs_1_ = f32[1024,256]{1,0:T(8,128)S(1)} collective-permute-done((f32[1024,256]{1,0:T(8,128)S(1)}, f32[1024,256]{1,0:T(8,128)S(1)}, u32[]{:S(2)}, u32[]{:S(2)}) %collective-permute-start.11) | collective-permute-done | bytes 1048608 | tf_op jit(solution)/shard_map/major_gather/ppermute | solution.py:249
  59.0 0.1 fusion.2
  59.1 4.4 %collective-permute-start.19 = (f32[512,256]{1,0:T(8,128)S(1)}, f32[512,256]{1,0:T(8,128)S(1)}, u32[]{:S(2)}, u32[]{:S(2)}) collective-permute-start(f32[512,256]{1,0:T(8,128)S(1)} %get-tuple-element.64), channel_id=1, source_target_pairs={{0,8},{8,0},{16,24},{24,16},{32,40},{40,32},{48,56},{56,48},{64,72... | collective-permute-start | bytes 1572872 | tf_op jit(solution)/shard_map/core_gather/ppermute | solution.py:249
  63.5 0.1 collective-permute-start.18
  63.6 0.1 fusion.1
  63.7 0.5 collective-permute-start.21
  64.2 0.1 collective-permute-start.20
  64.3 0.1 fusion
  64.3 0.1 pad_maximum_fusion
  64.4 1.1 %collective-permute-start.17 = (f32[520,256]{1,0:T(8,128)S(1)}, f32[520,256]{1,0:T(8,128)S(1)}, u32[]{:S(2)}, u32[]{:S(2)}) collective-permute-start(f32[520,256]{1,0:T(8,128)S(1)} %get-tuple-element.72), channel_id=1, source_target_pairs={{0,48},{8,200},{16,0},{24,216},{32,16},{40,232},{48,32},{56,248},{... | collective-permute-start | bytes 1597448 | tf_op jit(solution)/shard_map/major_forward/ppermute | solution.py:249
  65.5 0.0 collective-permute-done.19.refs_6_
  65.5 0.5 collective-permute-start.16
  66.0 0.0 collective-permute-done.18.refs_5_
  66.0 2.1 %collective-permute-start.22 = (f32[512,256]{1,0:T(8,128)S(1)}, f32[512,256]{1,0:T(8,128)S(1)}, u32[]{:S(2)}, u32[]{:S(2)}) collective-permute-start(f32[512,256]{1,0:T(8,128)S(1)} %get-tuple-element.60), channel_id=1, source_target_pairs={{0,8},{8,0},{16,24},{24,16},{32,40},{40,32},{48,56},{56,48},{64,72... | collective-permute-start | bytes 1572872 | tf_op jit(solution)/shard_map/core_gather/ppermute | solution.py:249
  68.1 0.0 collective-permute-done.21.refs_8_
  68.1 0.1 collective-permute-start.23
  68.2 1.2 %collective-permute-start.24 = (f32[8,256]{1,0:T(8,128)S(1)}, f32[8,256]{1,0:T(8,128)S(1)}, u32[]{:S(2)}, u32[]{:S(2)}) collective-permute-start(f32[8,256]{1,0:T(8,128)S(1)} %add.64), channel_id=1, source_target_pairs={{0,32},{8,136},{16,48},{24,152},{32,0},{40,168},{48,16},{56,184},{... | collective-permute-start | bytes 24584 | tf_op jit(solution)/shard_map/square_sum/ppermute | solution.py:249
  69.5 0.2 collective-permute-done.22.refs_9_
  69.6 0.7 collective-permute-done.23.refs_10_
  70.4 3.7 %collective-permute-done.24 = f32[8,256]{1,0:T(8,128)S(1)} collective-permute-done((f32[8,256]{1,0:T(8,128)S(1)}, f32[8,256]{1,0:T(8,128)S(1)}, u32[]{:S(2)}, u32[]{:S(2)}) %collective-permute-start.24) | collective-permute-done | bytes 8224 | tf_op jit(solution)/shard_map/square_sum/ppermute | solution.py:249
  74.1 1.2 %collective-permute-done.16 = f32[520,256]{1,0:T(8,128)S(1)} collective-permute-done((f32[520,256]{1,0:T(8,128)S(1)}, f32[520,256]{1,0:T(8,128)S(1)}, u32[]{:S(2)}, u32[]{:S(2)}) %collective-permute-start.16) | collective-permute-done | bytes 532512 | tf_op jit(solution)/shard_map/major_forward/ppermute | solution.py:249
  75.2 3.3 %collective-permute-start.25 = (f32[8,256]{1,0:T(8,128)S(1)}, f32[8,256]{1,0:T(8,128)S(1)}, u32[]{:S(2)}, u32[]{:S(2)}) collective-permute-start(f32[8,256]{1,0:T(8,128)S(1)} %slice_add_fusion.4.refs_11_.refs_2_), channel_id=1, source_target_pairs={{0,8},{8,0},{16,24},{24,16},{32,40},{40,32},{48,56},{56,48},{64,72... | collective-permute-start | bytes 24584 | tf_op jit(solution)/shard_map/update/ppermute | solution.py:249
  78.7 0.7 collective-permute-done.25.refs_12_.refs_3_
  79.4 0.3 collective-permute-start.26
  79.8 0.2 collective-permute-start.27
  79.9 2.9 %update.2 = (f32[128,256]{1,0:T(8,128)}, f32[128,8192]{1,0:T(8,128)}) custom-call(f32[1024,256]{1,0:T(8,128)S(1)} %slice_dynamic-update-slice_fusion.refs_0_, f32[1024,256]{1,0:T(8,128)S(1)} %collective-permute-done.11.refs_1_, f32[1024,256]{1,0:T(8,128)S(1)} %collective-permute-done.12.refs_2_, f32[512,256]{1,0:T(8,128)S(1)} %slice.86.refs_3_, ...), custom_call_target="tpu_custom_call" | custom-call | flops 1835008 | bytes 3670016 | tf_op jit(solution)/shard_map/update/update/pallas_call | solution.py:222
  82.8 0.0 collective-permute-done.27.refs_1_
  82.8 1.0 %update.3 = f32[128,8192]{1,0:T(8,128)} custom-call(f32[512,256]{1,0:T(8,128)S(1)} %collective-permute-done.26.refs_0_, f32[512,256]{1,0:T(8,128)S(1)} %collective-permute-done.27.refs_1_, f32[8,256]{1,0:T(8,128)S(1)} %slice_add_fusion.4.refs_11_.refs_2_, f32[8,256]{1,0:T(8,128)S(1)} %collective-permute-done.25.refs_12_.refs_3_, ...), custom_call_target="tpu_custom_call", output_to_operand_aliasing={{}: (4, {})} | custom-call | flops 262144 | bytes 524288 | tf_op jit(solution)/shard_map/update/update/pallas_call | solution.py:222
  (31 shorter events, 0.5 us)
Async XLA Ops:
  4.6 4.9 %collective-permute-start.1 = (f32[4,128,256]{2,1,0:T(8,128)S(1)}, f32[4,128,256]{2,1,0:T(8,128)S(1)}, u32[]{:S(2)}, u32[]{:S(2)}) collective-permute-start(f32[4,128,256]{2,1,0:T(8,128)S(1)} %get-tuple-element.34), channel_id=1, source_target_pairs={{0,8},{8,0},{16,24},{24,16},{32,40},{40,32},{48,56},{56,48},{64,72... | collective-permute-start | bytes 1572872 | tf_op jit(solution)/shard_map/core_sum/ppermute | solution.py:249
  7.9 2.9 %collective-permute-start.3 = (f32[4,128,256]{2,1,0:T(8,128)S(1)}, f32[4,128,256]{2,1,0:T(8,128)S(1)}, u32[]{:S(2)}, u32[]{:S(2)}) collective-permute-start(f32[4,128,256]{2,1,0:T(8,128)S(1)} %get-tuple-element.36), channel_id=1, source_target_pairs={{0,8},{8,0},{16,24},{24,16},{32,40},{40,32},{48,56},{56,48},{64,72... | collective-permute-start | bytes 1572872 | tf_op jit(solution)/shard_map/core_sum/ppermute | solution.py:249
  8.0 3.3 %collective-permute-start.5 = (f32[4,128,256]{2,1,0:T(8,128)S(1)}, f32[4,128,256]{2,1,0:T(8,128)S(1)}, u32[]{:S(2)}, u32[]{:S(2)}) collective-permute-start(f32[4,128,256]{2,1,0:T(8,128)S(1)} %get-tuple-element.38), channel_id=1, source_target_pairs={{0,8},{8,0},{16,24},{24,16},{32,40},{40,32},{48,56},{56,48},{64,72... | collective-permute-start | bytes 1572872 | tf_op jit(solution)/shard_map/core_sum/ppermute | solution.py:249
  8.5 5.4 %collective-permute-start = (f32[4,128,256]{2,1,0:T(8,128)S(1)}, f32[4,128,256]{2,1,0:T(8,128)S(1)}, u32[]{:S(2)}, u32[]{:S(2)}) collective-permute-start(f32[4,128,256]{2,1,0:T(8,128)S(1)} %get-tuple-element.32), channel_id=1, source_target_pairs={{0,8},{8,0},{16,24},{24,16},{32,40},{40,32},{48,56},{56,48},{64,72... | collective-permute-start | bytes 1572872 | tf_op jit(solution)/shard_map/core_sum/ppermute | solution.py:249
  9.5 10.0 %collective-permute-start.2 = (f32[4,128,256]{2,1,0:T(8,128)S(1)}, f32[4,128,256]{2,1,0:T(8,128)S(1)}, u32[]{:S(2)}, u32[]{:S(2)}) collective-permute-start(f32[4,128,256]{2,1,0:T(8,128)S(1)} %add.52), channel_id=1, source_target_pairs={{0,32},{8,136},{16,48},{24,152},{32,0},{40,168},{48,16},{56,184},{... | collective-permute-start | bytes 1572872 | tf_op jit(solution)/shard_map/major_sum/ppermute | solution.py:249
  10.9 14.2 %collective-permute-start.4 = (f32[4,128,256]{2,1,0:T(8,128)S(1)}, f32[4,128,256]{2,1,0:T(8,128)S(1)}, u32[]{:S(2)}, u32[]{:S(2)}) collective-permute-start(f32[4,128,256]{2,1,0:T(8,128)S(1)} %add.54), channel_id=1, source_target_pairs={{0,16},{8,72},{16,32},{24,88},{32,48},{40,104},{48,0},{56,120},{64... | collective-permute-start | bytes 1572872 | tf_op jit(solution)/shard_map/major_sum/ppermute | solution.py:249
  11.4 13.6 %collective-permute-start.6 = (f32[4,128,256]{2,1,0:T(8,128)S(1)}, f32[4,128,256]{2,1,0:T(8,128)S(1)}, u32[]{:S(2)}, u32[]{:S(2)}) collective-permute-start(f32[4,128,256]{2,1,0:T(8,128)S(1)} %add.56), channel_id=1, source_target_pairs={{0,48},{8,200},{16,0},{24,216},{32,16},{40,232},{48,32},{56,248},{... | collective-permute-start | bytes 1572872 | tf_op jit(solution)/shard_map/major_sum/ppermute | solution.py:249
  25.3 7.5 %collective-permute-start.9 = (f32[320,256]{1,0:T(8,128)S(1)}, f32[320,256]{1,0:T(8,128)S(1)}, u32[]{:S(2)}, u32[]{:S(2)}) collective-permute-start(f32[320,256]{1,0:T(8,128)S(1)} %pad_maximum_fusion.5), channel_id=1, source_target_pairs={{0,192},{8,56},{16,208},{24,40},{32,224},{40,24},{48,240},{56,8},{... | collective-permute-start | bytes 983048 | tf_op jit(solution)/shard_map/minor_sum/ppermute | solution.py:249
  26.6 6.5 %collective-permute-start.7 = (f32[320,256]{1,0:T(8,128)S(1)}, f32[320,256]{1,0:T(8,128)S(1)}, u32[]{:S(2)}, u32[]{:S(2)}) collective-permute-start(f32[320,256]{1,0:T(8,128)S(1)} %pad_maximum_fusion.4), channel_id=1, source_target_pairs={{0,64},{8,24},{16,80},{24,8},{32,96},{40,56},{48,112},{56,40},{64,... | collective-permute-start | bytes 983048 | tf_op jit(solution)/shard_map/minor_sum/ppermute | solution.py:249
  32.9 7.0 %collective-permute-start.10 = (f32[384,256]{1,0:T(8,128)S(1)}, f32[384,256]{1,0:T(8,128)S(1)}, u32[]{:S(2)}, u32[]{:S(2)}) collective-permute-start(f32[384,256]{1,0:T(8,128)S(1)} %pad_maximum_fusion.3), channel_id=1, source_target_pairs={{0,64},{8,24},{16,80},{24,8},{32,96},{40,56},{48,112},{56,40},{64,... | collective-permute-start | bytes 1179656 | tf_op jit(solution)/shard_map/minor_sum/ppermute | solution.py:249
  33.1 8.2 %collective-permute-start.8 = (f32[384,256]{1,0:T(8,128)S(1)}, f32[384,256]{1,0:T(8,128)S(1)}, u32[]{:S(2)}, u32[]{:S(2)}) collective-permute-start(f32[384,256]{1,0:T(8,128)S(1)} %pad_maximum_fusion.2), channel_id=1, source_target_pairs={{0,192},{8,56},{16,208},{24,40},{32,224},{40,24},{48,240},{56,8},{... | collective-permute-start | bytes 1179656 | tf_op jit(solution)/shard_map/minor_sum/ppermute | solution.py:249
  41.6 15.2 %collective-permute-start.12 = (f32[1024,256]{1,0:T(8,128)S(1)}, f32[1024,256]{1,0:T(8,128)S(1)}, u32[]{:S(2)}, u32[]{:S(2)}) collective-permute-start(f32[1024,256]{1,0:T(8,128)S(1)} %slice_dynamic-update-slice_fusion.refs_0_), channel_id=1, source_target_pairs={{0,48},{8,200},{16,0},{24,216},{32,16},{40,232},{48,32},{56,248},{... | collective-permute-start | bytes 3145736 | tf_op jit(solution)/shard_map/major_gather/ppermute | solution.py:249
  43.8 15.2 %collective-permute-start.11 = (f32[1024,256]{1,0:T(8,128)S(1)}, f32[1024,256]{1,0:T(8,128)S(1)}, u32[]{:S(2)}, u32[]{:S(2)}) collective-permute-start(f32[1024,256]{1,0:T(8,128)S(1)} %slice_dynamic-update-slice_fusion.refs_0_), channel_id=1, source_target_pairs={{0,16},{8,72},{16,32},{24,88},{32,48},{40,104},{48,0},{56,120},{64... | collective-permute-start | bytes 3145736 | tf_op jit(solution)/shard_map/major_gather/ppermute | solution.py:249
  43.9 2.8 %collective-permute-start.13 = (f32[8,256]{1,0:T(8,128)S(1)}, f32[8,256]{1,0:T(8,128)S(1)}, u32[]{:S(2)}, u32[]{:S(2)}) collective-permute-start(f32[8,256]{1,0:T(8,128)S(1)} %squares.1), channel_id=1, source_target_pairs={{0,1},{1,0},{2,3},{3,2},{4,5},{5,4},{6,7},{7,6},{8,9},{9,8},{10,11... | collective-permute-start | bytes 24584 | tf_op jit(solution)/shard_map/square_sum/ppermute | solution.py:275
  46.7 4.0 %collective-permute-start.14 = (f32[8,256]{1,0:T(8,128)S(1)}, f32[8,256]{1,0:T(8,128)S(1)}, u32[]{:S(2)}, u32[]{:S(2)}) collective-permute-start(f32[8,256]{1,0:T(8,128)S(1)} %add.62), channel_id=1, source_target_pairs={{0,2},{1,3},{2,0},{3,1},{4,6},{5,7},{6,4},{7,5},{8,10},{9,11},{10,... | collective-permute-start | bytes 24584 | tf_op jit(solution)/shard_map/square_sum/ppermute | solution.py:277
  50.7 6.1 %collective-permute-start.15 = (f32[8,256]{1,0:T(8,128)S(1)}, f32[8,256]{1,0:T(8,128)S(1)}, u32[]{:S(2)}, u32[]{:S(2)}) collective-permute-start(f32[8,256]{1,0:T(8,128)S(1)} %add.63), channel_id=1, source_target_pairs={{0,7},{1,6},{2,5},{3,4},{4,3},{5,2},{6,1},{7,0},{8,15},{9,14},{10,... | collective-permute-start | bytes 24584 | tf_op jit(solution)/shard_map/square_sum/ppermute | solution.py:277
  59.1 6.5 %collective-permute-start.19 = (f32[512,256]{1,0:T(8,128)S(1)}, f32[512,256]{1,0:T(8,128)S(1)}, u32[]{:S(2)}, u32[]{:S(2)}) collective-permute-start(f32[512,256]{1,0:T(8,128)S(1)} %get-tuple-element.64), channel_id=1, source_target_pairs={{0,8},{8,0},{16,24},{24,16},{32,40},{40,32},{48,56},{56,48},{64,72... | collective-permute-start | bytes 1572872 | tf_op jit(solution)/shard_map/core_gather/ppermute | solution.py:249
  63.5 16.4 %copy-start = (f32[128,256]{1,0:T(8,128)S(1)}, f32[128,256]{1,0:T(8,128)}, u32[]{:S(2)}) copy-start(f32[128,256]{1,0:T(8,128)} %refs_13_.1) | copy-start | bytes 393220
  63.5 2.5 %collective-permute-start.18 = (f32[512,256]{1,0:T(8,128)S(1)}, f32[512,256]{1,0:T(8,128)S(1)}, u32[]{:S(2)}, u32[]{:S(2)}) collective-permute-start(f32[512,256]{1,0:T(8,128)S(1)} %get-tuple-element.65), channel_id=1, source_target_pairs={{0,8},{8,0},{16,24},{24,16},{32,40},{40,32},{48,56},{56,48},{64,72... | collective-permute-start | bytes 1572872 | tf_op jit(solution)/shard_map/core_gather/ppermute | solution.py:249
  63.7 4.4 %collective-permute-start.21 = (f32[512,256]{1,0:T(8,128)S(1)}, f32[512,256]{1,0:T(8,128)S(1)}, u32[]{:S(2)}, u32[]{:S(2)}) collective-permute-start(f32[512,256]{1,0:T(8,128)S(1)} %get-tuple-element.62), channel_id=1, source_target_pairs={{0,8},{8,0},{16,24},{24,16},{32,40},{40,32},{48,56},{56,48},{64,72... | collective-permute-start | bytes 1572872 | tf_op jit(solution)/shard_map/core_gather/ppermute | solution.py:249
  64.2 4.0 %collective-permute-start.20 = (f32[512,256]{1,0:T(8,128)S(1)}, f32[512,256]{1,0:T(8,128)S(1)}, u32[]{:S(2)}, u32[]{:S(2)}) collective-permute-start(f32[512,256]{1,0:T(8,128)S(1)} %get-tuple-element.63), channel_id=1, source_target_pairs={{0,8},{8,0},{16,24},{24,16},{32,40},{40,32},{48,56},{56,48},{64,72... | collective-permute-start | bytes 1572872 | tf_op jit(solution)/shard_map/core_gather/ppermute | solution.py:249
  64.4 9.7 %collective-permute-start.17 = (f32[520,256]{1,0:T(8,128)S(1)}, f32[520,256]{1,0:T(8,128)S(1)}, u32[]{:S(2)}, u32[]{:S(2)}) collective-permute-start(f32[520,256]{1,0:T(8,128)S(1)} %get-tuple-element.72), channel_id=1, source_target_pairs={{0,48},{8,200},{16,0},{24,216},{32,16},{40,232},{48,32},{56,248},{... | collective-permute-start | bytes 1597448 | tf_op jit(solution)/shard_map/major_forward/ppermute | solution.py:249
  65.5 9.7 %collective-permute-start.16 = (f32[520,256]{1,0:T(8,128)S(1)}, f32[520,256]{1,0:T(8,128)S(1)}, u32[]{:S(2)}, u32[]{:S(2)}) collective-permute-start(f32[520,256]{1,0:T(8,128)S(1)} %get-tuple-element.73), channel_id=1, source_target_pairs={{0,16},{8,72},{16,32},{24,88},{32,48},{40,104},{48,0},{56,120},{64... | collective-permute-start | bytes 1597448 | tf_op jit(solution)/shard_map/major_forward/ppermute | solution.py:249
  66.0 3.7 %collective-permute-start.22 = (f32[512,256]{1,0:T(8,128)S(1)}, f32[512,256]{1,0:T(8,128)S(1)}, u32[]{:S(2)}, u32[]{:S(2)}) collective-permute-start(f32[512,256]{1,0:T(8,128)S(1)} %get-tuple-element.60), channel_id=1, source_target_pairs={{0,8},{8,0},{16,24},{24,16},{32,40},{40,32},{48,56},{56,48},{64,72... | collective-permute-start | bytes 1572872 | tf_op jit(solution)/shard_map/core_gather/ppermute | solution.py:249
  68.1 2.3 %collective-permute-start.23 = (f32[512,256]{1,0:T(8,128)S(1)}, f32[512,256]{1,0:T(8,128)S(1)}, u32[]{:S(2)}, u32[]{:S(2)}) collective-permute-start(f32[512,256]{1,0:T(8,128)S(1)} %get-tuple-element.61), channel_id=1, source_target_pairs={{0,8},{8,0},{16,24},{24,16},{32,40},{40,32},{48,56},{56,48},{64,72... | collective-permute-start | bytes 1572872 | tf_op jit(solution)/shard_map/core_gather/ppermute | solution.py:249
  68.2 5.9 %collective-permute-start.24 = (f32[8,256]{1,0:T(8,128)S(1)}, f32[8,256]{1,0:T(8,128)S(1)}, u32[]{:S(2)}, u32[]{:S(2)}) collective-permute-start(f32[8,256]{1,0:T(8,128)S(1)} %add.64), channel_id=1, source_target_pairs={{0,32},{8,136},{16,48},{24,152},{32,0},{40,168},{48,16},{56,184},{... | collective-permute-start | bytes 24584 | tf_op jit(solution)/shard_map/square_sum/ppermute | solution.py:249
  75.2 4.2 %collective-permute-start.25 = (f32[8,256]{1,0:T(8,128)S(1)}, f32[8,256]{1,0:T(8,128)S(1)}, u32[]{:S(2)}, u32[]{:S(2)}) collective-permute-start(f32[8,256]{1,0:T(8,128)S(1)} %slice_add_fusion.4.refs_11_.refs_2_), channel_id=1, source_target_pairs={{0,8},{8,0},{16,24},{24,16},{32,40},{40,32},{48,56},{56,48},{64,72... | collective-permute-start | bytes 24584 | tf_op jit(solution)/shard_map/update/ppermute | solution.py:249
  79.4 3.4 %collective-permute-start.26 = (f32[512,256]{1,0:T(8,128)S(1)}, f32[512,256]{1,0:T(8,128)S(1)}, u32[]{:S(2)}, u32[]{:S(2)}) collective-permute-start(f32[512,256]{1,0:T(8,128)S(1)} %slice.86.refs_3_), channel_id=1, source_target_pairs={{0,8},{8,0},{16,24},{24,16},{32,40},{40,32},{48,56},{56,48},{64,72... | collective-permute-start | bytes 1572872 | tf_op jit(solution)/shard_map/update/ppermute | solution.py:249
  79.8 3.0 %collective-permute-start.27 = (f32[512,256]{1,0:T(8,128)S(1)}, f32[512,256]{1,0:T(8,128)S(1)}, u32[]{:S(2)}, u32[]{:S(2)}) collective-permute-start(f32[512,256]{1,0:T(8,128)S(1)} %slice.87.refs_4_), channel_id=1, source_target_pairs={{0,8},{8,0},{16,24},{24,16},{32,40},{40,32},{48,56},{56,48},{64,72... | collective-permute-start | bytes 1572872 | tf_op jit(solution)/shard_map/update/ppermute | solution.py:249

commit v3 on v1

--- a/solution.py
+++ b/solution.py
@@ -11,7 +11,7 @@
 BLOCK = 128
 SIDE = 4
 WIDTH = 256
-LOADS = 8
+LOADS = 2
 STEPS = (2, 1, 3)
 
 FP8_LIMIT = 448.0

time: 84 us -> 83.3 us (level)
  no operation moved by 1% of the time
where the time goes in v3:
time: 83.3 us; the launch traced here: 83.2 us
  waiting for transfers between devices  38.6 us (46%)
  starting transfers between devices  35.9 us (43%)
  Pallas kernels  6.42 us (8%)
  between operations  1.04 us (1%)
  other arithmetic  0.86 us (1%)
    ppermute x24, waiting for transfers between devices, move(): return lax.ppermute(value, 'replica', perm)  35.2 us
    ppermute x24, starting transfers between devices, move(): return lax.ppermute(value, 'replica', perm)  26.4 us
    ppermute x2, starting transfers between devices, per_device(): squares = squares + lax.ppermute(squares, 'fsdp', perm)  7.76 us
    pallas_call x1, Pallas kernels, encode(): pl.pallas_call(encode_kernel, out_shape=[*blocks, *blocks, jax.ShapeDtype...  3.29 us
    pallas_call x1, Pallas kernels, update(): pl.pallas_call(functools.partial(update_kernel, threshold), out_shape=[ja...  3.07 us
    ppermute x2, waiting for transfers between devices, per_device(): squares = squares + lax.ppermute(squares, 'fsdp', perm)  2.37 us
    ppermute x1, starting transfers between devices, per_device(): squares = squares + lax.ppermute(squares, 'fsdp', Z_ROUNDS[0])  1.72 us
  transfers between devices with their start and end apart: 27, of which 15 were waited for; matrix products, arithmetic and copies ran while one was open for 1% of the time, Pallas kernels for 0%

profile of v3, /device:TPU:1, one launch (start us, length us, event | category | flops | bytes accessed | tf_op | source)
XLA Modules:
  0.0 83.2 jit_solution(12120962395167536676)
XLA Ops:
  0.6 3.3 %encode.1 = (f32[4,128,256]{2,1,0:T(8,128)S(1)}, f32[4,128,256]{2,1,0:T(8,128)S(1)}, f32[4,128,256]{2,1,0:T(8,128)S(1)}, f32[4,128,256]{2,1,0:T(8,128)S(1)}, f32...) custom-call(f32[128,8192]{1,0:T(8,128)} %weights.1, ...), custom_call_target="tpu_custom_call" | custom-call | flops 4194304 | bytes 6291456 | tf_op jit(solution)/shard_map/core_sum/encode/pallas_call | solution.py:132
  3.9 3.3 %collective-permute-start.1 = (f32[4,128,256]{2,1,0:T(8,128)S(1)}, f32[4,128,256]{2,1,0:T(8,128)S(1)}, u32[]{:S(2)}, u32[]{:S(2)}) collective-permute-start(f32[4,128,256]{2,1,0:T(8,128)S(1)} %get-tuple-element.28), channel_id=1, source_target_pairs={{0,8},{8,0},{16,24},{24,16},{32,40},{40,32},{48,56},{56,48},{64,72... | collective-permute-start | bytes 1572872 | tf_op jit(solution)/shard_map/core_sum/ppermute | solution.py:243
  7.2 0.1 collective-permute-start.3
  7.3 0.4 collective-permute-start.5
  7.8 0.1 collective-permute-start
  7.9 0.9 %collective-permute-done.1 = f32[4,128,256]{2,1,0:T(8,128)S(1)} collective-permute-done((f32[4,128,256]{2,1,0:T(8,128)S(1)}, f32[4,128,256]{2,1,0:T(8,128)S(1)}, u32[]{:S(2)}, u32[]{:S(2)}) %collective-permute-start.1) | collective-permute-done | bytes 524320 | tf_op jit(solution)/shard_map/core_sum/ppermute | solution.py:243
  8.8 0.1 add.52
  8.9 1.3 %collective-permute-start.2 = (f32[4,128,256]{2,1,0:T(8,128)S(1)}, f32[4,128,256]{2,1,0:T(8,128)S(1)}, u32[]{:S(2)}, u32[]{:S(2)}) collective-permute-start(f32[4,128,256]{2,1,0:T(8,128)S(1)} %add.52), channel_id=1, source_target_pairs={{0,32},{8,136},{16,48},{24,152},{32,0},{40,168},{48,16},{56,184},{... | collective-permute-start | bytes 1572872 | tf_op jit(solution)/shard_map/major_sum/ppermute | solution.py:243
  10.1 0.0 collective-permute-done.3
  10.1 0.1 add.54
  10.2 0.5 collective-permute-start.4
  10.7 0.0 collective-permute-done.5
  10.7 0.1 add.56
  10.7 2.4 %collective-permute-start.6 = (f32[4,128,256]{2,1,0:T(8,128)S(1)}, f32[4,128,256]{2,1,0:T(8,128)S(1)}, u32[]{:S(2)}, u32[]{:S(2)}) collective-permute-start(f32[4,128,256]{2,1,0:T(8,128)S(1)} %add.56), channel_id=1, source_target_pairs={{0,48},{8,200},{16,0},{24,216},{32,16},{40,232},{48,32},{56,248},{... | collective-permute-start | bytes 1572872 | tf_op jit(solution)/shard_map/major_sum/ppermute | solution.py:243
  13.1 0.0 collective-permute-done
  13.1 5.7 %collective-permute-done.2 = f32[4,128,256]{2,1,0:T(8,128)S(1)} collective-permute-done((f32[4,128,256]{2,1,0:T(8,128)S(1)}, f32[4,128,256]{2,1,0:T(8,128)S(1)}, u32[]{:S(2)}, u32[]{:S(2)}) %collective-permute-start.2) | collective-permute-done | bytes 524320 | tf_op jit(solution)/shard_map/major_sum/ppermute | solution.py:243
  18.8 5.6 %collective-permute-done.4 = f32[4,128,256]{2,1,0:T(8,128)S(1)} collective-permute-done((f32[4,128,256]{2,1,0:T(8,128)S(1)}, f32[4,128,256]{2,1,0:T(8,128)S(1)}, u32[]{:S(2)}, u32[]{:S(2)}) %collective-permute-start.4) | collective-permute-done | bytes 524320 | tf_op jit(solution)/shard_map/major_sum/ppermute | solution.py:243
  24.4 0.0 collective-permute-done.6
  24.4 0.2 add_add_fusion
  24.6 1.2 %collective-permute-start.9 = (f32[320,256]{1,0:T(8,128)S(1)}, f32[320,256]{1,0:T(8,128)S(1)}, u32[]{:S(2)}, u32[]{:S(2)}) collective-permute-start(f32[320,256]{1,0:T(8,128)S(1)} %pad_maximum_fusion.6), channel_id=1, source_target_pairs={{0,192},{8,56},{16,208},{24,40},{32,224},{40,24},{48,240},{56,8},{... | collective-permute-start | bytes 983048 | tf_op jit(solution)/shard_map/minor_sum/ppermute | solution.py:243
  25.9 0.1 collective-permute-start.7
  26.0 6.2 %collective-permute-done.9 = f32[320,256]{1,0:T(8,128)S(1)} collective-permute-done((f32[320,256]{1,0:T(8,128)S(1)}, f32[320,256]{1,0:T(8,128)S(1)}, u32[]{:S(2)}, u32[]{:S(2)}) %collective-permute-start.9) | collective-permute-done | bytes 327712 | tf_op jit(solution)/shard_map/minor_sum/ppermute | solution.py:243
  32.2 0.1 collective-permute-start.10
  32.3 0.0 collective-permute-done.7
  32.5 1.5 %collective-permute-start.8 = (f32[384,256]{1,0:T(8,128)S(1)}, f32[384,256]{1,0:T(8,128)S(1)}, u32[]{:S(2)}, u32[]{:S(2)}) collective-permute-start(f32[384,256]{1,0:T(8,128)S(1)} %pad_maximum_fusion.3), channel_id=1, source_target_pairs={{0,192},{8,56},{16,208},{24,40},{32,224},{40,24},{48,240},{56,8},{... | collective-permute-start | bytes 1179656 | tf_op jit(solution)/shard_map/minor_sum/ppermute | solution.py:243
  33.9 5.3 %collective-permute-done.10 = f32[384,256]{1,0:T(8,128)S(1)} collective-permute-done((f32[384,256]{1,0:T(8,128)S(1)}, f32[384,256]{1,0:T(8,128)S(1)}, u32[]{:S(2)}, u32[]{:S(2)}) %collective-permute-start.10) | collective-permute-done | bytes 393248 | tf_op jit(solution)/shard_map/minor_sum/ppermute | solution.py:243
  39.3 1.4 %collective-permute-done.8 = f32[384,256]{1,0:T(8,128)S(1)} collective-permute-done((f32[384,256]{1,0:T(8,128)S(1)}, f32[384,256]{1,0:T(8,128)S(1)}, u32[]{:S(2)}, u32[]{:S(2)}) %collective-permute-start.8) | collective-permute-done | bytes 393248 | tf_op jit(solution)/shard_map/minor_sum/ppermute | solution.py:243
  40.7 0.1 maximum_multiply_fusion
  40.9 2.3 %collective-permute-start.12 = (f32[1024,256]{1,0:T(8,128)S(1)}, f32[1024,256]{1,0:T(8,128)S(1)}, u32[]{:S(2)}, u32[]{:S(2)}) collective-permute-start(f32[1024,256]{1,0:T(8,128)S(1)} %slice_dynamic-update-slice_fusion.refs_0_), channel_id=1, source_target_pairs={{0,48},{8,200},{16,0},{24,216},{32,16},{40,232},{48,32},{56,248},{... | collective-permute-start | bytes 3145736 | tf_op jit(solution)/shard_map/major_gather/ppermute | solution.py:243
  43.1 0.1 squares.1
  43.2 1.7 %collective-permute-start.13 = (f32[8,256]{1,0:T(8,128)S(1)}, f32[8,256]{1,0:T(8,128)S(1)}, u32[]{:S(2)}, u32[]{:S(2)}) collective-permute-start(f32[8,256]{1,0:T(8,128)S(1)} %squares.1), channel_id=1, source_target_pairs={{0,1},{1,0},{2,3},{3,2},{4,5},{5,4},{6,7},{7,6},{8,9},{9,8},{10,11... | collective-permute-start | bytes 24584 | tf_op jit(solution)/shard_map/square_sum/ppermute | solution.py:269
  44.9 1.0 %collective-permute-done.13 = f32[8,256]{1,0:T(8,128)S(1)} collective-permute-done((f32[8,256]{1,0:T(8,128)S(1)}, f32[8,256]{1,0:T(8,128)S(1)}, u32[]{:S(2)}, u32[]{:S(2)}) %collective-permute-start.13) | collective-permute-done | bytes 8224 | tf_op jit(solution)/shard_map/square_sum/ppermute | solution.py:269
  46.0 3.0 %collective-permute-start.14 = (f32[8,256]{1,0:T(8,128)S(1)}, f32[8,256]{1,0:T(8,128)S(1)}, u32[]{:S(2)}, u32[]{:S(2)}) collective-permute-start(f32[8,256]{1,0:T(8,128)S(1)} %add.62), channel_id=1, source_target_pairs={{0,2},{1,3},{2,0},{3,1},{4,6},{5,7},{6,4},{7,5},{8,10},{9,11},{10,... | collective-permute-start | bytes 24584 | tf_op jit(solution)/shard_map/square_sum/ppermute | solution.py:271
  49.0 1.0 %collective-permute-done.14 = f32[8,256]{1,0:T(8,128)S(1)} collective-permute-done((f32[8,256]{1,0:T(8,128)S(1)}, f32[8,256]{1,0:T(8,128)S(1)}, u32[]{:S(2)}, u32[]{:S(2)}) %collective-permute-start.14) | collective-permute-done | bytes 8224 | tf_op jit(solution)/shard_map/square_sum/ppermute | solution.py:271
  50.0 4.8 %collective-permute-start.15 = (f32[8,256]{1,0:T(8,128)S(1)}, f32[8,256]{1,0:T(8,128)S(1)}, u32[]{:S(2)}, u32[]{:S(2)}) collective-permute-start(f32[8,256]{1,0:T(8,128)S(1)} %add.63), channel_id=1, source_target_pairs={{0,7},{1,6},{2,5},{3,4},{4,3},{5,2},{6,1},{7,0},{8,15},{9,14},{10,... | collective-permute-start | bytes 24584 | tf_op jit(solution)/shard_map/square_sum/ppermute | solution.py:271
  54.8 1.3 %collective-permute-done.15 = f32[8,256]{1,0:T(8,128)S(1)} collective-permute-done((f32[8,256]{1,0:T(8,128)S(1)}, f32[8,256]{1,0:T(8,128)S(1)}, u32[]{:S(2)}, u32[]{:S(2)}) %collective-permute-start.15) | collective-permute-done | bytes 8224 | tf_op jit(solution)/shard_map/square_sum/ppermute | solution.py:271
  56.1 0.0 collective-permute-done.12.refs_2_
  56.1 2.2 %collective-permute-done.11.refs_1_ = f32[1024,256]{1,0:T(8,128)S(1)} collective-permute-done((f32[1024,256]{1,0:T(8,128)S(1)}, f32[1024,256]{1,0:T(8,128)S(1)}, u32[]{:S(2)}, u32[]{:S(2)}) %collective-permute-start.11) | collective-permute-done | bytes 1048608 | tf_op jit(solution)/shard_map/major_gather/ppermute | solution.py:243
  58.3 0.1 fusion.2
  58.4 4.4 %collective-permute-start.19 = (f32[512,256]{1,0:T(8,128)S(1)}, f32[512,256]{1,0:T(8,128)S(1)}, u32[]{:S(2)}, u32[]{:S(2)}) collective-permute-start(f32[512,256]{1,0:T(8,128)S(1)} %get-tuple-element.52), channel_id=1, source_target_pairs={{0,8},{8,0},{16,24},{24,16},{32,40},{40,32},{48,56},{56,48},{64,72... | collective-permute-start | bytes 1572872 | tf_op jit(solution)/shard_map/core_gather/ppermute | solution.py:243
  62.8 0.1 collective-permute-start.18
  62.9 0.1 fusion.1
  63.0 0.0 copy-start
  63.0 0.5 collective-permute-start.21
  63.5 0.1 fusion
  63.6 0.1 pad_maximum_fusion
  63.7 1.1 %collective-permute-start.17 = (f32[520,256]{1,0:T(8,128)S(1)}, f32[520,256]{1,0:T(8,128)S(1)}, u32[]{:S(2)}, u32[]{:S(2)}) collective-permute-start(f32[520,256]{1,0:T(8,128)S(1)} %get-tuple-element.60), channel_id=1, source_target_pairs={{0,48},{8,200},{16,0},{24,216},{32,16},{40,232},{48,32},{56,248},{... | collective-permute-start | bytes 1597448 | tf_op jit(solution)/shard_map/major_forward/ppermute | solution.py:243
  64.8 0.5 collective-permute-start.16
  65.2 1.7 %collective-permute-start.20 = (f32[512,256]{1,0:T(8,128)S(1)}, f32[512,256]{1,0:T(8,128)S(1)}, u32[]{:S(2)}, u32[]{:S(2)}) collective-permute-start(f32[512,256]{1,0:T(8,128)S(1)} %get-tuple-element.51), channel_id=1, source_target_pairs={{0,8},{8,0},{16,24},{24,16},{32,40},{40,32},{48,56},{56,48},{64,72... | collective-permute-start | bytes 1572872 | tf_op jit(solution)/shard_map/core_gather/ppermute | solution.py:243
  66.9 0.0 collective-permute-done.18.refs_5_
  67.0 0.1 collective-permute-start.22
  67.1 0.0 collective-permute-done.21.refs_8_
  67.1 0.4 collective-permute-start.23
  67.5 1.0 %collective-permute-done.20.refs_7_ = f32[512,256]{1,0:T(8,128)S(1)} collective-permute-done((f32[512,256]{1,0:T(8,128)S(1)}, f32[512,256]{1,0:T(8,128)S(1)}, u32[]{:S(2)}, u32[]{:S(2)}) %collective-permute-start.20) | collective-permute-done | bytes 524320 | tf_op jit(solution)/shard_map/core_gather/ppermute | solution.py:243
  68.5 1.2 %collective-permute-start.24 = (f32[8,256]{1,0:T(8,128)S(1)}, f32[8,256]{1,0:T(8,128)S(1)}, u32[]{:S(2)}, u32[]{:S(2)}) collective-permute-start(f32[8,256]{1,0:T(8,128)S(1)} %add.64), channel_id=1, source_target_pairs={{0,32},{8,136},{16,48},{24,152},{32,0},{40,168},{48,16},{56,184},{... | collective-permute-start | bytes 24584 | tf_op jit(solution)/shard_map/square_sum/ppermute | solution.py:243
  69.7 0.0 collective-permute-done.22.refs_9_
  69.7 0.3 collective-permute-done.23.refs_10_
  70.0 2.2 %collective-permute-done.17 = f32[520,256]{1,0:T(8,128)S(1)} collective-permute-done((f32[520,256]{1,0:T(8,128)S(1)}, f32[520,256]{1,0:T(8,128)S(1)}, u32[]{:S(2)}, u32[]{:S(2)}) %collective-permute-start.17) | collective-permute-done | bytes 532512 | tf_op jit(solution)/shard_map/major_forward/ppermute | solution.py:243
  72.2 2.3 %collective-permute-done.16 = f32[520,256]{1,0:T(8,128)S(1)} collective-permute-done((f32[520,256]{1,0:T(8,128)S(1)}, f32[520,256]{1,0:T(8,128)S(1)}, u32[]{:S(2)}, u32[]{:S(2)}) %collective-permute-start.16) | collective-permute-done | bytes 532512 | tf_op jit(solution)/shard_map/major_forward/ppermute | solution.py:243
  74.5 0.0 collective-permute-done.24
  74.6 3.1 %collective-permute-start.26 = (f32[520,256]{1,0:T(8,128)S(1)}, f32[520,256]{1,0:T(8,128)S(1)}, u32[]{:S(2)}, u32[]{:S(2)}) collective-permute-start(f32[520,256]{1,0:T(8,128)S(1)} %pad_maximum_fusion.2.refs_4_), channel_id=1, source_target_pairs={{0,8},{8,0},{16,24},{24,16},{32,40},{40,32},{48,56},{56,48},{64,72... | collective-permute-start | bytes 1597448 | tf_op jit(solution)/shard_map/update/ppermute | solution.py:243
  77.7 0.1 collective-permute-start.25
  77.8 2.2 %collective-permute-done.25.refs_11_ = f32[512,256]{1,0:T(8,128)S(1)} collective-permute-done((f32[512,256]{1,0:T(8,128)S(1)}, f32[512,256]{1,0:T(8,128)S(1)}, u32[]{:S(2)}, u32[]{:S(2)}) %collective-permute-start.25) | collective-permute-done | bytes 524320 | tf_op jit(solution)/shard_map/update/ppermute | solution.py:243
  80.0 3.1 %update.1 = (f32[128,256]{1,0:T(8,128)}, f32[128,8192]{1,0:T(8,128)}) custom-call(f32[1024,256]{1,0:T(8,128)S(1)} %slice_dynamic-update-slice_fusion.refs_0_, f32[1024,256]{1,0:T(8,128)S(1)} %collective-permute-done.11.refs_1_, f32[1024,256]{1,0:T(8,128)S(1)} %collective-permute-done.12.refs_2_, f32[512,256]{1,0:T(8,128)S(1)} %slice.86.refs_3_, ...), custom_call_target="tpu_custom_call" | custom-call | flops 2097152 | bytes 4194304 | tf_op jit(solution)/shard_map/update/update/pallas_call | solution.py:214
  (29 shorter events, 0.5 us)
Async XLA Ops:
  3.9 4.9 %collective-permute-start.1 = (f32[4,128,256]{2,1,0:T(8,128)S(1)}, f32[4,128,256]{2,1,0:T(8,128)S(1)}, u32[]{:S(2)}, u32[]{:S(2)}) collective-permute-start(f32[4,128,256]{2,1,0:T(8,128)S(1)} %get-tuple-element.28), channel_id=1, source_target_pairs={{0,8},{8,0},{16,24},{24,16},{32,40},{40,32},{48,56},{56,48},{64,72... | collective-permute-start | bytes 1572872 | tf_op jit(solution)/shard_map/core_sum/ppermute | solution.py:243
  7.2 2.9 %collective-permute-start.3 = (f32[4,128,256]{2,1,0:T(8,128)S(1)}, f32[4,128,256]{2,1,0:T(8,128)S(1)}, u32[]{:S(2)}, u32[]{:S(2)}) collective-permute-start(f32[4,128,256]{2,1,0:T(8,128)S(1)} %get-tuple-element.30), channel_id=1, source_target_pairs={{0,8},{8,0},{16,24},{24,16},{32,40},{40,32},{48,56},{56,48},{64,72... | collective-permute-start | bytes 1572872 | tf_op jit(solution)/shard_map/core_sum/ppermute | solution.py:243
  7.3 3.3 %collective-permute-start.5 = (f32[4,128,256]{2,1,0:T(8,128)S(1)}, f32[4,128,256]{2,1,0:T(8,128)S(1)}, u32[]{:S(2)}, u32[]{:S(2)}) collective-permute-start(f32[4,128,256]{2,1,0:T(8,128)S(1)} %get-tuple-element.32), channel_id=1, source_target_pairs={{0,8},{8,0},{16,24},{24,16},{32,40},{40,32},{48,56},{56,48},{64,72... | collective-permute-start | bytes 1572872 | tf_op jit(solution)/shard_map/core_sum/ppermute | solution.py:243
  7.8 5.4 %collective-permute-start = (f32[4,128,256]{2,1,0:T(8,128)S(1)}, f32[4,128,256]{2,1,0:T(8,128)S(1)}, u32[]{:S(2)}, u32[]{:S(2)}) collective-permute-start(f32[4,128,256]{2,1,0:T(8,128)S(1)} %get-tuple-element.26), channel_id=1, source_target_pairs={{0,8},{8,0},{16,24},{24,16},{32,40},{40,32},{48,56},{56,48},{64,72... | collective-permute-start | bytes 1572872 | tf_op jit(solution)/shard_map/core_sum/ppermute | solution.py:243
  8.9 10.0 %collective-permute-start.2 = (f32[4,128,256]{2,1,0:T(8,128)S(1)}, f32[4,128,256]{2,1,0:T(8,128)S(1)}, u32[]{:S(2)}, u32[]{:S(2)}) collective-permute-start(f32[4,128,256]{2,1,0:T(8,128)S(1)} %add.52), channel_id=1, source_target_pairs={{0,32},{8,136},{16,48},{24,152},{32,0},{40,168},{48,16},{56,184},{... | collective-permute-start | bytes 1572872 | tf_op jit(solution)/shard_map/major_sum/ppermute | solution.py:243
  10.2 14.2 %collective-permute-start.4 = (f32[4,128,256]{2,1,0:T(8,128)S(1)}, f32[4,128,256]{2,1,0:T(8,128)S(1)}, u32[]{:S(2)}, u32[]{:S(2)}) collective-permute-start(f32[4,128,256]{2,1,0:T(8,128)S(1)} %add.54), channel_id=1, source_target_pairs={{0,16},{8,72},{16,32},{24,88},{32,48},{40,104},{48,0},{56,120},{64... | collective-permute-start | bytes 1572872 | tf_op jit(solution)/shard_map/major_sum/ppermute | solution.py:243
  10.7 13.6 %collective-permute-start.6 = (f32[4,128,256]{2,1,0:T(8,128)S(1)}, f32[4,128,256]{2,1,0:T(8,128)S(1)}, u32[]{:S(2)}, u32[]{:S(2)}) collective-permute-start(f32[4,128,256]{2,1,0:T(8,128)S(1)} %add.56), channel_id=1, source_target_pairs={{0,48},{8,200},{16,0},{24,216},{32,16},{40,232},{48,32},{56,248},{... | collective-permute-start | bytes 1572872 | tf_op jit(solution)/shard_map/major_sum/ppermute | solution.py:243
  24.6 7.5 %collective-permute-start.9 = (f32[320,256]{1,0:T(8,128)S(1)}, f32[320,256]{1,0:T(8,128)S(1)}, u32[]{:S(2)}, u32[]{:S(2)}) collective-permute-start(f32[320,256]{1,0:T(8,128)S(1)} %pad_maximum_fusion.6), channel_id=1, source_target_pairs={{0,192},{8,56},{16,208},{24,40},{32,224},{40,24},{48,240},{56,8},{... | collective-permute-start | bytes 983048 | tf_op jit(solution)/shard_map/minor_sum/ppermute | solution.py:243
  25.9 6.5 %collective-permute-start.7 = (f32[320,256]{1,0:T(8,128)S(1)}, f32[320,256]{1,0:T(8,128)S(1)}, u32[]{:S(2)}, u32[]{:S(2)}) collective-permute-start(f32[320,256]{1,0:T(8,128)S(1)} %pad_maximum_fusion.5), channel_id=1, source_target_pairs={{0,64},{8,24},{16,80},{24,8},{32,96},{40,56},{48,112},{56,40},{64,... | collective-permute-start | bytes 983048 | tf_op jit(solution)/shard_map/minor_sum/ppermute | solution.py:243
  32.2 7.0 %collective-permute-start.10 = (f32[384,256]{1,0:T(8,128)S(1)}, f32[384,256]{1,0:T(8,128)S(1)}, u32[]{:S(2)}, u32[]{:S(2)}) collective-permute-start(f32[384,256]{1,0:T(8,128)S(1)} %pad_maximum_fusion.4), channel_id=1, source_target_pairs={{0,64},{8,24},{16,80},{24,8},{32,96},{40,56},{48,112},{56,40},{64,... | collective-permute-start | bytes 1179656 | tf_op jit(solution)/shard_map/minor_sum/ppermute | solution.py:243
  32.5 8.2 %collective-permute-start.8 = (f32[384,256]{1,0:T(8,128)S(1)}, f32[384,256]{1,0:T(8,128)S(1)}, u32[]{:S(2)}, u32[]{:S(2)}) collective-permute-start(f32[384,256]{1,0:T(8,128)S(1)} %pad_maximum_fusion.3), channel_id=1, source_target_pairs={{0,192},{8,56},{16,208},{24,40},{32,224},{40,24},{48,240},{56,8},{... | collective-permute-start | bytes 1179656 | tf_op jit(solution)/shard_map/minor_sum/ppermute | solution.py:243
  40.9 15.2 %collective-permute-start.12 = (f32[1024,256]{1,0:T(8,128)S(1)}, f32[1024,256]{1,0:T(8,128)S(1)}, u32[]{:S(2)}, u32[]{:S(2)}) collective-permute-start(f32[1024,256]{1,0:T(8,128)S(1)} %slice_dynamic-update-slice_fusion.refs_0_), channel_id=1, source_target_pairs={{0,48},{8,200},{16,0},{24,216},{32,16},{40,232},{48,32},{56,248},{... | collective-permute-start | bytes 3145736 | tf_op jit(solution)/shard_map/major_gather/ppermute | solution.py:243
  43.1 15.2 %collective-permute-start.11 = (f32[1024,256]{1,0:T(8,128)S(1)}, f32[1024,256]{1,0:T(8,128)S(1)}, u32[]{:S(2)}, u32[]{:S(2)}) collective-permute-start(f32[1024,256]{1,0:T(8,128)S(1)} %slice_dynamic-update-slice_fusion.refs_0_), channel_id=1, source_target_pairs={{0,16},{8,72},{16,32},{24,88},{32,48},{40,104},{48,0},{56,120},{64... | collective-permute-start | bytes 3145736 | tf_op jit(solution)/shard_map/major_gather/ppermute | solution.py:243
  43.2 2.8 %collective-permute-start.13 = (f32[8,256]{1,0:T(8,128)S(1)}, f32[8,256]{1,0:T(8,128)S(1)}, u32[]{:S(2)}, u32[]{:S(2)}) collective-permute-start(f32[8,256]{1,0:T(8,128)S(1)} %squares.1), channel_id=1, source_target_pairs={{0,1},{1,0},{2,3},{3,2},{4,5},{5,4},{6,7},{7,6},{8,9},{9,8},{10,11... | collective-permute-start | bytes 24584 | tf_op jit(solution)/shard_map/square_sum/ppermute | solution.py:269
  46.0 4.0 %collective-permute-start.14 = (f32[8,256]{1,0:T(8,128)S(1)}, f32[8,256]{1,0:T(8,128)S(1)}, u32[]{:S(2)}, u32[]{:S(2)}) collective-permute-start(f32[8,256]{1,0:T(8,128)S(1)} %add.62), channel_id=1, source_target_pairs={{0,2},{1,3},{2,0},{3,1},{4,6},{5,7},{6,4},{7,5},{8,10},{9,11},{10,... | collective-permute-start | bytes 24584 | tf_op jit(solution)/shard_map/square_sum/ppermute | solution.py:271
  50.0 6.1 %collective-permute-start.15 = (f32[8,256]{1,0:T(8,128)S(1)}, f32[8,256]{1,0:T(8,128)S(1)}, u32[]{:S(2)}, u32[]{:S(2)}) collective-permute-start(f32[8,256]{1,0:T(8,128)S(1)} %add.63), channel_id=1, source_target_pairs={{0,7},{1,6},{2,5},{3,4},{4,3},{5,2},{6,1},{7,0},{8,15},{9,14},{10,... | collective-permute-start | bytes 24584 | tf_op jit(solution)/shard_map/square_sum/ppermute | solution.py:271
  58.4 6.8 %collective-permute-start.19 = (f32[512,256]{1,0:T(8,128)S(1)}, f32[512,256]{1,0:T(8,128)S(1)}, u32[]{:S(2)}, u32[]{:S(2)}) collective-permute-start(f32[512,256]{1,0:T(8,128)S(1)} %get-tuple-element.52), channel_id=1, source_target_pairs={{0,8},{8,0},{16,24},{24,16},{32,40},{40,32},{48,56},{56,48},{64,72... | collective-permute-start | bytes 1572872 | tf_op jit(solution)/shard_map/core_gather/ppermute | solution.py:243
  62.8 4.1 %collective-permute-start.18 = (f32[512,256]{1,0:T(8,128)S(1)}, f32[512,256]{1,0:T(8,128)S(1)}, u32[]{:S(2)}, u32[]{:S(2)}) collective-permute-start(f32[512,256]{1,0:T(8,128)S(1)} %get-tuple-element.53), channel_id=1, source_target_pairs={{0,8},{8,0},{16,24},{24,16},{32,40},{40,32},{48,56},{56,48},{64,72... | collective-permute-start | bytes 1572872 | tf_op jit(solution)/shard_map/core_gather/ppermute | solution.py:243
  63.0 17.0 %copy-start = (f32[128,256]{1,0:T(8,128)S(1)}, f32[128,256]{1,0:T(8,128)}, u32[]{:S(2)}) copy-start(f32[128,256]{1,0:T(8,128)} %refs_13_.1) | copy-start | bytes 393220
  63.0 4.1 %collective-permute-start.21 = (f32[512,256]{1,0:T(8,128)S(1)}, f32[512,256]{1,0:T(8,128)S(1)}, u32[]{:S(2)}, u32[]{:S(2)}) collective-permute-start(f32[512,256]{1,0:T(8,128)S(1)} %get-tuple-element.50), channel_id=1, source_target_pairs={{0,8},{8,0},{16,24},{24,16},{32,40},{40,32},{48,56},{56,48},{64,72... | collective-permute-start | bytes 1572872 | tf_op jit(solution)/shard_map/core_gather/ppermute | solution.py:243
  63.7 8.5 %collective-permute-start.17 = (f32[520,256]{1,0:T(8,128)S(1)}, f32[520,256]{1,0:T(8,128)S(1)}, u32[]{:S(2)}, u32[]{:S(2)}) collective-permute-start(f32[520,256]{1,0:T(8,128)S(1)} %get-tuple-element.60), channel_id=1, source_target_pairs={{0,48},{8,200},{16,0},{24,216},{32,16},{40,232},{48,32},{56,248},{... | collective-permute-start | bytes 1597448 | tf_op jit(solution)/shard_map/major_forward/ppermute | solution.py:243
  64.8 9.7 %collective-permute-start.16 = (f32[520,256]{1,0:T(8,128)S(1)}, f32[520,256]{1,0:T(8,128)S(1)}, u32[]{:S(2)}, u32[]{:S(2)}) collective-permute-start(f32[520,256]{1,0:T(8,128)S(1)} %get-tuple-element.61), channel_id=1, source_target_pairs={{0,16},{8,72},{16,32},{24,88},{32,48},{40,104},{48,0},{56,120},{64... | collective-permute-start | bytes 1597448 | tf_op jit(solution)/shard_map/major_forward/ppermute | solution.py:243
  65.2 3.3 %collective-permute-start.20 = (f32[512,256]{1,0:T(8,128)S(1)}, f32[512,256]{1,0:T(8,128)S(1)}, u32[]{:S(2)}, u32[]{:S(2)}) collective-permute-start(f32[512,256]{1,0:T(8,128)S(1)} %get-tuple-element.51), channel_id=1, source_target_pairs={{0,8},{8,0},{16,24},{24,16},{32,40},{40,32},{48,56},{56,48},{64,72... | collective-permute-start | bytes 1572872 | tf_op jit(solution)/shard_map/core_gather/ppermute | solution.py:243
  67.0 2.8 %collective-permute-start.22 = (f32[512,256]{1,0:T(8,128)S(1)}, f32[512,256]{1,0:T(8,128)S(1)}, u32[]{:S(2)}, u32[]{:S(2)}) collective-permute-start(f32[512,256]{1,0:T(8,128)S(1)} %get-tuple-element.48), channel_id=1, source_target_pairs={{0,8},{8,0},{16,24},{24,16},{32,40},{40,32},{48,56},{56,48},{64,72... | collective-permute-start | bytes 1572872 | tf_op jit(solution)/shard_map/core_gather/ppermute | solution.py:243
  67.1 2.9 %collective-permute-start.23 = (f32[512,256]{1,0:T(8,128)S(1)}, f32[512,256]{1,0:T(8,128)S(1)}, u32[]{:S(2)}, u32[]{:S(2)}) collective-permute-start(f32[512,256]{1,0:T(8,128)S(1)} %get-tuple-element.49), channel_id=1, source_target_pairs={{0,8},{8,0},{16,24},{24,16},{32,40},{40,32},{48,56},{56,48},{64,72... | collective-permute-start | bytes 1572872 | tf_op jit(solution)/shard_map/core_gather/ppermute | solution.py:243
  68.5 6.0 %collective-permute-start.24 = (f32[8,256]{1,0:T(8,128)S(1)}, f32[8,256]{1,0:T(8,128)S(1)}, u32[]{:S(2)}, u32[]{:S(2)}) collective-permute-start(f32[8,256]{1,0:T(8,128)S(1)} %add.64), channel_id=1, source_target_pairs={{0,32},{8,136},{16,48},{24,152},{32,0},{40,168},{48,16},{56,184},{... | collective-permute-start | bytes 24584 | tf_op jit(solution)/shard_map/square_sum/ppermute | solution.py:243
  74.6 5.4 %collective-permute-start.26 = (f32[520,256]{1,0:T(8,128)S(1)}, f32[520,256]{1,0:T(8,128)S(1)}, u32[]{:S(2)}, u32[]{:S(2)}) collective-permute-start(f32[520,256]{1,0:T(8,128)S(1)} %pad_maximum_fusion.2.refs_4_), channel_id=1, source_target_pairs={{0,8},{8,0},{16,24},{24,16},{32,40},{40,32},{48,56},{56,48},{64,72... | collective-permute-start | bytes 1597448 | tf_op jit(solution)/shard_map/update/ppermute | solution.py:243
  77.7 2.3 %collective-permute-start.25 = (f32[512,256]{1,0:T(8,128)S(1)}, f32[512,256]{1,0:T(8,128)S(1)}, u32[]{:S(2)}, u32[]{:S(2)}) collective-permute-start(f32[512,256]{1,0:T(8,128)S(1)} %slice.86.refs_3_), channel_id=1, source_target_pairs={{0,8},{8,0},{16,24},{24,16},{32,40},{40,32},{48,56},{56,48},{64,72... | collective-permute-start | bytes 1572872 | tf_op jit(solution)/shard_map/update/ppermute | solution.py:243

commit v4 on v3

--- a/solution.py
+++ b/solution.py
@@ -12,6 +12,7 @@
 SIDE = 4
 WIDTH = 256
 LOADS = 2
+GROUPS = 4
 STEPS = (2, 1, 3)
 
 FP8_LIMIT = 448.0
@@ -184,7 +185,7 @@
     own = [(k, mine[n], 0, mine[n], size) for n, k in enumerate((0, 1, 3))]
     own.append((2, mine[3], 0, mine[4], 0))
     other = [(k, handed[2 * n], 0, handed[2 * n + 1], 0) for n, k in enumerate((0, 1, 3, 2))]
-    copies = []
+    work = []
     for side, sources in ((core, own), (1 - core, other)):
         major, minor = axes_of(me, side)
         for k, averages, first, bases, offset in sources:
@@ -193,15 +194,20 @@
                 apart = minor ^ j
                 low = jnp.where(apart < 2, apart, 5 - apart)
                 high = jnp.where(apart == 0, 0, lax.rem(apart, SIDE - 1) + 1)
-                at = len(copies)
-                for n, slot in enumerate((low, SIDE + high)):
-                    base = pl.ds(pl.multiple_of(offset + slot * half, half), half)
-                    average = averages[first + j * rows + n * half : first + j * rows + (n + 1) * half, :]
-                    buf[at, n * half : (n + 1) * half, :] = bases[base, :] - rate * average
-                columns = columns_of(owner_of(side, place, j))
-                copy = pltpu.make_async_copy(buf.at[at], out.at[:, columns], sem.at[at])
-                copy.start()
-                copies.append(copy)
+                places = offset + low * half, offset + (SIDE + high) * half
+                work.append((averages, first + j * rows, bases, places, columns_of(owner_of(side, place, j))))
+    copies = []
+    group = rows // GROUPS
+    for g in range(GROUPS):
+        top = g * group
+        part = pl.ds(top, group)
+        for averages, first, bases, places, columns in work:
+            start = places[top // half] + top % half
+            base = bases[pl.ds(pl.multiple_of(start, group), group), :]
+            buf[part, columns] = base - rate * averages[first + top : first + top + group, :]
+        copy = pltpu.make_async_copy(buf.at[part], out.at[part], sem.at[g])
+        copy.start()
+        copies.append(copy)
     here = pl.ds(pl.multiple_of(axes_of(me, core)[1] * rows, rows), rows)
     new_momentum[...] = OUTER_MOMENTUM * momentum[...] + factor * mine[0][here, :]
     for copy in copies:
@@ -210,7 +216,6 @@
 
 def update(cols, threshold, mine, handed, momentum):
     rows = momentum.shape[0]
-    chunks = 2 * SIDE * SIDE
     return pl.pallas_call(
         functools.partial(update_kernel, threshold),
         out_shape=[
@@ -220,8 +225,8 @@
         in_specs=[VMEM] * (len(mine) + len(handed) + 1),
         out_specs=[VMEM, HBM],
         scratch_shapes=[
-            pltpu.VMEM((chunks, rows, WIDTH), jnp.float32),
-            pltpu.SemaphoreType.DMA((chunks,)),
+            pltpu.VMEM((rows, cols), jnp.float32),
+            pltpu.SemaphoreType.DMA((GROUPS,)),
         ],
         compiler_params=pltpu.CompilerParams(vmem_limit_bytes=SCOPED),
         cost_estimate=pl.CostEstimate(flops=2**21, bytes_accessed=2**22, transcendentals=0),

time: 83.3 us -> 83.3 us (level)
  no operation moved by 1% of the time
where the time goes in v4:
time: 83.3 us; the launch traced here: 83.2 us
  waiting for transfers between devices  38.6 us (46%)
  starting transfers between devices  35.9 us (43%)
  Pallas kernels  6.41 us (8%)
  between operations  1.04 us (1%)
  other arithmetic  0.86 us (1%)
    ppermute x24, waiting for transfers between devices, move(): return lax.ppermute(value, 'replica', perm)  35.2 us
    ppermute x24, starting transfers between devices, move(): return lax.ppermute(value, 'replica', perm)  26.4 us
    ppermute x2, starting transfers between devices, per_device(): squares = squares + lax.ppermute(squares, 'fsdp', perm)  7.76 us
    pallas_call x1, Pallas kernels, encode(): pl.pallas_call(encode_kernel, out_shape=[*blocks, *blocks, jax.ShapeDtype...  3.29 us
    pallas_call x1, Pallas kernels, update(): pl.pallas_call(functools.partial(update_kernel, threshold), out_shape=[ja...  3.06 us
    ppermute x2, waiting for transfers between devices, per_device(): squares = squares + lax.ppermute(squares, 'fsdp', perm)  2.37 us
    ppermute x1, starting transfers between devices, per_device(): squares = squares + lax.ppermute(squares, 'fsdp', Z_ROUNDS[0])  1.72 us
  transfers between devices with their start and end apart: 27, of which 15 were waited for; matrix products, arithmetic and copies ran while one was open for 1% of the time, Pallas kernels for 0%

profile of v4, /device:TPU:1, one launch (start us, length us, event | category | flops | bytes accessed | tf_op | source)
XLA Modules:
  0.0 83.2 jit_solution(6255042450306673854)
XLA Ops:
  0.6 3.3 %encode.1 = (f32[4,128,256]{2,1,0:T(8,128)S(1)}, f32[4,128,256]{2,1,0:T(8,128)S(1)}, f32[4,128,256]{2,1,0:T(8,128)S(1)}, f32[4,128,256]{2,1,0:T(8,128)S(1)}, f32...) custom-call(f32[128,8192]{1,0:T(8,128)} %weights.1, ...), custom_call_target="tpu_custom_call" | custom-call | flops 4194304 | bytes 6291456 | tf_op jit(solution)/shard_map/core_sum/encode/pallas_call | solution.py:133
  3.9 3.3 %collective-permute-start.1 = (f32[4,128,256]{2,1,0:T(8,128)S(1)}, f32[4,128,256]{2,1,0:T(8,128)S(1)}, u32[]{:S(2)}, u32[]{:S(2)}) collective-permute-start(f32[4,128,256]{2,1,0:T(8,128)S(1)} %get-tuple-element.28), channel_id=1, source_target_pairs={{0,8},{8,0},{16,24},{24,16},{32,40},{40,32},{48,56},{56,48},{64,72... | collective-permute-start | bytes 1572872 | tf_op jit(solution)/shard_map/core_sum/ppermute | solution.py:248
  7.2 0.1 collective-permute-start.3
  7.3 0.4 collective-permute-start.5
  7.8 0.1 collective-permute-start
  7.9 0.9 %collective-permute-done.1 = f32[4,128,256]{2,1,0:T(8,128)S(1)} collective-permute-done((f32[4,128,256]{2,1,0:T(8,128)S(1)}, f32[4,128,256]{2,1,0:T(8,128)S(1)}, u32[]{:S(2)}, u32[]{:S(2)}) %collective-permute-start.1) | collective-permute-done | bytes 524320 | tf_op jit(solution)/shard_map/core_sum/ppermute | solution.py:248
  8.8 0.1 add.52
  8.9 1.3 %collective-permute-start.2 = (f32[4,128,256]{2,1,0:T(8,128)S(1)}, f32[4,128,256]{2,1,0:T(8,128)S(1)}, u32[]{:S(2)}, u32[]{:S(2)}) collective-permute-start(f32[4,128,256]{2,1,0:T(8,128)S(1)} %add.52), channel_id=1, source_target_pairs={{0,32},{8,136},{16,48},{24,152},{32,0},{40,168},{48,16},{56,184},{... | collective-permute-start | bytes 1572872 | tf_op jit(solution)/shard_map/major_sum/ppermute | solution.py:248
  10.1 0.0 collective-permute-done.3
  10.1 0.1 add.54
  10.2 0.5 collective-permute-start.4
  10.7 0.0 collective-permute-done.5
  10.7 0.1 add.56
  10.7 2.4 %collective-permute-start.6 = (f32[4,128,256]{2,1,0:T(8,128)S(1)}, f32[4,128,256]{2,1,0:T(8,128)S(1)}, u32[]{:S(2)}, u32[]{:S(2)}) collective-permute-start(f32[4,128,256]{2,1,0:T(8,128)S(1)} %add.56), channel_id=1, source_target_pairs={{0,48},{8,200},{16,0},{24,216},{32,16},{40,232},{48,32},{56,248},{... | collective-permute-start | bytes 1572872 | tf_op jit(solution)/shard_map/major_sum/ppermute | solution.py:248
  13.1 0.0 collective-permute-done
  13.1 5.7 %collective-permute-done.2 = f32[4,128,256]{2,1,0:T(8,128)S(1)} collective-permute-done((f32[4,128,256]{2,1,0:T(8,128)S(1)}, f32[4,128,256]{2,1,0:T(8,128)S(1)}, u32[]{:S(2)}, u32[]{:S(2)}) %collective-permute-start.2) | collective-permute-done | bytes 524320 | tf_op jit(solution)/shard_map/major_sum/ppermute | solution.py:248
  18.8 5.6 %collective-permute-done.4 = f32[4,128,256]{2,1,0:T(8,128)S(1)} collective-permute-done((f32[4,128,256]{2,1,0:T(8,128)S(1)}, f32[4,128,256]{2,1,0:T(8,128)S(1)}, u32[]{:S(2)}, u32[]{:S(2)}) %collective-permute-start.4) | collective-permute-done | bytes 524320 | tf_op jit(solution)/shard_map/major_sum/ppermute | solution.py:248
  24.4 0.0 collective-permute-done.6
  24.4 0.2 add_add_fusion
  24.6 1.2 %collective-permute-start.9 = (f32[320,256]{1,0:T(8,128)S(1)}, f32[320,256]{1,0:T(8,128)S(1)}, u32[]{:S(2)}, u32[]{:S(2)}) collective-permute-start(f32[320,256]{1,0:T(8,128)S(1)} %pad_maximum_fusion.6), channel_id=1, source_target_pairs={{0,192},{8,56},{16,208},{24,40},{32,224},{40,24},{48,240},{56,8},{... | collective-permute-start | bytes 983048 | tf_op jit(solution)/shard_map/minor_sum/ppermute | solution.py:248
  25.9 0.1 collective-permute-start.7
  26.0 6.2 %collective-permute-done.9 = f32[320,256]{1,0:T(8,128)S(1)} collective-permute-done((f32[320,256]{1,0:T(8,128)S(1)}, f32[320,256]{1,0:T(8,128)S(1)}, u32[]{:S(2)}, u32[]{:S(2)}) %collective-permute-start.9) | collective-permute-done | bytes 327712 | tf_op jit(solution)/shard_map/minor_sum/ppermute | solution.py:248
  32.2 0.1 collective-permute-start.10
  32.3 0.0 collective-permute-done.7
  32.5 1.5 %collective-permute-start.8 = (f32[384,256]{1,0:T(8,128)S(1)}, f32[384,256]{1,0:T(8,128)S(1)}, u32[]{:S(2)}, u32[]{:S(2)}) collective-permute-start(f32[384,256]{1,0:T(8,128)S(1)} %pad_maximum_fusion.3), channel_id=1, source_target_pairs={{0,192},{8,56},{16,208},{24,40},{32,224},{40,24},{48,240},{56,8},{... | collective-permute-start | bytes 1179656 | tf_op jit(solution)/shard_map/minor_sum/ppermute | solution.py:248
  33.9 5.3 %collective-permute-done.10 = f32[384,256]{1,0:T(8,128)S(1)} collective-permute-done((f32[384,256]{1,0:T(8,128)S(1)}, f32[384,256]{1,0:T(8,128)S(1)}, u32[]{:S(2)}, u32[]{:S(2)}) %collective-permute-start.10) | collective-permute-done | bytes 393248 | tf_op jit(solution)/shard_map/minor_sum/ppermute | solution.py:248
  39.3 1.4 %collective-permute-done.8 = f32[384,256]{1,0:T(8,128)S(1)} collective-permute-done((f32[384,256]{1,0:T(8,128)S(1)}, f32[384,256]{1,0:T(8,128)S(1)}, u32[]{:S(2)}, u32[]{:S(2)}) %collective-permute-start.8) | collective-permute-done | bytes 393248 | tf_op jit(solution)/shard_map/minor_sum/ppermute | solution.py:248
  40.7 0.1 maximum_multiply_fusion
  40.9 2.3 %collective-permute-start.12 = (f32[1024,256]{1,0:T(8,128)S(1)}, f32[1024,256]{1,0:T(8,128)S(1)}, u32[]{:S(2)}, u32[]{:S(2)}) collective-permute-start(f32[1024,256]{1,0:T(8,128)S(1)} %slice_dynamic-update-slice_fusion.refs_0_), channel_id=1, source_target_pairs={{0,48},{8,200},{16,0},{24,216},{32,16},{40,232},{48,32},{56,248},{... | collective-permute-start | bytes 3145736 | tf_op jit(solution)/shard_map/major_gather/ppermute | solution.py:248
  43.1 0.0 collective-permute-start.11
  43.1 0.1 squares.1
  43.2 1.7 %collective-permute-start.13 = (f32[8,256]{1,0:T(8,128)S(1)}, f32[8,256]{1,0:T(8,128)S(1)}, u32[]{:S(2)}, u32[]{:S(2)}) collective-permute-start(f32[8,256]{1,0:T(8,128)S(1)} %squares.1), channel_id=1, source_target_pairs={{0,1},{1,0},{2,3},{3,2},{4,5},{5,4},{6,7},{7,6},{8,9},{9,8},{10,11... | collective-permute-start | bytes 24584 | tf_op jit(solution)/shard_map/square_sum/ppermute | solution.py:274
  44.9 1.0 %collective-permute-done.13 = f32[8,256]{1,0:T(8,128)S(1)} collective-permute-done((f32[8,256]{1,0:T(8,128)S(1)}, f32[8,256]{1,0:T(8,128)S(1)}, u32[]{:S(2)}, u32[]{:S(2)}) %collective-permute-start.13) | collective-permute-done | bytes 8224 | tf_op jit(solution)/shard_map/square_sum/ppermute | solution.py:274
  46.0 3.0 %collective-permute-start.14 = (f32[8,256]{1,0:T(8,128)S(1)}, f32[8,256]{1,0:T(8,128)S(1)}, u32[]{:S(2)}, u32[]{:S(2)}) collective-permute-start(f32[8,256]{1,0:T(8,128)S(1)} %add.62), channel_id=1, source_target_pairs={{0,2},{1,3},{2,0},{3,1},{4,6},{5,7},{6,4},{7,5},{8,10},{9,11},{10,... | collective-permute-start | bytes 24584 | tf_op jit(solution)/shard_map/square_sum/ppermute | solution.py:276
  49.0 1.0 %collective-permute-done.14 = f32[8,256]{1,0:T(8,128)S(1)} collective-permute-done((f32[8,256]{1,0:T(8,128)S(1)}, f32[8,256]{1,0:T(8,128)S(1)}, u32[]{:S(2)}, u32[]{:S(2)}) %collective-permute-start.14) | collective-permute-done | bytes 8224 | tf_op jit(solution)/shard_map/square_sum/ppermute | solution.py:276
  50.0 4.8 %collective-permute-start.15 = (f32[8,256]{1,0:T(8,128)S(1)}, f32[8,256]{1,0:T(8,128)S(1)}, u32[]{:S(2)}, u32[]{:S(2)}) collective-permute-start(f32[8,256]{1,0:T(8,128)S(1)} %add.63), channel_id=1, source_target_pairs={{0,7},{1,6},{2,5},{3,4},{4,3},{5,2},{6,1},{7,0},{8,15},{9,14},{10,... | collective-permute-start | bytes 24584 | tf_op jit(solution)/shard_map/square_sum/ppermute | solution.py:276
  54.8 1.3 %collective-permute-done.15 = f32[8,256]{1,0:T(8,128)S(1)} collective-permute-done((f32[8,256]{1,0:T(8,128)S(1)}, f32[8,256]{1,0:T(8,128)S(1)}, u32[]{:S(2)}, u32[]{:S(2)}) %collective-permute-start.15) | collective-permute-done | bytes 8224 | tf_op jit(solution)/shard_map/square_sum/ppermute | solution.py:276
  56.1 0.0 collective-permute-done.12.refs_2_
  56.1 2.2 %collective-permute-done.11.refs_1_ = f32[1024,256]{1,0:T(8,128)S(1)} collective-permute-done((f32[1024,256]{1,0:T(8,128)S(1)}, f32[1024,256]{1,0:T(8,128)S(1)}, u32[]{:S(2)}, u32[]{:S(2)}) %collective-permute-start.11) | collective-permute-done | bytes 1048608 | tf_op jit(solution)/shard_map/major_gather/ppermute | solution.py:248
  58.3 0.1 fusion.2
  58.4 4.4 %collective-permute-start.19 = (f32[512,256]{1,0:T(8,128)S(1)}, f32[512,256]{1,0:T(8,128)S(1)}, u32[]{:S(2)}, u32[]{:S(2)}) collective-permute-start(f32[512,256]{1,0:T(8,128)S(1)} %get-tuple-element.52), channel_id=1, source_target_pairs={{0,8},{8,0},{16,24},{24,16},{32,40},{40,32},{48,56},{56,48},{64,72... | collective-permute-start | bytes 1572872 | tf_op jit(solution)/shard_map/core_gather/ppermute | solution.py:248
  62.8 0.1 collective-permute-start.18
  62.9 0.1 fusion.1
  63.0 0.0 copy-start
  63.0 0.5 collective-permute-start.21
  63.5 0.1 fusion
  63.6 0.1 pad_maximum_fusion
  63.7 1.1 %collective-permute-start.17 = (f32[520,256]{1,0:T(8,128)S(1)}, f32[520,256]{1,0:T(8,128)S(1)}, u32[]{:S(2)}, u32[]{:S(2)}) collective-permute-start(f32[520,256]{1,0:T(8,128)S(1)} %get-tuple-element.60), channel_id=1, source_target_pairs={{0,48},{8,200},{16,0},{24,216},{32,16},{40,232},{48,32},{56,248},{... | collective-permute-start | bytes 1597448 | tf_op jit(solution)/shard_map/major_forward/ppermute | solution.py:248
  64.8 0.5 collective-permute-start.16
  65.2 0.0 collective-permute-done.19.refs_6_
  65.2 1.7 %collective-permute-start.20 = (f32[512,256]{1,0:T(8,128)S(1)}, f32[512,256]{1,0:T(8,128)S(1)}, u32[]{:S(2)}, u32[]{:S(2)}) collective-permute-start(f32[512,256]{1,0:T(8,128)S(1)} %get-tuple-element.51), channel_id=1, source_target_pairs={{0,8},{8,0},{16,24},{24,16},{32,40},{40,32},{48,56},{56,48},{64,72... | collective-permute-start | bytes 1572872 | tf_op jit(solution)/shard_map/core_gather/ppermute | solution.py:248
  66.9 0.0 collective-permute-done.18.refs_5_
  67.0 0.1 collective-permute-start.22
  67.1 0.0 collective-permute-done.21.refs_8_
  67.1 0.4 collective-permute-start.23
  67.5 1.0 %collective-permute-done.20.refs_7_ = f32[512,256]{1,0:T(8,128)S(1)} collective-permute-done((f32[512,256]{1,0:T(8,128)S(1)}, f32[512,256]{1,0:T(8,128)S(1)}, u32[]{:S(2)}, u32[]{:S(2)}) %collective-permute-start.20) | collective-permute-done | bytes 524320 | tf_op jit(solution)/shard_map/core_gather/ppermute | solution.py:248
  68.5 1.2 %collective-permute-start.24 = (f32[8,256]{1,0:T(8,128)S(1)}, f32[8,256]{1,0:T(8,128)S(1)}, u32[]{:S(2)}, u32[]{:S(2)}) collective-permute-start(f32[8,256]{1,0:T(8,128)S(1)} %add.64), channel_id=1, source_target_pairs={{0,32},{8,136},{16,48},{24,152},{32,0},{40,168},{48,16},{56,184},{... | collective-permute-start | bytes 24584 | tf_op jit(solution)/shard_map/square_sum/ppermute | solution.py:248
  69.7 0.3 collective-permute-done.23.refs_10_
  70.0 2.2 %collective-permute-done.17 = f32[520,256]{1,0:T(8,128)S(1)} collective-permute-done((f32[520,256]{1,0:T(8,128)S(1)}, f32[520,256]{1,0:T(8,128)S(1)}, u32[]{:S(2)}, u32[]{:S(2)}) %collective-permute-start.17) | collective-permute-done | bytes 532512 | tf_op jit(solution)/shard_map/major_forward/ppermute | solution.py:248
  72.2 2.3 %collective-permute-done.16 = f32[520,256]{1,0:T(8,128)S(1)} collective-permute-done((f32[520,256]{1,0:T(8,128)S(1)}, f32[520,256]{1,0:T(8,128)S(1)}, u32[]{:S(2)}, u32[]{:S(2)}) %collective-permute-start.16) | collective-permute-done | bytes 532512 | tf_op jit(solution)/shard_map/major_forward/ppermute | solution.py:248
  74.6 3.1 %collective-permute-start.26 = (f32[520,256]{1,0:T(8,128)S(1)}, f32[520,256]{1,0:T(8,128)S(1)}, u32[]{:S(2)}, u32[]{:S(2)}) collective-permute-start(f32[520,256]{1,0:T(8,128)S(1)} %pad_maximum_fusion.2.refs_4_), channel_id=1, source_target_pairs={{0,8},{8,0},{16,24},{24,16},{32,40},{40,32},{48,56},{56,48},{64,72... | collective-permute-start | bytes 1597448 | tf_op jit(solution)/shard_map/update/ppermute | solution.py:248
  77.7 0.1 collective-permute-start.25
  77.8 2.2 %collective-permute-done.25.refs_11_ = f32[512,256]{1,0:T(8,128)S(1)} collective-permute-done((f32[512,256]{1,0:T(8,128)S(1)}, f32[512,256]{1,0:T(8,128)S(1)}, u32[]{:S(2)}, u32[]{:S(2)}) %collective-permute-start.25) | collective-permute-done | bytes 524320 | tf_op jit(solution)/shard_map/update/ppermute | solution.py:248
  80.0 3.1 %update.1 = (f32[128,256]{1,0:T(8,128)}, f32[128,8192]{1,0:T(8,128)}) custom-call(f32[1024,256]{1,0:T(8,128)S(1)} %slice_dynamic-update-slice_fusion.refs_0_, f32[1024,256]{1,0:T(8,128)S(1)} %collective-permute-done.11.refs_1_, f32[1024,256]{1,0:T(8,128)S(1)} %collective-permute-done.12.refs_2_, f32[512,256]{1,0:T(8,128)S(1)} %slice.86.refs_3_, ...), custom_call_target="tpu_custom_call" | custom-call | flops 2097152 | bytes 4194304 | tf_op jit(solution)/shard_map/update/update/pallas_call | solution.py:219
  (29 shorter events, 0.5 us)
Async XLA Ops:
  3.9 4.9 %collective-permute-start.1 = (f32[4,128,256]{2,1,0:T(8,128)S(1)}, f32[4,128,256]{2,1,0:T(8,128)S(1)}, u32[]{:S(2)}, u32[]{:S(2)}) collective-permute-start(f32[4,128,256]{2,1,0:T(8,128)S(1)} %get-tuple-element.28), channel_id=1, source_target_pairs={{0,8},{8,0},{16,24},{24,16},{32,40},{40,32},{48,56},{56,48},{64,72... | collective-permute-start | bytes 1572872 | tf_op jit(solution)/shard_map/core_sum/ppermute | solution.py:248
  7.2 2.9 %collective-permute-start.3 = (f32[4,128,256]{2,1,0:T(8,128)S(1)}, f32[4,128,256]{2,1,0:T(8,128)S(1)}, u32[]{:S(2)}, u32[]{:S(2)}) collective-permute-start(f32[4,128,256]{2,1,0:T(8,128)S(1)} %get-tuple-element.30), channel_id=1, source_target_pairs={{0,8},{8,0},{16,24},{24,16},{32,40},{40,32},{48,56},{56,48},{64,72... | collective-permute-start | bytes 1572872 | tf_op jit(solution)/shard_map/core_sum/ppermute | solution.py:248
  7.3 3.3 %collective-permute-start.5 = (f32[4,128,256]{2,1,0:T(8,128)S(1)}, f32[4,128,256]{2,1,0:T(8,128)S(1)}, u32[]{:S(2)}, u32[]{:S(2)}) collective-permute-start(f32[4,128,256]{2,1,0:T(8,128)S(1)} %get-tuple-element.32), channel_id=1, source_target_pairs={{0,8},{8,0},{16,24},{24,16},{32,40},{40,32},{48,56},{56,48},{64,72... | collective-permute-start | bytes 1572872 | tf_op jit(solution)/shard_map/core_sum/ppermute | solution.py:248
  7.8 5.4 %collective-permute-start = (f32[4,128,256]{2,1,0:T(8,128)S(1)}, f32[4,128,256]{2,1,0:T(8,128)S(1)}, u32[]{:S(2)}, u32[]{:S(2)}) collective-permute-start(f32[4,128,256]{2,1,0:T(8,128)S(1)} %get-tuple-element.26), channel_id=1, source_target_pairs={{0,8},{8,0},{16,24},{24,16},{32,40},{40,32},{48,56},{56,48},{64,72... | collective-permute-start | bytes 1572872 | tf_op jit(solution)/shard_map/core_sum/ppermute | solution.py:248
  8.9 10.0 %collective-permute-start.2 = (f32[4,128,256]{2,1,0:T(8,128)S(1)}, f32[4,128,256]{2,1,0:T(8,128)S(1)}, u32[]{:S(2)}, u32[]{:S(2)}) collective-permute-start(f32[4,128,256]{2,1,0:T(8,128)S(1)} %add.52), channel_id=1, source_target_pairs={{0,32},{8,136},{16,48},{24,152},{32,0},{40,168},{48,16},{56,184},{... | collective-permute-start | bytes 1572872 | tf_op jit(solution)/shard_map/major_sum/ppermute | solution.py:248
  10.2 14.2 %collective-permute-start.4 = (f32[4,128,256]{2,1,0:T(8,128)S(1)}, f32[4,128,256]{2,1,0:T(8,128)S(1)}, u32[]{:S(2)}, u32[]{:S(2)}) collective-permute-start(f32[4,128,256]{2,1,0:T(8,128)S(1)} %add.54), channel_id=1, source_target_pairs={{0,16},{8,72},{16,32},{24,88},{32,48},{40,104},{48,0},{56,120},{64... | collective-permute-start | bytes 1572872 | tf_op jit(solution)/shard_map/major_sum/ppermute | solution.py:248
  10.7 13.6 %collective-permute-start.6 = (f32[4,128,256]{2,1,0:T(8,128)S(1)}, f32[4,128,256]{2,1,0:T(8,128)S(1)}, u32[]{:S(2)}, u32[]{:S(2)}) collective-permute-start(f32[4,128,256]{2,1,0:T(8,128)S(1)} %add.56), channel_id=1, source_target_pairs={{0,48},{8,200},{16,0},{24,216},{32,16},{40,232},{48,32},{56,248},{... | collective-permute-start | bytes 1572872 | tf_op jit(solution)/shard_map/major_sum/ppermute | solution.py:248
  24.6 7.5 %collective-permute-start.9 = (f32[320,256]{1,0:T(8,128)S(1)}, f32[320,256]{1,0:T(8,128)S(1)}, u32[]{:S(2)}, u32[]{:S(2)}) collective-permute-start(f32[320,256]{1,0:T(8,128)S(1)} %pad_maximum_fusion.6), channel_id=1, source_target_pairs={{0,192},{8,56},{16,208},{24,40},{32,224},{40,24},{48,240},{56,8},{... | collective-permute-start | bytes 983048 | tf_op jit(solution)/shard_map/minor_sum/ppermute | solution.py:248
  25.9 6.5 %collective-permute-start.7 = (f32[320,256]{1,0:T(8,128)S(1)}, f32[320,256]{1,0:T(8,128)S(1)}, u32[]{:S(2)}, u32[]{:S(2)}) collective-permute-start(f32[320,256]{1,0:T(8,128)S(1)} %pad_maximum_fusion.5), channel_id=1, source_target_pairs={{0,64},{8,24},{16,80},{24,8},{32,96},{40,56},{48,112},{56,40},{64,... | collective-permute-start | bytes 983048 | tf_op jit(solution)/shard_map/minor_sum/ppermute | solution.py:248
  32.2 7.0 %collective-permute-start.10 = (f32[384,256]{1,0:T(8,128)S(1)}, f32[384,256]{1,0:T(8,128)S(1)}, u32[]{:S(2)}, u32[]{:S(2)}) collective-permute-start(f32[384,256]{1,0:T(8,128)S(1)} %pad_maximum_fusion.4), channel_id=1, source_target_pairs={{0,64},{8,24},{16,80},{24,8},{32,96},{40,56},{48,112},{56,40},{64,... | collective-permute-start | bytes 1179656 | tf_op jit(solution)/shard_map/minor_sum/ppermute | solution.py:248
  32.5 8.2 %collective-permute-start.8 = (f32[384,256]{1,0:T(8,128)S(1)}, f32[384,256]{1,0:T(8,128)S(1)}, u32[]{:S(2)}, u32[]{:S(2)}) collective-permute-start(f32[384,256]{1,0:T(8,128)S(1)} %pad_maximum_fusion.3), channel_id=1, source_target_pairs={{0,192},{8,56},{16,208},{24,40},{32,224},{40,24},{48,240},{56,8},{... | collective-permute-start | bytes 1179656 | tf_op jit(solution)/shard_map/minor_sum/ppermute | solution.py:248
  40.9 15.2 %collective-permute-start.12 = (f32[1024,256]{1,0:T(8,128)S(1)}, f32[1024,256]{1,0:T(8,128)S(1)}, u32[]{:S(2)}, u32[]{:S(2)}) collective-permute-start(f32[1024,256]{1,0:T(8,128)S(1)} %slice_dynamic-update-slice_fusion.refs_0_), channel_id=1, source_target_pairs={{0,48},{8,200},{16,0},{24,216},{32,16},{40,232},{48,32},{56,248},{... | collective-permute-start | bytes 3145736 | tf_op jit(solution)/shard_map/major_gather/ppermute | solution.py:248
  43.1 15.2 %collective-permute-start.11 = (f32[1024,256]{1,0:T(8,128)S(1)}, f32[1024,256]{1,0:T(8,128)S(1)}, u32[]{:S(2)}, u32[]{:S(2)}) collective-permute-start(f32[1024,256]{1,0:T(8,128)S(1)} %slice_dynamic-update-slice_fusion.refs_0_), channel_id=1, source_target_pairs={{0,16},{8,72},{16,32},{24,88},{32,48},{40,104},{48,0},{56,120},{64... | collective-permute-start | bytes 3145736 | tf_op jit(solution)/shard_map/major_gather/ppermute | solution.py:248
  43.2 2.8 %collective-permute-start.13 = (f32[8,256]{1,0:T(8,128)S(1)}, f32[8,256]{1,0:T(8,128)S(1)}, u32[]{:S(2)}, u32[]{:S(2)}) collective-permute-start(f32[8,256]{1,0:T(8,128)S(1)} %squares.1), channel_id=1, source_target_pairs={{0,1},{1,0},{2,3},{3,2},{4,5},{5,4},{6,7},{7,6},{8,9},{9,8},{10,11... | collective-permute-start | bytes 24584 | tf_op jit(solution)/shard_map/square_sum/ppermute | solution.py:274
  46.0 4.0 %collective-permute-start.14 = (f32[8,256]{1,0:T(8,128)S(1)}, f32[8,256]{1,0:T(8,128)S(1)}, u32[]{:S(2)}, u32[]{:S(2)}) collective-permute-start(f32[8,256]{1,0:T(8,128)S(1)} %add.62), channel_id=1, source_target_pairs={{0,2},{1,3},{2,0},{3,1},{4,6},{5,7},{6,4},{7,5},{8,10},{9,11},{10,... | collective-permute-start | bytes 24584 | tf_op jit(solution)/shard_map/square_sum/ppermute | solution.py:276
  50.0 6.1 %collective-permute-start.15 = (f32[8,256]{1,0:T(8,128)S(1)}, f32[8,256]{1,0:T(8,128)S(1)}, u32[]{:S(2)}, u32[]{:S(2)}) collective-permute-start(f32[8,256]{1,0:T(8,128)S(1)} %add.63), channel_id=1, source_target_pairs={{0,7},{1,6},{2,5},{3,4},{4,3},{5,2},{6,1},{7,0},{8,15},{9,14},{10,... | collective-permute-start | bytes 24584 | tf_op jit(solution)/shard_map/square_sum/ppermute | solution.py:276
  58.4 6.8 %collective-permute-start.19 = (f32[512,256]{1,0:T(8,128)S(1)}, f32[512,256]{1,0:T(8,128)S(1)}, u32[]{:S(2)}, u32[]{:S(2)}) collective-permute-start(f32[512,256]{1,0:T(8,128)S(1)} %get-tuple-element.52), channel_id=1, source_target_pairs={{0,8},{8,0},{16,24},{24,16},{32,40},{40,32},{48,56},{56,48},{64,72... | collective-permute-start | bytes 1572872 | tf_op jit(solution)/shard_map/core_gather/ppermute | solution.py:248
  62.8 4.1 %collective-permute-start.18 = (f32[512,256]{1,0:T(8,128)S(1)}, f32[512,256]{1,0:T(8,128)S(1)}, u32[]{:S(2)}, u32[]{:S(2)}) collective-permute-start(f32[512,256]{1,0:T(8,128)S(1)} %get-tuple-element.53), channel_id=1, source_target_pairs={{0,8},{8,0},{16,24},{24,16},{32,40},{40,32},{48,56},{56,48},{64,72... | collective-permute-start | bytes 1572872 | tf_op jit(solution)/shard_map/core_gather/ppermute | solution.py:248
  63.0 17.0 %copy-start = (f32[128,256]{1,0:T(8,128)S(1)}, f32[128,256]{1,0:T(8,128)}, u32[]{:S(2)}) copy-start(f32[128,256]{1,0:T(8,128)} %refs_13_.1) | copy-start | bytes 393220
  63.0 4.1 %collective-permute-start.21 = (f32[512,256]{1,0:T(8,128)S(1)}, f32[512,256]{1,0:T(8,128)S(1)}, u32[]{:S(2)}, u32[]{:S(2)}) collective-permute-start(f32[512,256]{1,0:T(8,128)S(1)} %get-tuple-element.50), channel_id=1, source_target_pairs={{0,8},{8,0},{16,24},{24,16},{32,40},{40,32},{48,56},{56,48},{64,72... | collective-permute-start | bytes 1572872 | tf_op jit(solution)/shard_map/core_gather/ppermute | solution.py:248
  63.7 8.5 %collective-permute-start.17 = (f32[520,256]{1,0:T(8,128)S(1)}, f32[520,256]{1,0:T(8,128)S(1)}, u32[]{:S(2)}, u32[]{:S(2)}) collective-permute-start(f32[520,256]{1,0:T(8,128)S(1)} %get-tuple-element.60), channel_id=1, source_target_pairs={{0,48},{8,200},{16,0},{24,216},{32,16},{40,232},{48,32},{56,248},{... | collective-permute-start | bytes 1597448 | tf_op jit(solution)/shard_map/major_forward/ppermute | solution.py:248
  64.8 9.7 %collective-permute-start.16 = (f32[520,256]{1,0:T(8,128)S(1)}, f32[520,256]{1,0:T(8,128)S(1)}, u32[]{:S(2)}, u32[]{:S(2)}) collective-permute-start(f32[520,256]{1,0:T(8,128)S(1)} %get-tuple-element.61), channel_id=1, source_target_pairs={{0,16},{8,72},{16,32},{24,88},{32,48},{40,104},{48,0},{56,120},{64... | collective-permute-start | bytes 1597448 | tf_op jit(solution)/shard_map/major_forward/ppermute | solution.py:248
  65.2 3.3 %collective-permute-start.20 = (f32[512,256]{1,0:T(8,128)S(1)}, f32[512,256]{1,0:T(8,128)S(1)}, u32[]{:S(2)}, u32[]{:S(2)}) collective-permute-start(f32[512,256]{1,0:T(8,128)S(1)} %get-tuple-element.51), channel_id=1, source_target_pairs={{0,8},{8,0},{16,24},{24,16},{32,40},{40,32},{48,56},{56,48},{64,72... | collective-permute-start | bytes 1572872 | tf_op jit(solution)/shard_map/core_gather/ppermute | solution.py:248
  67.0 2.8 %collective-permute-start.22 = (f32[512,256]{1,0:T(8,128)S(1)}, f32[512,256]{1,0:T(8,128)S(1)}, u32[]{:S(2)}, u32[]{:S(2)}) collective-permute-start(f32[512,256]{1,0:T(8,128)S(1)} %get-tuple-element.48), channel_id=1, source_target_pairs={{0,8},{8,0},{16,24},{24,16},{32,40},{40,32},{48,56},{56,48},{64,72... | collective-permute-start | bytes 1572872 | tf_op jit(solution)/shard_map/core_gather/ppermute | solution.py:248
  67.1 2.9 %collective-permute-start.23 = (f32[512,256]{1,0:T(8,128)S(1)}, f32[512,256]{1,0:T(8,128)S(1)}, u32[]{:S(2)}, u32[]{:S(2)}) collective-permute-start(f32[512,256]{1,0:T(8,128)S(1)} %get-tuple-element.49), channel_id=1, source_target_pairs={{0,8},{8,0},{16,24},{24,16},{32,40},{40,32},{48,56},{56,48},{64,72... | collective-permute-start | bytes 1572872 | tf_op jit(solution)/shard_map/core_gather/ppermute | solution.py:248
  68.5 6.0 %collective-permute-start.24 = (f32[8,256]{1,0:T(8,128)S(1)}, f32[8,256]{1,0:T(8,128)S(1)}, u32[]{:S(2)}, u32[]{:S(2)}) collective-permute-start(f32[8,256]{1,0:T(8,128)S(1)} %add.64), channel_id=1, source_target_pairs={{0,32},{8,136},{16,48},{24,152},{32,0},{40,168},{48,16},{56,184},{... | collective-permute-start | bytes 24584 | tf_op jit(solution)/shard_map/square_sum/ppermute | solution.py:248
  74.6 5.4 %collective-permute-start.26 = (f32[520,256]{1,0:T(8,128)S(1)}, f32[520,256]{1,0:T(8,128)S(1)}, u32[]{:S(2)}, u32[]{:S(2)}) collective-permute-start(f32[520,256]{1,0:T(8,128)S(1)} %pad_maximum_fusion.2.refs_4_), channel_id=1, source_target_pairs={{0,8},{8,0},{16,24},{24,16},{32,40},{40,32},{48,56},{56,48},{64,72... | collective-permute-start | bytes 1597448 | tf_op jit(solution)/shard_map/update/ppermute | solution.py:248
  77.7 2.3 %collective-permute-start.25 = (f32[512,256]{1,0:T(8,128)S(1)}, f32[512,256]{1,0:T(8,128)S(1)}, u32[]{:S(2)}, u32[]{:S(2)}) collective-permute-start(f32[512,256]{1,0:T(8,128)S(1)} %slice.86.refs_3_), channel_id=1, source_target_pairs={{0,8},{8,0},{16,24},{24,16},{32,40},{40,32},{48,56},{56,48},{64,72... | collective-permute-start | bytes 1572872 | tf_op jit(solution)/shard_map/update/ppermute | solution.py:248

commit v5 on v4

--- a/solution.py
+++ b/solution.py
@@ -249,7 +249,9 @@
 
     with jax.named_scope("core_sum"):
         send, keep, base = encode(global_weights, replica_weights[0], exponents[0].T, momentum)
-        parts = [kept + move(sent, CORE_SWAP) for sent, kept in zip(send, keep)]
+        first = move(send[0], CORE_SWAP)
+        first, *others = tie(first, *send[1:])
+        parts = [kept + sent for sent, kept in zip((first, *(move(x, CORE_SWAP) for x in others)), keep)]
 
     with jax.named_scope("major_sum"):
         arrived = [move(part, major_shift(k)) for part, k in zip(parts, STEPS)]

time: 83.3 us -> 83.8 us (level)
  no operation moved by 1% of the time
where the time goes in v5:
time: 83.8 us; the launch traced here: 83.7 us
  waiting for transfers between devices  38.7 us (46%)
  starting transfers between devices  36.4 us (43%)
  Pallas kernels  6.41 us (8%)
  between operations  1.03 us (1%)
  other arithmetic  0.86 us (1%)
    ppermute x24, waiting for transfers between devices, move(): return lax.ppermute(value, 'replica', perm)  35.3 us
    ppermute x24, starting transfers between devices, move(): return lax.ppermute(value, 'replica', perm)  26.9 us
    ppermute x2, starting transfers between devices, per_device(): squares = squares + lax.ppermute(squares, 'fsdp', perm)  7.76 us
    pallas_call x1, Pallas kernels, encode(): pl.pallas_call(encode_kernel, out_shape=[*blocks, *blocks, jax.ShapeDtype...  3.29 us
    pallas_call x1, Pallas kernels, update(): pl.pallas_call(functools.partial(update_kernel, threshold), out_shape=[ja...  3.06 us
    ppermute x2, waiting for transfers between devices, per_device(): squares = squares + lax.ppermute(squares, 'fsdp', perm)  2.37 us
    ppermute x1, starting transfers between devices, per_device(): squares = squares + lax.ppermute(squares, 'fsdp', Z_ROUNDS[0])  1.72 us
  transfers between devices with their start and end apart: 27, of which 15 were waited for; matrix products, arithmetic and copies ran while one was open for 1% of the time, Pallas kernels for 0%

profile of v5, /device:TPU:1, one launch (start us, length us, event | category | flops | bytes accessed | tf_op | source)
XLA Modules:
  0.0 83.7 jit_solution(4531298563721568594)
XLA Ops:
  0.6 3.3 %encode.1 = (f32[4,128,256]{2,1,0:T(8,128)S(1)}, f32[4,128,256]{2,1,0:T(8,128)S(1)}, f32[4,128,256]{2,1,0:T(8,128)S(1)}, f32[4,128,256]{2,1,0:T(8,128)S(1)}, f32...) custom-call(f32[128,8192]{1,0:T(8,128)} %weights.1, ...), custom_call_target="tpu_custom_call" | custom-call | flops 4194304 | bytes 6291456 | tf_op jit(solution)/shard_map/core_sum/encode/pallas_call | solution.py:133
  3.9 3.3 %collective-permute-start = (f32[4,128,256]{2,1,0:T(8,128)S(1)}, f32[4,128,256]{2,1,0:T(8,128)S(1)}, u32[]{:S(2)}, u32[]{:S(2)}) collective-permute-start(f32[4,128,256]{2,1,0:T(8,128)S(1)} %get-tuple-element.30), channel_id=1, source_target_pairs={{0,8},{8,0},{16,24},{24,16},{32,40},{40,32},{48,56},{56,48},{64,72... | collective-permute-start | bytes 1572872 | tf_op jit(solution)/shard_map/core_sum/ppermute | solution.py:248
  7.2 1.5 %collective-permute-done = f32[4,128,256]{2,1,0:T(8,128)S(1)} collective-permute-done((f32[4,128,256]{2,1,0:T(8,128)S(1)}, f32[4,128,256]{2,1,0:T(8,128)S(1)}, u32[]{:S(2)}, u32[]{:S(2)}) %collective-permute-start) | collective-permute-done | bytes 524320 | tf_op jit(solution)/shard_map/core_sum/ppermute | solution.py:248
  8.8 0.4 collective-permute-start.3
  9.2 0.1 collective-permute-start.5
  9.3 0.1 add.52
  9.4 1.3 %collective-permute-start.2 = (f32[4,128,256]{2,1,0:T(8,128)S(1)}, f32[4,128,256]{2,1,0:T(8,128)S(1)}, u32[]{:S(2)}, u32[]{:S(2)}) collective-permute-start(f32[4,128,256]{2,1,0:T(8,128)S(1)} %add.52), channel_id=1, source_target_pairs={{0,32},{8,136},{16,48},{24,152},{32,0},{40,168},{48,16},{56,184},{... | collective-permute-start | bytes 1572872 | tf_op jit(solution)/shard_map/major_sum/ppermute | solution.py:248
  10.6 0.5 collective-permute-start.1
  11.1 0.0 collective-permute-done.3
  11.1 0.1 add.54
  11.2 1.4 %collective-permute-start.4 = (f32[4,128,256]{2,1,0:T(8,128)S(1)}, f32[4,128,256]{2,1,0:T(8,128)S(1)}, u32[]{:S(2)}, u32[]{:S(2)}) collective-permute-start(f32[4,128,256]{2,1,0:T(8,128)S(1)} %add.54), channel_id=1, source_target_pairs={{0,16},{8,72},{16,32},{24,88},{32,48},{40,104},{48,0},{56,120},{64... | collective-permute-start | bytes 1572872 | tf_op jit(solution)/shard_map/major_sum/ppermute | solution.py:248
  12.6 0.0 collective-permute-done.5
  12.6 0.1 add.56
  12.6 1.5 %collective-permute-start.6 = (f32[4,128,256]{2,1,0:T(8,128)S(1)}, f32[4,128,256]{2,1,0:T(8,128)S(1)}, u32[]{:S(2)}, u32[]{:S(2)}) collective-permute-start(f32[4,128,256]{2,1,0:T(8,128)S(1)} %add.56), channel_id=1, source_target_pairs={{0,48},{8,200},{16,0},{24,216},{32,16},{40,232},{48,32},{56,248},{... | collective-permute-start | bytes 1572872 | tf_op jit(solution)/shard_map/major_sum/ppermute | solution.py:248
  14.2 5.1 %collective-permute-done.2 = f32[4,128,256]{2,1,0:T(8,128)S(1)} collective-permute-done((f32[4,128,256]{2,1,0:T(8,128)S(1)}, f32[4,128,256]{2,1,0:T(8,128)S(1)}, u32[]{:S(2)}, u32[]{:S(2)}) %collective-permute-start.2) | collective-permute-done | bytes 524320 | tf_op jit(solution)/shard_map/major_sum/ppermute | solution.py:248
  19.3 0.0 collective-permute-done.1
  19.3 5.6 %collective-permute-done.4 = f32[4,128,256]{2,1,0:T(8,128)S(1)} collective-permute-done((f32[4,128,256]{2,1,0:T(8,128)S(1)}, f32[4,128,256]{2,1,0:T(8,128)S(1)}, u32[]{:S(2)}, u32[]{:S(2)}) %collective-permute-start.4) | collective-permute-done | bytes 524320 | tf_op jit(solution)/shard_map/major_sum/ppermute | solution.py:248
  24.9 0.0 collective-permute-done.6
  24.9 0.2 add_add_fusion
  25.2 1.2 %collective-permute-start.9 = (f32[320,256]{1,0:T(8,128)S(1)}, f32[320,256]{1,0:T(8,128)S(1)}, u32[]{:S(2)}, u32[]{:S(2)}) collective-permute-start(f32[320,256]{1,0:T(8,128)S(1)} %pad_maximum_fusion.6), channel_id=1, source_target_pairs={{0,192},{8,56},{16,208},{24,40},{32,224},{40,24},{48,240},{56,8},{... | collective-permute-start | bytes 983048 | tf_op jit(solution)/shard_map/minor_sum/ppermute | solution.py:248
  26.4 0.1 collective-permute-start.7
  26.5 6.2 %collective-permute-done.9 = f32[320,256]{1,0:T(8,128)S(1)} collective-permute-done((f32[320,256]{1,0:T(8,128)S(1)}, f32[320,256]{1,0:T(8,128)S(1)}, u32[]{:S(2)}, u32[]{:S(2)}) %collective-permute-start.9) | collective-permute-done | bytes 327712 | tf_op jit(solution)/shard_map/minor_sum/ppermute | solution.py:248
  32.8 0.1 collective-permute-start.10
  32.9 0.0 collective-permute-done.7
  33.0 1.5 %collective-permute-start.8 = (f32[384,256]{1,0:T(8,128)S(1)}, f32[384,256]{1,0:T(8,128)S(1)}, u32[]{:S(2)}, u32[]{:S(2)}) collective-permute-start(f32[384,256]{1,0:T(8,128)S(1)} %pad_maximum_fusion.3), channel_id=1, source_target_pairs={{0,192},{8,56},{16,208},{24,40},{32,224},{40,24},{48,240},{56,8},{... | collective-permute-start | bytes 1179656 | tf_op jit(solution)/shard_map/minor_sum/ppermute | solution.py:248
  34.4 5.3 %collective-permute-done.10 = f32[384,256]{1,0:T(8,128)S(1)} collective-permute-done((f32[384,256]{1,0:T(8,128)S(1)}, f32[384,256]{1,0:T(8,128)S(1)}, u32[]{:S(2)}, u32[]{:S(2)}) %collective-permute-start.10) | collective-permute-done | bytes 393248 | tf_op jit(solution)/shard_map/minor_sum/ppermute | solution.py:248
  39.8 1.4 %collective-permute-done.8 = f32[384,256]{1,0:T(8,128)S(1)} collective-permute-done((f32[384,256]{1,0:T(8,128)S(1)}, f32[384,256]{1,0:T(8,128)S(1)}, u32[]{:S(2)}, u32[]{:S(2)}) %collective-permute-start.8) | collective-permute-done | bytes 393248 | tf_op jit(solution)/shard_map/minor_sum/ppermute | solution.py:248
  41.2 0.1 maximum_multiply_fusion
  41.4 2.3 %collective-permute-start.12 = (f32[1024,256]{1,0:T(8,128)S(1)}, f32[1024,256]{1,0:T(8,128)S(1)}, u32[]{:S(2)}, u32[]{:S(2)}) collective-permute-start(f32[1024,256]{1,0:T(8,128)S(1)} %slice_dynamic-update-slice_fusion.refs_0_), channel_id=1, source_target_pairs={{0,48},{8,200},{16,0},{24,216},{32,16},{40,232},{48,32},{56,248},{... | collective-permute-start | bytes 3145736 | tf_op jit(solution)/shard_map/major_gather/ppermute | solution.py:248
  43.7 0.1 squares.1
  43.7 1.7 %collective-permute-start.13 = (f32[8,256]{1,0:T(8,128)S(1)}, f32[8,256]{1,0:T(8,128)S(1)}, u32[]{:S(2)}, u32[]{:S(2)}) collective-permute-start(f32[8,256]{1,0:T(8,128)S(1)} %squares.1), channel_id=1, source_target_pairs={{0,1},{1,0},{2,3},{3,2},{4,5},{5,4},{6,7},{7,6},{8,9},{9,8},{10,11... | collective-permute-start | bytes 24584 | tf_op jit(solution)/shard_map/square_sum/ppermute | solution.py:276
  45.4 1.0 %collective-permute-done.13 = f32[8,256]{1,0:T(8,128)S(1)} collective-permute-done((f32[8,256]{1,0:T(8,128)S(1)}, f32[8,256]{1,0:T(8,128)S(1)}, u32[]{:S(2)}, u32[]{:S(2)}) %collective-permute-start.13) | collective-permute-done | bytes 8224 | tf_op jit(solution)/shard_map/square_sum/ppermute | solution.py:276
  46.5 3.0 %collective-permute-start.14 = (f32[8,256]{1,0:T(8,128)S(1)}, f32[8,256]{1,0:T(8,128)S(1)}, u32[]{:S(2)}, u32[]{:S(2)}) collective-permute-start(f32[8,256]{1,0:T(8,128)S(1)} %add.62), channel_id=1, source_target_pairs={{0,2},{1,3},{2,0},{3,1},{4,6},{5,7},{6,4},{7,5},{8,10},{9,11},{10,... | collective-permute-start | bytes 24584 | tf_op jit(solution)/shard_map/square_sum/ppermute | solution.py:278
  49.5 1.0 %collective-permute-done.14 = f32[8,256]{1,0:T(8,128)S(1)} collective-permute-done((f32[8,256]{1,0:T(8,128)S(1)}, f32[8,256]{1,0:T(8,128)S(1)}, u32[]{:S(2)}, u32[]{:S(2)}) %collective-permute-start.14) | collective-permute-done | bytes 8224 | tf_op jit(solution)/shard_map/square_sum/ppermute | solution.py:278
  50.5 4.8 %collective-permute-start.15 = (f32[8,256]{1,0:T(8,128)S(1)}, f32[8,256]{1,0:T(8,128)S(1)}, u32[]{:S(2)}, u32[]{:S(2)}) collective-permute-start(f32[8,256]{1,0:T(8,128)S(1)} %add.63), channel_id=1, source_target_pairs={{0,7},{1,6},{2,5},{3,4},{4,3},{5,2},{6,1},{7,0},{8,15},{9,14},{10,... | collective-permute-start | bytes 24584 | tf_op jit(solution)/shard_map/square_sum/ppermute | solution.py:278
  55.3 1.3 %collective-permute-done.15 = f32[8,256]{1,0:T(8,128)S(1)} collective-permute-done((f32[8,256]{1,0:T(8,128)S(1)}, f32[8,256]{1,0:T(8,128)S(1)}, u32[]{:S(2)}, u32[]{:S(2)}) %collective-permute-start.15) | collective-permute-done | bytes 8224 | tf_op jit(solution)/shard_map/square_sum/ppermute | solution.py:278
  56.6 0.0 collective-permute-done.12.refs_2_
  56.6 2.2 %collective-permute-done.11.refs_1_ = f32[1024,256]{1,0:T(8,128)S(1)} collective-permute-done((f32[1024,256]{1,0:T(8,128)S(1)}, f32[1024,256]{1,0:T(8,128)S(1)}, u32[]{:S(2)}, u32[]{:S(2)}) %collective-permute-start.11) | collective-permute-done | bytes 1048608 | tf_op jit(solution)/shard_map/major_gather/ppermute | solution.py:248
  58.8 0.1 fusion.2
  58.9 4.4 %collective-permute-start.19 = (f32[512,256]{1,0:T(8,128)S(1)}, f32[512,256]{1,0:T(8,128)S(1)}, u32[]{:S(2)}, u32[]{:S(2)}) collective-permute-start(f32[512,256]{1,0:T(8,128)S(1)} %get-tuple-element.60), channel_id=1, source_target_pairs={{0,8},{8,0},{16,24},{24,16},{32,40},{40,32},{48,56},{56,48},{64,72... | collective-permute-start | bytes 1572872 | tf_op jit(solution)/shard_map/core_gather/ppermute | solution.py:248
  63.3 0.1 collective-permute-start.18
  63.4 0.1 fusion.1
  63.5 0.0 copy-start
  63.5 0.5 collective-permute-start.21
  64.0 0.1 fusion
  64.1 0.1 pad_maximum_fusion
  64.2 1.1 %collective-permute-start.17 = (f32[520,256]{1,0:T(8,128)S(1)}, f32[520,256]{1,0:T(8,128)S(1)}, u32[]{:S(2)}, u32[]{:S(2)}) collective-permute-start(f32[520,256]{1,0:T(8,128)S(1)} %get-tuple-element.68), channel_id=1, source_target_pairs={{0,48},{8,200},{16,0},{24,216},{32,16},{40,232},{48,32},{56,248},{... | collective-permute-start | bytes 1597448 | tf_op jit(solution)/shard_map/major_forward/ppermute | solution.py:248
  65.3 0.5 collective-permute-start.16
  65.7 0.0 collective-permute-done.19.refs_6_
  65.7 1.7 %collective-permute-start.20 = (f32[512,256]{1,0:T(8,128)S(1)}, f32[512,256]{1,0:T(8,128)S(1)}, u32[]{:S(2)}, u32[]{:S(2)}) collective-permute-start(f32[512,256]{1,0:T(8,128)S(1)} %get-tuple-element.59), channel_id=1, source_target_pairs={{0,8},{8,0},{16,24},{24,16},{32,40},{40,32},{48,56},{56,48},{64,72... | collective-permute-start | bytes 1572872 | tf_op jit(solution)/shard_map/core_gather/ppermute | solution.py:248
  67.5 0.1 collective-permute-start.22
  67.6 0.4 collective-permute-start.23
  68.0 1.0 %collective-permute-done.20.refs_7_ = f32[512,256]{1,0:T(8,128)S(1)} collective-permute-done((f32[512,256]{1,0:T(8,128)S(1)}, f32[512,256]{1,0:T(8,128)S(1)}, u32[]{:S(2)}, u32[]{:S(2)}) %collective-permute-start.20) | collective-permute-done | bytes 524320 | tf_op jit(solution)/shard_map/core_gather/ppermute | solution.py:248
  69.0 1.2 %collective-permute-start.24 = (f32[8,256]{1,0:T(8,128)S(1)}, f32[8,256]{1,0:T(8,128)S(1)}, u32[]{:S(2)}, u32[]{:S(2)}) collective-permute-start(f32[8,256]{1,0:T(8,128)S(1)} %add.64), channel_id=1, source_target_pairs={{0,32},{8,136},{16,48},{24,152},{32,0},{40,168},{48,16},{56,184},{... | collective-permute-start | bytes 24584 | tf_op jit(solution)/shard_map/square_sum/ppermute | solution.py:248
  70.2 0.0 collective-permute-done.22.refs_9_
  70.2 0.3 collective-permute-done.23.refs_10_
  70.5 2.2 %collective-permute-done.17 = f32[520,256]{1,0:T(8,128)S(1)} collective-permute-done((f32[520,256]{1,0:T(8,128)S(1)}, f32[520,256]{1,0:T(8,128)S(1)}, u32[]{:S(2)}, u32[]{:S(2)}) %collective-permute-start.17) | collective-permute-done | bytes 532512 | tf_op jit(solution)/shard_map/major_forward/ppermute | solution.py:248
  72.7 2.3 %collective-permute-done.16 = f32[520,256]{1,0:T(8,128)S(1)} collective-permute-done((f32[520,256]{1,0:T(8,128)S(1)}, f32[520,256]{1,0:T(8,128)S(1)}, u32[]{:S(2)}, u32[]{:S(2)}) %collective-permute-start.16) | collective-permute-done | bytes 532512 | tf_op jit(solution)/shard_map/major_forward/ppermute | solution.py:248
  75.0 0.0 collective-permute-done.24
  75.1 3.1 %collective-permute-start.26 = (f32[520,256]{1,0:T(8,128)S(1)}, f32[520,256]{1,0:T(8,128)S(1)}, u32[]{:S(2)}, u32[]{:S(2)}) collective-permute-start(f32[520,256]{1,0:T(8,128)S(1)} %pad_maximum_fusion.2.refs_4_), channel_id=1, source_target_pairs={{0,8},{8,0},{16,24},{24,16},{32,40},{40,32},{48,56},{56,48},{64,72... | collective-permute-start | bytes 1597448 | tf_op jit(solution)/shard_map/update/ppermute | solution.py:248
  78.3 0.1 collective-permute-start.25
  78.4 2.2 %collective-permute-done.25.refs_11_ = f32[512,256]{1,0:T(8,128)S(1)} collective-permute-done((f32[512,256]{1,0:T(8,128)S(1)}, f32[512,256]{1,0:T(8,128)S(1)}, u32[]{:S(2)}, u32[]{:S(2)}) %collective-permute-start.25) | collective-permute-done | bytes 524320 | tf_op jit(solution)/shard_map/update/ppermute | solution.py:248
  80.5 0.0 collective-permute-done.26.refs_12_
  80.5 3.1 %update.1 = (f32[128,256]{1,0:T(8,128)}, f32[128,8192]{1,0:T(8,128)}) custom-call(f32[1024,256]{1,0:T(8,128)S(1)} %slice_dynamic-update-slice_fusion.refs_0_, f32[1024,256]{1,0:T(8,128)S(1)} %collective-permute-done.11.refs_1_, f32[1024,256]{1,0:T(8,128)S(1)} %collective-permute-done.12.refs_2_, f32[512,256]{1,0:T(8,128)S(1)} %slice.86.refs_3_, ...), custom_call_target="tpu_custom_call" | custom-call | flops 2097152 | bytes 4194304 | tf_op jit(solution)/shard_map/update/update/pallas_call | solution.py:219
  (29 shorter events, 0.5 us)
Async XLA Ops:
  3.9 4.9 %collective-permute-start = (f32[4,128,256]{2,1,0:T(8,128)S(1)}, f32[4,128,256]{2,1,0:T(8,128)S(1)}, u32[]{:S(2)}, u32[]{:S(2)}) collective-permute-start(f32[4,128,256]{2,1,0:T(8,128)S(1)} %get-tuple-element.30), channel_id=1, source_target_pairs={{0,8},{8,0},{16,24},{24,16},{32,40},{40,32},{48,56},{56,48},{64,72... | collective-permute-start | bytes 1572872 | tf_op jit(solution)/shard_map/core_sum/ppermute | solution.py:248
  8.8 2.3 %collective-permute-start.3 = (f32[4,128,256]{2,1,0:T(8,128)S(1)}, f32[4,128,256]{2,1,0:T(8,128)S(1)}, u32[]{:S(2)}, u32[]{:S(2)}) collective-permute-start(f32[4,128,256]{2,1,0:T(8,128)S(1)} %get-tuple-element.38), channel_id=1, source_target_pairs={{0,8},{8,0},{16,24},{24,16},{32,40},{40,32},{48,56},{56,48},{64,72... | collective-permute-start | bytes 1572872 | tf_op jit(solution)/shard_map/core_sum/ppermute | solution.py:248
  9.2 3.4 %collective-permute-start.5 = (f32[4,128,256]{2,1,0:T(8,128)S(1)}, f32[4,128,256]{2,1,0:T(8,128)S(1)}, u32[]{:S(2)}, u32[]{:S(2)}) collective-permute-start(f32[4,128,256]{2,1,0:T(8,128)S(1)} %get-tuple-element.40), channel_id=1, source_target_pairs={{0,8},{8,0},{16,24},{24,16},{32,40},{40,32},{48,56},{56,48},{64,72... | collective-permute-start | bytes 1572872 | tf_op jit(solution)/shard_map/core_sum/ppermute | solution.py:248
  9.4 10.0 %collective-permute-start.2 = (f32[4,128,256]{2,1,0:T(8,128)S(1)}, f32[4,128,256]{2,1,0:T(8,128)S(1)}, u32[]{:S(2)}, u32[]{:S(2)}) collective-permute-start(f32[4,128,256]{2,1,0:T(8,128)S(1)} %add.52), channel_id=1, source_target_pairs={{0,32},{8,136},{16,48},{24,152},{32,0},{40,168},{48,16},{56,184},{... | collective-permute-start | bytes 1572872 | tf_op jit(solution)/shard_map/major_sum/ppermute | solution.py:248
  10.6 8.7 %collective-permute-start.1 = (f32[4,128,256]{2,1,0:T(8,128)S(1)}, f32[4,128,256]{2,1,0:T(8,128)S(1)}, u32[]{:S(2)}, u32[]{:S(2)}) collective-permute-start(f32[4,128,256]{2,1,0:T(8,128)S(1)} %get-tuple-element.34), channel_id=1, source_target_pairs={{0,8},{8,0},{16,24},{24,16},{32,40},{40,32},{48,56},{56,48},{64,72... | collective-permute-start | bytes 1572872 | tf_op jit(solution)/shard_map/core_sum/ppermute | solution.py:248
  11.2 13.7 %collective-permute-start.4 = (f32[4,128,256]{2,1,0:T(8,128)S(1)}, f32[4,128,256]{2,1,0:T(8,128)S(1)}, u32[]{:S(2)}, u32[]{:S(2)}) collective-permute-start(f32[4,128,256]{2,1,0:T(8,128)S(1)} %add.54), channel_id=1, source_target_pairs={{0,16},{8,72},{16,32},{24,88},{32,48},{40,104},{48,0},{56,120},{64... | collective-permute-start | bytes 1572872 | tf_op jit(solution)/shard_map/major_sum/ppermute | solution.py:248
  12.6 12.3 %collective-permute-start.6 = (f32[4,128,256]{2,1,0:T(8,128)S(1)}, f32[4,128,256]{2,1,0:T(8,128)S(1)}, u32[]{:S(2)}, u32[]{:S(2)}) collective-permute-start(f32[4,128,256]{2,1,0:T(8,128)S(1)} %add.56), channel_id=1, source_target_pairs={{0,48},{8,200},{16,0},{24,216},{32,16},{40,232},{48,32},{56,248},{... | collective-permute-start | bytes 1572872 | tf_op jit(solution)/shard_map/major_sum/ppermute | solution.py:248
  25.2 7.5 %collective-permute-start.9 = (f32[320,256]{1,0:T(8,128)S(1)}, f32[320,256]{1,0:T(8,128)S(1)}, u32[]{:S(2)}, u32[]{:S(2)}) collective-permute-start(f32[320,256]{1,0:T(8,128)S(1)} %pad_maximum_fusion.6), channel_id=1, source_target_pairs={{0,192},{8,56},{16,208},{24,40},{32,224},{40,24},{48,240},{56,8},{... | collective-permute-start | bytes 983048 | tf_op jit(solution)/shard_map/minor_sum/ppermute | solution.py:248
  26.4 6.5 %collective-permute-start.7 = (f32[320,256]{1,0:T(8,128)S(1)}, f32[320,256]{1,0:T(8,128)S(1)}, u32[]{:S(2)}, u32[]{:S(2)}) collective-permute-start(f32[320,256]{1,0:T(8,128)S(1)} %pad_maximum_fusion.5), channel_id=1, source_target_pairs={{0,64},{8,24},{16,80},{24,8},{32,96},{40,56},{48,112},{56,40},{64,... | collective-permute-start | bytes 983048 | tf_op jit(solution)/shard_map/minor_sum/ppermute | solution.py:248
  32.8 7.0 %collective-permute-start.10 = (f32[384,256]{1,0:T(8,128)S(1)}, f32[384,256]{1,0:T(8,128)S(1)}, u32[]{:S(2)}, u32[]{:S(2)}) collective-permute-start(f32[384,256]{1,0:T(8,128)S(1)} %pad_maximum_fusion.4), channel_id=1, source_target_pairs={{0,64},{8,24},{16,80},{24,8},{32,96},{40,56},{48,112},{56,40},{64,... | collective-permute-start | bytes 1179656 | tf_op jit(solution)/shard_map/minor_sum/ppermute | solution.py:248
  33.0 8.2 %collective-permute-start.8 = (f32[384,256]{1,0:T(8,128)S(1)}, f32[384,256]{1,0:T(8,128)S(1)}, u32[]{:S(2)}, u32[]{:S(2)}) collective-permute-start(f32[384,256]{1,0:T(8,128)S(1)} %pad_maximum_fusion.3), channel_id=1, source_target_pairs={{0,192},{8,56},{16,208},{24,40},{32,224},{40,24},{48,240},{56,8},{... | collective-permute-start | bytes 1179656 | tf_op jit(solution)/shard_map/minor_sum/ppermute | solution.py:248
  41.4 15.2 %collective-permute-start.12 = (f32[1024,256]{1,0:T(8,128)S(1)}, f32[1024,256]{1,0:T(8,128)S(1)}, u32[]{:S(2)}, u32[]{:S(2)}) collective-permute-start(f32[1024,256]{1,0:T(8,128)S(1)} %slice_dynamic-update-slice_fusion.refs_0_), channel_id=1, source_target_pairs={{0,48},{8,200},{16,0},{24,216},{32,16},{40,232},{48,32},{56,248},{... | collective-permute-start | bytes 3145736 | tf_op jit(solution)/shard_map/major_gather/ppermute | solution.py:248
  43.7 15.2 %collective-permute-start.11 = (f32[1024,256]{1,0:T(8,128)S(1)}, f32[1024,256]{1,0:T(8,128)S(1)}, u32[]{:S(2)}, u32[]{:S(2)}) collective-permute-start(f32[1024,256]{1,0:T(8,128)S(1)} %slice_dynamic-update-slice_fusion.refs_0_), channel_id=1, source_target_pairs={{0,16},{8,72},{16,32},{24,88},{32,48},{40,104},{48,0},{56,120},{64... | collective-permute-start | bytes 3145736 | tf_op jit(solution)/shard_map/major_gather/ppermute | solution.py:248
  43.7 2.8 %collective-permute-start.13 = (f32[8,256]{1,0:T(8,128)S(1)}, f32[8,256]{1,0:T(8,128)S(1)}, u32[]{:S(2)}, u32[]{:S(2)}) collective-permute-start(f32[8,256]{1,0:T(8,128)S(1)} %squares.1), channel_id=1, source_target_pairs={{0,1},{1,0},{2,3},{3,2},{4,5},{5,4},{6,7},{7,6},{8,9},{9,8},{10,11... | collective-permute-start | bytes 24584 | tf_op jit(solution)/shard_map/square_sum/ppermute | solution.py:276
  46.5 4.0 %collective-permute-start.14 = (f32[8,256]{1,0:T(8,128)S(1)}, f32[8,256]{1,0:T(8,128)S(1)}, u32[]{:S(2)}, u32[]{:S(2)}) collective-permute-start(f32[8,256]{1,0:T(8,128)S(1)} %add.62), channel_id=1, source_target_pairs={{0,2},{1,3},{2,0},{3,1},{4,6},{5,7},{6,4},{7,5},{8,10},{9,11},{10,... | collective-permute-start | bytes 24584 | tf_op jit(solution)/shard_map/square_sum/ppermute | solution.py:278
  50.5 6.1 %collective-permute-start.15 = (f32[8,256]{1,0:T(8,128)S(1)}, f32[8,256]{1,0:T(8,128)S(1)}, u32[]{:S(2)}, u32[]{:S(2)}) collective-permute-start(f32[8,256]{1,0:T(8,128)S(1)} %add.63), channel_id=1, source_target_pairs={{0,7},{1,6},{2,5},{3,4},{4,3},{5,2},{6,1},{7,0},{8,15},{9,14},{10,... | collective-permute-start | bytes 24584 | tf_op jit(solution)/shard_map/square_sum/ppermute | solution.py:278
  58.9 6.8 %collective-permute-start.19 = (f32[512,256]{1,0:T(8,128)S(1)}, f32[512,256]{1,0:T(8,128)S(1)}, u32[]{:S(2)}, u32[]{:S(2)}) collective-permute-start(f32[512,256]{1,0:T(8,128)S(1)} %get-tuple-element.60), channel_id=1, source_target_pairs={{0,8},{8,0},{16,24},{24,16},{32,40},{40,32},{48,56},{56,48},{64,72... | collective-permute-start | bytes 1572872 | tf_op jit(solution)/shard_map/core_gather/ppermute | solution.py:248
  63.3 4.1 %collective-permute-start.18 = (f32[512,256]{1,0:T(8,128)S(1)}, f32[512,256]{1,0:T(8,128)S(1)}, u32[]{:S(2)}, u32[]{:S(2)}) collective-permute-start(f32[512,256]{1,0:T(8,128)S(1)} %get-tuple-element.61), channel_id=1, source_target_pairs={{0,8},{8,0},{16,24},{24,16},{32,40},{40,32},{48,56},{56,48},{64,72... | collective-permute-start | bytes 1572872 | tf_op jit(solution)/shard_map/core_gather/ppermute | solution.py:248
  63.5 17.0 %copy-start = (f32[128,256]{1,0:T(8,128)S(1)}, f32[128,256]{1,0:T(8,128)}, u32[]{:S(2)}) copy-start(f32[128,256]{1,0:T(8,128)} %refs_13_.1) | copy-start | bytes 393220
  63.5 4.1 %collective-permute-start.21 = (f32[512,256]{1,0:T(8,128)S(1)}, f32[512,256]{1,0:T(8,128)S(1)}, u32[]{:S(2)}, u32[]{:S(2)}) collective-permute-start(f32[512,256]{1,0:T(8,128)S(1)} %get-tuple-element.58), channel_id=1, source_target_pairs={{0,8},{8,0},{16,24},{24,16},{32,40},{40,32},{48,56},{56,48},{64,72... | collective-permute-start | bytes 1572872 | tf_op jit(solution)/shard_map/core_gather/ppermute | solution.py:248
  64.2 8.5 %collective-permute-start.17 = (f32[520,256]{1,0:T(8,128)S(1)}, f32[520,256]{1,0:T(8,128)S(1)}, u32[]{:S(2)}, u32[]{:S(2)}) collective-permute-start(f32[520,256]{1,0:T(8,128)S(1)} %get-tuple-element.68), channel_id=1, source_target_pairs={{0,48},{8,200},{16,0},{24,216},{32,16},{40,232},{48,32},{56,248},{... | collective-permute-start | bytes 1597448 | tf_op jit(solution)/shard_map/major_forward/ppermute | solution.py:248
  65.3 9.7 %collective-permute-start.16 = (f32[520,256]{1,0:T(8,128)S(1)}, f32[520,256]{1,0:T(8,128)S(1)}, u32[]{:S(2)}, u32[]{:S(2)}) collective-permute-start(f32[520,256]{1,0:T(8,128)S(1)} %get-tuple-element.69), channel_id=1, source_target_pairs={{0,16},{8,72},{16,32},{24,88},{32,48},{40,104},{48,0},{56,120},{64... | collective-permute-start | bytes 1597448 | tf_op jit(solution)/shard_map/major_forward/ppermute | solution.py:248
  65.7 3.3 %collective-permute-start.20 = (f32[512,256]{1,0:T(8,128)S(1)}, f32[512,256]{1,0:T(8,128)S(1)}, u32[]{:S(2)}, u32[]{:S(2)}) collective-permute-start(f32[512,256]{1,0:T(8,128)S(1)} %get-tuple-element.59), channel_id=1, source_target_pairs={{0,8},{8,0},{16,24},{24,16},{32,40},{40,32},{48,56},{56,48},{64,72... | collective-permute-start | bytes 1572872 | tf_op jit(solution)/shard_map/core_gather/ppermute | solution.py:248
  67.5 2.8 %collective-permute-start.22 = (f32[512,256]{1,0:T(8,128)S(1)}, f32[512,256]{1,0:T(8,128)S(1)}, u32[]{:S(2)}, u32[]{:S(2)}) collective-permute-start(f32[512,256]{1,0:T(8,128)S(1)} %get-tuple-element.56), channel_id=1, source_target_pairs={{0,8},{8,0},{16,24},{24,16},{32,40},{40,32},{48,56},{56,48},{64,72... | collective-permute-start | bytes 1572872 | tf_op jit(solution)/shard_map/core_gather/ppermute | solution.py:248
  67.6 2.9 %collective-permute-start.23 = (f32[512,256]{1,0:T(8,128)S(1)}, f32[512,256]{1,0:T(8,128)S(1)}, u32[]{:S(2)}, u32[]{:S(2)}) collective-permute-start(f32[512,256]{1,0:T(8,128)S(1)} %get-tuple-element.57), channel_id=1, source_target_pairs={{0,8},{8,0},{16,24},{24,16},{32,40},{40,32},{48,56},{56,48},{64,72... | collective-permute-start | bytes 1572872 | tf_op jit(solution)/shard_map/core_gather/ppermute | solution.py:248
  69.0 6.0 %collective-permute-start.24 = (f32[8,256]{1,0:T(8,128)S(1)}, f32[8,256]{1,0:T(8,128)S(1)}, u32[]{:S(2)}, u32[]{:S(2)}) collective-permute-start(f32[8,256]{1,0:T(8,128)S(1)} %add.64), channel_id=1, source_target_pairs={{0,32},{8,136},{16,48},{24,152},{32,0},{40,168},{48,16},{56,184},{... | collective-permute-start | bytes 24584 | tf_op jit(solution)/shard_map/square_sum/ppermute | solution.py:248
  75.1 5.4 %collective-permute-start.26 = (f32[520,256]{1,0:T(8,128)S(1)}, f32[520,256]{1,0:T(8,128)S(1)}, u32[]{:S(2)}, u32[]{:S(2)}) collective-permute-start(f32[520,256]{1,0:T(8,128)S(1)} %pad_maximum_fusion.2.refs_4_), channel_id=1, source_target_pairs={{0,8},{8,0},{16,24},{24,16},{32,40},{40,32},{48,56},{56,48},{64,72... | collective-permute-start | bytes 1597448 | tf_op jit(solution)/shard_map/update/ppermute | solution.py:248
  78.3 2.3 %collective-permute-start.25 = (f32[512,256]{1,0:T(8,128)S(1)}, f32[512,256]{1,0:T(8,128)S(1)}, u32[]{:S(2)}, u32[]{:S(2)}) collective-permute-start(f32[512,256]{1,0:T(8,128)S(1)} %slice.86.refs_3_), channel_id=1, source_target_pairs={{0,8},{8,0},{16,24},{24,16},{32,40},{40,32},{48,56},{56,48},{64,72... | collective-permute-start | bytes 1572872 | tf_op jit(solution)/shard_map/update/ppermute | solution.py:248

commit v6 on v4

--- a/solution.py
+++ b/solution.py
@@ -173,7 +173,7 @@
 
 
 def update_kernel(threshold, *refs):
-    mine, handed, (momentum, new_momentum, out, buf, sem) = refs[:5], refs[5:13], refs[13:]
+    mine, handed, (momentum, new_momentum, out, buf, sem) = refs[:5], refs[5:8], refs[8:]
     rows = momentum.shape[0]
     size, half = SIDE * rows, rows // 2
     me = lax.axis_index("replica")
@@ -184,7 +184,8 @@
     rate = OUTER_RATE * (1.0 + OUTER_MOMENTUM) * factor
     own = [(k, mine[n], 0, mine[n], size) for n, k in enumerate((0, 1, 3))]
     own.append((2, mine[3], 0, mine[4], 0))
-    other = [(k, handed[2 * n], 0, handed[2 * n + 1], 0) for n, k in enumerate((0, 1, 3, 2))]
+    other = [(k, handed[0], 2 * n * size, handed[0], (2 * n + 1) * size) for n, k in enumerate((0, 1, 3))]
+    other.append((2, handed[1], 0, handed[2], 0))
     work = []
     for side, sources in ((core, own), (1 - core, other)):
         major, minor = axes_of(me, side)
@@ -284,18 +285,16 @@
         far_high = move(jnp.concatenate([above[middle:], squares]), down)
 
     with jax.named_scope("core_gather"):
-        whole = tie(mine, squares)[0], below, above
-        near = [move(part, CORE_SWAP) for x in whole for part in (x[:middle], x[middle:])]
+        near = move(jnp.concatenate([mine, below, above]), CORE_SWAP)
 
     with jax.named_scope("square_sum"):
         across = move(squares, major_shift(2))
-        far_low, far_high, near = tie(far_low, far_high, near)
         squares = squares + across + far_low[middle:] + far_high[middle:]
 
     with jax.named_scope("update"):
         (far_low,) = tie(far_low[:middle])
         far_high = jnp.concatenate([far_high[:middle], squares])
-        handed = [*near, move(far_low, CORE_SWAP), move(far_high, CORE_SWAP)]
+        handed = [near, move(far_low, CORE_SWAP), move(far_high, CORE_SWAP)]
         new_momentum, new_weights = update(
             col_count, threshold, [mine, below, above, far_low, far_high], handed, momentum
         )

time: 83.3 us -> 82.6 us (level)
  starting transfers between devices: 35.9 us -> 33 us
  waiting for transfers between devices: 38.6 us -> 40.8 us
    ppermute x24 -> x19, starting transfers between devices: 26.4 us -> 23.5 us  [move(): return lax.ppermute(value, 'replica', perm)]
    ppermute x24 -> x19, waiting for transfers between devices: 35.2 us -> 37.4 us  [move(): return lax.ppermute(value, 'replica', perm)]
  transfers between devices with their start and end apart: 27 -> 22, of which waited for: 15 -> 14; matrix products, arithmetic and copies ran while one was open for 1% -> 1% of each run, Pallas kernels for 0% -> 0%
where the time goes in v6:
time: 82.6 us; the launch traced here: 82.5 us
  waiting for transfers between devices  40.8 us (49%)
  starting transfers between devices  33 us (40%)
  Pallas kernels  6.39 us (8%)
  between operations  1.03 us (1%)
  other arithmetic  0.88 us (1%)
    ppermute x19, waiting for transfers between devices, move(): return lax.ppermute(value, 'replica', perm)  37.4 us
    ppermute x19, starting transfers between devices, move(): return lax.ppermute(value, 'replica', perm)  23.5 us
    ppermute x2, starting transfers between devices, per_device(): squares = squares + lax.ppermute(squares, 'fsdp', perm)  7.76 us
    pallas_call x1, Pallas kernels, encode(): pl.pallas_call(encode_kernel, out_shape=[*blocks, *blocks, jax.ShapeDtype...  3.29 us
    pallas_call x1, Pallas kernels, update(): pl.pallas_call(functools.partial(update_kernel, threshold), out_shape=[ja...  3.03 us
    ppermute x2, waiting for transfers between devices, per_device(): squares = squares + lax.ppermute(squares, 'fsdp', perm)  2.37 us
    ppermute x1, starting transfers between devices, per_device(): squares = squares + lax.ppermute(squares, 'fsdp', Z_ROUNDS[0])  1.72 us
  transfers between devices with their start and end apart: 22, of which 14 were waited for; matrix products, arithmetic and copies ran while one was open for 1% of the time, Pallas kernels for 0%

profile of v6, /device:TPU:1, one launch (start us, length us, event | category | flops | bytes accessed | tf_op | source)
XLA Modules:
  0.0 82.5 jit_solution(12654551803053187087)
XLA Ops:
  0.6 3.3 %encode.1 = (f32[4,128,256]{2,1,0:T(8,128)S(1)}, f32[4,128,256]{2,1,0:T(8,128)S(1)}, f32[4,128,256]{2,1,0:T(8,128)S(1)}, f32[4,128,256]{2,1,0:T(8,128)S(1)}, f32...) custom-call(f32[128,8192]{1,0:T(8,128)} %weights.1, ...), custom_call_target="tpu_custom_call" | custom-call | flops 4194304 | bytes 6291456 | tf_op jit(solution)/shard_map/core_sum/encode/pallas_call | solution.py:133
  3.9 3.3 %collective-permute-start.1 = (f32[4,128,256]{2,1,0:T(8,128)S(1)}, f32[4,128,256]{2,1,0:T(8,128)S(1)}, u32[]{:S(2)}, u32[]{:S(2)}) collective-permute-start(f32[4,128,256]{2,1,0:T(8,128)S(1)} %get-tuple-element.19), channel_id=1, source_target_pairs={{0,8},{8,0},{16,24},{24,16},{32,40},{40,32},{48,56},{56,48},{64,72... | collective-permute-start | bytes 1572872 | tf_op jit(solution)/shard_map/core_sum/ppermute | solution.py:249
  7.2 0.1 collective-permute-start.3
  7.3 0.4 collective-permute-start.5
  7.8 0.1 collective-permute-start
  7.9 0.9 %collective-permute-done.1 = f32[4,128,256]{2,1,0:T(8,128)S(1)} collective-permute-done((f32[4,128,256]{2,1,0:T(8,128)S(1)}, f32[4,128,256]{2,1,0:T(8,128)S(1)}, u32[]{:S(2)}, u32[]{:S(2)}) %collective-permute-start.1) | collective-permute-done | bytes 524320 | tf_op jit(solution)/shard_map/core_sum/ppermute | solution.py:249
  8.8 0.1 add.52
  8.9 1.3 %collective-permute-start.2 = (f32[4,128,256]{2,1,0:T(8,128)S(1)}, f32[4,128,256]{2,1,0:T(8,128)S(1)}, u32[]{:S(2)}, u32[]{:S(2)}) collective-permute-start(f32[4,128,256]{2,1,0:T(8,128)S(1)} %add.52), channel_id=1, source_target_pairs={{0,32},{8,136},{16,48},{24,152},{32,0},{40,168},{48,16},{56,184},{... | collective-permute-start | bytes 1572872 | tf_op jit(solution)/shard_map/major_sum/ppermute | solution.py:249
  10.1 0.0 collective-permute-done.3
  10.1 0.1 add.54
  10.2 0.5 collective-permute-start.4
  10.7 0.0 collective-permute-done.5
  10.7 0.1 add.56
  10.7 2.4 %collective-permute-start.6 = (f32[4,128,256]{2,1,0:T(8,128)S(1)}, f32[4,128,256]{2,1,0:T(8,128)S(1)}, u32[]{:S(2)}, u32[]{:S(2)}) collective-permute-start(f32[4,128,256]{2,1,0:T(8,128)S(1)} %add.56), channel_id=1, source_target_pairs={{0,48},{8,200},{16,0},{24,216},{32,16},{40,232},{48,32},{56,248},{... | collective-permute-start | bytes 1572872 | tf_op jit(solution)/shard_map/major_sum/ppermute | solution.py:249
  13.1 0.0 collective-permute-done
  13.1 5.7 %collective-permute-done.2 = f32[4,128,256]{2,1,0:T(8,128)S(1)} collective-permute-done((f32[4,128,256]{2,1,0:T(8,128)S(1)}, f32[4,128,256]{2,1,0:T(8,128)S(1)}, u32[]{:S(2)}, u32[]{:S(2)}) %collective-permute-start.2) | collective-permute-done | bytes 524320 | tf_op jit(solution)/shard_map/major_sum/ppermute | solution.py:249
  18.8 5.6 %collective-permute-done.4 = f32[4,128,256]{2,1,0:T(8,128)S(1)} collective-permute-done((f32[4,128,256]{2,1,0:T(8,128)S(1)}, f32[4,128,256]{2,1,0:T(8,128)S(1)}, u32[]{:S(2)}, u32[]{:S(2)}) %collective-permute-start.4) | collective-permute-done | bytes 524320 | tf_op jit(solution)/shard_map/major_sum/ppermute | solution.py:249
  24.4 0.0 collective-permute-done.6
  24.4 0.2 add_add_fusion
  24.6 1.2 %collective-permute-start.9 = (f32[320,256]{1,0:T(8,128)S(1)}, f32[320,256]{1,0:T(8,128)S(1)}, u32[]{:S(2)}, u32[]{:S(2)}) collective-permute-start(f32[320,256]{1,0:T(8,128)S(1)} %pad_maximum_fusion.6), channel_id=1, source_target_pairs={{0,192},{8,56},{16,208},{24,40},{32,224},{40,24},{48,240},{56,8},{... | collective-permute-start | bytes 983048 | tf_op jit(solution)/shard_map/minor_sum/ppermute | solution.py:249
  25.9 0.1 collective-permute-start.7
  26.0 6.2 %collective-permute-done.9 = f32[320,256]{1,0:T(8,128)S(1)} collective-permute-done((f32[320,256]{1,0:T(8,128)S(1)}, f32[320,256]{1,0:T(8,128)S(1)}, u32[]{:S(2)}, u32[]{:S(2)}) %collective-permute-start.9) | collective-permute-done | bytes 327712 | tf_op jit(solution)/shard_map/minor_sum/ppermute | solution.py:249
  32.2 0.1 collective-permute-start.10
  32.3 0.0 collective-permute-done.7
  32.5 1.5 %collective-permute-start.8 = (f32[384,256]{1,0:T(8,128)S(1)}, f32[384,256]{1,0:T(8,128)S(1)}, u32[]{:S(2)}, u32[]{:S(2)}) collective-permute-start(f32[384,256]{1,0:T(8,128)S(1)} %pad_maximum_fusion.3), channel_id=1, source_target_pairs={{0,192},{8,56},{16,208},{24,40},{32,224},{40,24},{48,240},{56,8},{... | collective-permute-start | bytes 1179656 | tf_op jit(solution)/shard_map/minor_sum/ppermute | solution.py:249
  33.9 5.3 %collective-permute-done.10 = f32[384,256]{1,0:T(8,128)S(1)} collective-permute-done((f32[384,256]{1,0:T(8,128)S(1)}, f32[384,256]{1,0:T(8,128)S(1)}, u32[]{:S(2)}, u32[]{:S(2)}) %collective-permute-start.10) | collective-permute-done | bytes 393248 | tf_op jit(solution)/shard_map/minor_sum/ppermute | solution.py:249
  39.3 1.4 %collective-permute-done.8 = f32[384,256]{1,0:T(8,128)S(1)} collective-permute-done((f32[384,256]{1,0:T(8,128)S(1)}, f32[384,256]{1,0:T(8,128)S(1)}, u32[]{:S(2)}, u32[]{:S(2)}) %collective-permute-start.8) | collective-permute-done | bytes 393248 | tf_op jit(solution)/shard_map/minor_sum/ppermute | solution.py:249
  40.7 0.1 constant_dynamic-update-slice_fusion.11
  41.0 2.3 %collective-permute-start.12 = (f32[1024,256]{1,0:T(8,128)S(1)}, f32[1024,256]{1,0:T(8,128)S(1)}, u32[]{:S(2)}, u32[]{:S(2)}) collective-permute-start(f32[1024,256]{1,0:T(8,128)S(1)} %get-tuple-element.36.refs_0_), channel_id=1, source_target_pairs={{0,48},{8,200},{16,0},{24,216},{32,16},{40,232},{48,32},{56,248},{... | collective-permute-start | bytes 3145736 | tf_op jit(solution)/shard_map/major_gather/ppermute | solution.py:249
  43.2 0.0 collective-permute-start.11
  43.2 0.1 squares.1
  43.3 1.7 %collective-permute-start.13 = (f32[8,256]{1,0:T(8,128)S(1)}, f32[8,256]{1,0:T(8,128)S(1)}, u32[]{:S(2)}, u32[]{:S(2)}) collective-permute-start(f32[8,256]{1,0:T(8,128)S(1)} %squares.1), channel_id=1, source_target_pairs={{0,1},{1,0},{2,3},{3,2},{4,5},{5,4},{6,7},{7,6},{8,9},{9,8},{10,11... | collective-permute-start | bytes 24584 | tf_op jit(solution)/shard_map/square_sum/ppermute | solution.py:275
  45.0 1.0 %collective-permute-done.13 = f32[8,256]{1,0:T(8,128)S(1)} collective-permute-done((f32[8,256]{1,0:T(8,128)S(1)}, f32[8,256]{1,0:T(8,128)S(1)}, u32[]{:S(2)}, u32[]{:S(2)}) %collective-permute-start.13) | collective-permute-done | bytes 8224 | tf_op jit(solution)/shard_map/square_sum/ppermute | solution.py:275
  46.1 3.0 %collective-permute-start.14 = (f32[8,256]{1,0:T(8,128)S(1)}, f32[8,256]{1,0:T(8,128)S(1)}, u32[]{:S(2)}, u32[]{:S(2)}) collective-permute-start(f32[8,256]{1,0:T(8,128)S(1)} %add.62), channel_id=1, source_target_pairs={{0,2},{1,3},{2,0},{3,1},{4,6},{5,7},{6,4},{7,5},{8,10},{9,11},{10,... | collective-permute-start | bytes 24584 | tf_op jit(solution)/shard_map/square_sum/ppermute | solution.py:277
  49.1 1.0 %collective-permute-done.14 = f32[8,256]{1,0:T(8,128)S(1)} collective-permute-done((f32[8,256]{1,0:T(8,128)S(1)}, f32[8,256]{1,0:T(8,128)S(1)}, u32[]{:S(2)}, u32[]{:S(2)}) %collective-permute-start.14) | collective-permute-done | bytes 8224 | tf_op jit(solution)/shard_map/square_sum/ppermute | solution.py:277
  50.1 4.8 %collective-permute-start.15 = (f32[8,256]{1,0:T(8,128)S(1)}, f32[8,256]{1,0:T(8,128)S(1)}, u32[]{:S(2)}, u32[]{:S(2)}) collective-permute-start(f32[8,256]{1,0:T(8,128)S(1)} %add.63), channel_id=1, source_target_pairs={{0,7},{1,6},{2,5},{3,4},{4,3},{5,2},{6,1},{7,0},{8,15},{9,14},{10,... | collective-permute-start | bytes 24584 | tf_op jit(solution)/shard_map/square_sum/ppermute | solution.py:277
  54.9 1.3 %collective-permute-done.15 = f32[8,256]{1,0:T(8,128)S(1)} collective-permute-done((f32[8,256]{1,0:T(8,128)S(1)}, f32[8,256]{1,0:T(8,128)S(1)}, u32[]{:S(2)}, u32[]{:S(2)}) %collective-permute-start.15) | collective-permute-done | bytes 8224 | tf_op jit(solution)/shard_map/square_sum/ppermute | solution.py:277
  56.2 0.0 collective-permute-done.12.refs_2_
  56.2 2.2 %collective-permute-done.11.refs_1_ = f32[1024,256]{1,0:T(8,128)S(1)} collective-permute-done((f32[1024,256]{1,0:T(8,128)S(1)}, f32[1024,256]{1,0:T(8,128)S(1)}, u32[]{:S(2)}, u32[]{:S(2)}) %collective-permute-start.11) | collective-permute-done | bytes 1048608 | tf_op jit(solution)/shard_map/major_gather/ppermute | solution.py:249
  58.4 0.1 constant_dynamic-update-slice_fusion.6
  58.5 0.1 constant_dynamic-update-slice_fusion.5
  58.5 4.4 %collective-permute-start.19 = (f32[3072,256]{1,0:T(8,128)S(1)}, f32[3072,256]{1,0:T(8,128)S(1)}, u32[]{:S(2)}, u32[]{:S(2)}) collective-permute-start(f32[3072,256]{1,0:T(8,128)S(1)} %constant_dynamic-update-slice_fusion.5), channel_id=1, source_target_pairs={{0,8},{8,0},{16,24},{24,16},{32,40},{40,32},{48,56},{56,48},{64,72... | collective-permute-start | bytes 9437192 | tf_op jit(solution)/shard_map/core_gather/ppermute | solution.py:249
  63.0 0.0 copy-start
  63.1 0.1 pad_maximum_fusion
  63.2 1.1 %collective-permute-start.17 = (f32[520,256]{1,0:T(8,128)S(1)}, f32[520,256]{1,0:T(8,128)S(1)}, u32[]{:S(2)}, u32[]{:S(2)}) collective-permute-start(f32[520,256]{1,0:T(8,128)S(1)} %get-tuple-element.49), channel_id=1, source_target_pairs={{0,48},{8,200},{16,0},{24,216},{32,16},{40,232},{48,32},{56,248},{... | collective-permute-start | bytes 1597448 | tf_op jit(solution)/shard_map/major_forward/ppermute | solution.py:249
  64.2 0.5 collective-permute-start.16
  64.7 1.2 %collective-permute-start.18 = (f32[8,256]{1,0:T(8,128)S(1)}, f32[8,256]{1,0:T(8,128)S(1)}, u32[]{:S(2)}, u32[]{:S(2)}) collective-permute-start(f32[8,256]{1,0:T(8,128)S(1)} %add.64), channel_id=1, source_target_pairs={{0,32},{8,136},{16,48},{24,152},{32,0},{40,168},{48,16},{56,184},{... | collective-permute-start | bytes 24584 | tf_op jit(solution)/shard_map/square_sum/ppermute | solution.py:249
  65.9 5.7 %collective-permute-done.17 = f32[520,256]{1,0:T(8,128)S(1)} collective-permute-done((f32[520,256]{1,0:T(8,128)S(1)}, f32[520,256]{1,0:T(8,128)S(1)}, u32[]{:S(2)}, u32[]{:S(2)}) %collective-permute-start.17) | collective-permute-done | bytes 532512 | tf_op jit(solution)/shard_map/major_forward/ppermute | solution.py:249
  71.7 1.1 %collective-permute-done.18 = f32[8,256]{1,0:T(8,128)S(1)} collective-permute-done((f32[8,256]{1,0:T(8,128)S(1)}, f32[8,256]{1,0:T(8,128)S(1)}, u32[]{:S(2)}, u32[]{:S(2)}) %collective-permute-start.18) | collective-permute-done | bytes 8224 | tf_op jit(solution)/shard_map/square_sum/ppermute | solution.py:249
  72.8 1.2 %collective-permute-done.16 = f32[520,256]{1,0:T(8,128)S(1)} collective-permute-done((f32[520,256]{1,0:T(8,128)S(1)}, f32[520,256]{1,0:T(8,128)S(1)}, u32[]{:S(2)}, u32[]{:S(2)}) %collective-permute-start.16) | collective-permute-done | bytes 532512 | tf_op jit(solution)/shard_map/major_forward/ppermute | solution.py:249
  74.0 3.0 %collective-permute-start.21 = (f32[520,256]{1,0:T(8,128)S(1)}, f32[520,256]{1,0:T(8,128)S(1)}, u32[]{:S(2)}, u32[]{:S(2)}) collective-permute-start(f32[520,256]{1,0:T(8,128)S(1)} %pad_maximum_fusion.2.refs_4_), channel_id=1, source_target_pairs={{0,8},{8,0},{16,24},{24,16},{32,40},{40,32},{48,56},{56,48},{64,72... | collective-permute-start | bytes 1597448 | tf_op jit(solution)/shard_map/update/ppermute | solution.py:249
  77.1 0.1 collective-permute-start.20
  77.2 2.2 %collective-permute-done.20.refs_6_ = f32[512,256]{1,0:T(8,128)S(1)} collective-permute-done((f32[512,256]{1,0:T(8,128)S(1)}, f32[512,256]{1,0:T(8,128)S(1)}, u32[]{:S(2)}, u32[]{:S(2)}) %collective-permute-start.20) | collective-permute-done | bytes 524320 | tf_op jit(solution)/shard_map/update/ppermute | solution.py:249
  79.3 0.0 collective-permute-done.21.refs_7_
  79.3 0.0 collective-permute-done.19.refs_5_
  79.3 0.0 copy-done
  79.4 3.0 %update.1 = (f32[128,256]{1,0:T(8,128)}, f32[128,8192]{1,0:T(8,128)}) custom-call(f32[1024,256]{1,0:T(8,128)S(1)} %get-tuple-element.36.refs_0_, f32[1024,256]{1,0:T(8,128)S(1)} %collective-permute-done.11.refs_1_, f32[1024,256]{1,0:T(8,128)S(1)} %collective-permute-done.12.refs_2_, f32[512,256]{1,0:T(8,128)S(1)} %slice.82.refs_3_, ...), custom_call_target="tpu_custom_call" | custom-call | flops 2097152 | bytes 4194304 | tf_op jit(solution)/shard_map/update/update/pallas_call | solution.py:220
  (27 shorter events, 0.6 us)
Async XLA Ops:
  3.9 4.9 %collective-permute-start.1 = (f32[4,128,256]{2,1,0:T(8,128)S(1)}, f32[4,128,256]{2,1,0:T(8,128)S(1)}, u32[]{:S(2)}, u32[]{:S(2)}) collective-permute-start(f32[4,128,256]{2,1,0:T(8,128)S(1)} %get-tuple-element.19), channel_id=1, source_target_pairs={{0,8},{8,0},{16,24},{24,16},{32,40},{40,32},{48,56},{56,48},{64,72... | collective-permute-start | bytes 1572872 | tf_op jit(solution)/shard_map/core_sum/ppermute | solution.py:249
  7.2 2.9 %collective-permute-start.3 = (f32[4,128,256]{2,1,0:T(8,128)S(1)}, f32[4,128,256]{2,1,0:T(8,128)S(1)}, u32[]{:S(2)}, u32[]{:S(2)}) collective-permute-start(f32[4,128,256]{2,1,0:T(8,128)S(1)} %get-tuple-element.21), channel_id=1, source_target_pairs={{0,8},{8,0},{16,24},{24,16},{32,40},{40,32},{48,56},{56,48},{64,72... | collective-permute-start | bytes 1572872 | tf_op jit(solution)/shard_map/core_sum/ppermute | solution.py:249
  7.3 3.3 %collective-permute-start.5 = (f32[4,128,256]{2,1,0:T(8,128)S(1)}, f32[4,128,256]{2,1,0:T(8,128)S(1)}, u32[]{:S(2)}, u32[]{:S(2)}) collective-permute-start(f32[4,128,256]{2,1,0:T(8,128)S(1)} %get-tuple-element.23), channel_id=1, source_target_pairs={{0,8},{8,0},{16,24},{24,16},{32,40},{40,32},{48,56},{56,48},{64,72... | collective-permute-start | bytes 1572872 | tf_op jit(solution)/shard_map/core_sum/ppermute | solution.py:249
  7.8 5.4 %collective-permute-start = (f32[4,128,256]{2,1,0:T(8,128)S(1)}, f32[4,128,256]{2,1,0:T(8,128)S(1)}, u32[]{:S(2)}, u32[]{:S(2)}) collective-permute-start(f32[4,128,256]{2,1,0:T(8,128)S(1)} %get-tuple-element.17), channel_id=1, source_target_pairs={{0,8},{8,0},{16,24},{24,16},{32,40},{40,32},{48,56},{56,48},{64,72... | collective-permute-start | bytes 1572872 | tf_op jit(solution)/shard_map/core_sum/ppermute | solution.py:249
  8.9 10.0 %collective-permute-start.2 = (f32[4,128,256]{2,1,0:T(8,128)S(1)}, f32[4,128,256]{2,1,0:T(8,128)S(1)}, u32[]{:S(2)}, u32[]{:S(2)}) collective-permute-start(f32[4,128,256]{2,1,0:T(8,128)S(1)} %add.52), channel_id=1, source_target_pairs={{0,32},{8,136},{16,48},{24,152},{32,0},{40,168},{48,16},{56,184},{... | collective-permute-start | bytes 1572872 | tf_op jit(solution)/shard_map/major_sum/ppermute | solution.py:249
  10.2 14.2 %collective-permute-start.4 = (f32[4,128,256]{2,1,0:T(8,128)S(1)}, f32[4,128,256]{2,1,0:T(8,128)S(1)}, u32[]{:S(2)}, u32[]{:S(2)}) collective-permute-start(f32[4,128,256]{2,1,0:T(8,128)S(1)} %add.54), channel_id=1, source_target_pairs={{0,16},{8,72},{16,32},{24,88},{32,48},{40,104},{48,0},{56,120},{64... | collective-permute-start | bytes 1572872 | tf_op jit(solution)/shard_map/major_sum/ppermute | solution.py:249
  10.7 13.6 %collective-permute-start.6 = (f32[4,128,256]{2,1,0:T(8,128)S(1)}, f32[4,128,256]{2,1,0:T(8,128)S(1)}, u32[]{:S(2)}, u32[]{:S(2)}) collective-permute-start(f32[4,128,256]{2,1,0:T(8,128)S(1)} %add.56), channel_id=1, source_target_pairs={{0,48},{8,200},{16,0},{24,216},{32,16},{40,232},{48,32},{56,248},{... | collective-permute-start | bytes 1572872 | tf_op jit(solution)/shard_map/major_sum/ppermute | solution.py:249
  24.6 7.5 %collective-permute-start.9 = (f32[320,256]{1,0:T(8,128)S(1)}, f32[320,256]{1,0:T(8,128)S(1)}, u32[]{:S(2)}, u32[]{:S(2)}) collective-permute-start(f32[320,256]{1,0:T(8,128)S(1)} %pad_maximum_fusion.6), channel_id=1, source_target_pairs={{0,192},{8,56},{16,208},{24,40},{32,224},{40,24},{48,240},{56,8},{... | collective-permute-start | bytes 983048 | tf_op jit(solution)/shard_map/minor_sum/ppermute | solution.py:249
  25.9 6.5 %collective-permute-start.7 = (f32[320,256]{1,0:T(8,128)S(1)}, f32[320,256]{1,0:T(8,128)S(1)}, u32[]{:S(2)}, u32[]{:S(2)}) collective-permute-start(f32[320,256]{1,0:T(8,128)S(1)} %pad_maximum_fusion.5), channel_id=1, source_target_pairs={{0,64},{8,24},{16,80},{24,8},{32,96},{40,56},{48,112},{56,40},{64,... | collective-permute-start | bytes 983048 | tf_op jit(solution)/shard_map/minor_sum/ppermute | solution.py:249
  32.2 7.0 %collective-permute-start.10 = (f32[384,256]{1,0:T(8,128)S(1)}, f32[384,256]{1,0:T(8,128)S(1)}, u32[]{:S(2)}, u32[]{:S(2)}) collective-permute-start(f32[384,256]{1,0:T(8,128)S(1)} %pad_maximum_fusion.4), channel_id=1, source_target_pairs={{0,64},{8,24},{16,80},{24,8},{32,96},{40,56},{48,112},{56,40},{64,... | collective-permute-start | bytes 1179656 | tf_op jit(solution)/shard_map/minor_sum/ppermute | solution.py:249
  32.5 8.2 %collective-permute-start.8 = (f32[384,256]{1,0:T(8,128)S(1)}, f32[384,256]{1,0:T(8,128)S(1)}, u32[]{:S(2)}, u32[]{:S(2)}) collective-permute-start(f32[384,256]{1,0:T(8,128)S(1)} %pad_maximum_fusion.3), channel_id=1, source_target_pairs={{0,192},{8,56},{16,208},{24,40},{32,224},{40,24},{48,240},{56,8},{... | collective-permute-start | bytes 1179656 | tf_op jit(solution)/shard_map/minor_sum/ppermute | solution.py:249
  41.0 15.2 %collective-permute-start.12 = (f32[1024,256]{1,0:T(8,128)S(1)}, f32[1024,256]{1,0:T(8,128)S(1)}, u32[]{:S(2)}, u32[]{:S(2)}) collective-permute-start(f32[1024,256]{1,0:T(8,128)S(1)} %get-tuple-element.36.refs_0_), channel_id=1, source_target_pairs={{0,48},{8,200},{16,0},{24,216},{32,16},{40,232},{48,32},{56,248},{... | collective-permute-start | bytes 3145736 | tf_op jit(solution)/shard_map/major_gather/ppermute | solution.py:249
  43.2 15.2 %collective-permute-start.11 = (f32[1024,256]{1,0:T(8,128)S(1)}, f32[1024,256]{1,0:T(8,128)S(1)}, u32[]{:S(2)}, u32[]{:S(2)}) collective-permute-start(f32[1024,256]{1,0:T(8,128)S(1)} %get-tuple-element.36.refs_0_), channel_id=1, source_target_pairs={{0,16},{8,72},{16,32},{24,88},{32,48},{40,104},{48,0},{56,120},{64... | collective-permute-start | bytes 3145736 | tf_op jit(solution)/shard_map/major_gather/ppermute | solution.py:249
  43.3 2.8 %collective-permute-start.13 = (f32[8,256]{1,0:T(8,128)S(1)}, f32[8,256]{1,0:T(8,128)S(1)}, u32[]{:S(2)}, u32[]{:S(2)}) collective-permute-start(f32[8,256]{1,0:T(8,128)S(1)} %squares.1), channel_id=1, source_target_pairs={{0,1},{1,0},{2,3},{3,2},{4,5},{5,4},{6,7},{7,6},{8,9},{9,8},{10,11... | collective-permute-start | bytes 24584 | tf_op jit(solution)/shard_map/square_sum/ppermute | solution.py:275
  46.1 4.0 %collective-permute-start.14 = (f32[8,256]{1,0:T(8,128)S(1)}, f32[8,256]{1,0:T(8,128)S(1)}, u32[]{:S(2)}, u32[]{:S(2)}) collective-permute-start(f32[8,256]{1,0:T(8,128)S(1)} %add.62), channel_id=1, source_target_pairs={{0,2},{1,3},{2,0},{3,1},{4,6},{5,7},{6,4},{7,5},{8,10},{9,11},{10,... | collective-permute-start | bytes 24584 | tf_op jit(solution)/shard_map/square_sum/ppermute | solution.py:277
  50.1 6.1 %collective-permute-start.15 = (f32[8,256]{1,0:T(8,128)S(1)}, f32[8,256]{1,0:T(8,128)S(1)}, u32[]{:S(2)}, u32[]{:S(2)}) collective-permute-start(f32[8,256]{1,0:T(8,128)S(1)} %add.63), channel_id=1, source_target_pairs={{0,7},{1,6},{2,5},{3,4},{4,3},{5,2},{6,1},{7,0},{8,15},{9,14},{10,... | collective-permute-start | bytes 24584 | tf_op jit(solution)/shard_map/square_sum/ppermute | solution.py:277
  58.5 20.8 %collective-permute-start.19 = (f32[3072,256]{1,0:T(8,128)S(1)}, f32[3072,256]{1,0:T(8,128)S(1)}, u32[]{:S(2)}, u32[]{:S(2)}) collective-permute-start(f32[3072,256]{1,0:T(8,128)S(1)} %constant_dynamic-update-slice_fusion.5), channel_id=1, source_target_pairs={{0,8},{8,0},{16,24},{24,16},{32,40},{40,32},{48,56},{56,48},{64,72... | collective-permute-start | bytes 9437192 | tf_op jit(solution)/shard_map/core_gather/ppermute | solution.py:249
  63.0 16.3 %copy-start = (f32[128,256]{1,0:T(8,128)S(1)}, f32[128,256]{1,0:T(8,128)}, u32[]{:S(2)}) copy-start(f32[128,256]{1,0:T(8,128)} %refs_8_.1) | copy-start | bytes 393220
  63.2 8.5 %collective-permute-start.17 = (f32[520,256]{1,0:T(8,128)S(1)}, f32[520,256]{1,0:T(8,128)S(1)}, u32[]{:S(2)}, u32[]{:S(2)}) collective-permute-start(f32[520,256]{1,0:T(8,128)S(1)} %get-tuple-element.49), channel_id=1, source_target_pairs={{0,48},{8,200},{16,0},{24,216},{32,16},{40,232},{48,32},{56,248},{... | collective-permute-start | bytes 1597448 | tf_op jit(solution)/shard_map/major_forward/ppermute | solution.py:249
  64.2 9.7 %collective-permute-start.16 = (f32[520,256]{1,0:T(8,128)S(1)}, f32[520,256]{1,0:T(8,128)S(1)}, u32[]{:S(2)}, u32[]{:S(2)}) collective-permute-start(f32[520,256]{1,0:T(8,128)S(1)} %get-tuple-element.50), channel_id=1, source_target_pairs={{0,16},{8,72},{16,32},{24,88},{32,48},{40,104},{48,0},{56,120},{64... | collective-permute-start | bytes 1597448 | tf_op jit(solution)/shard_map/major_forward/ppermute | solution.py:249
  64.7 8.1 %collective-permute-start.18 = (f32[8,256]{1,0:T(8,128)S(1)}, f32[8,256]{1,0:T(8,128)S(1)}, u32[]{:S(2)}, u32[]{:S(2)}) collective-permute-start(f32[8,256]{1,0:T(8,128)S(1)} %add.64), channel_id=1, source_target_pairs={{0,32},{8,136},{16,48},{24,152},{32,0},{40,168},{48,16},{56,184},{... | collective-permute-start | bytes 24584 | tf_op jit(solution)/shard_map/square_sum/ppermute | solution.py:249
  74.0 5.3 %collective-permute-start.21 = (f32[520,256]{1,0:T(8,128)S(1)}, f32[520,256]{1,0:T(8,128)S(1)}, u32[]{:S(2)}, u32[]{:S(2)}) collective-permute-start(f32[520,256]{1,0:T(8,128)S(1)} %pad_maximum_fusion.2.refs_4_), channel_id=1, source_target_pairs={{0,8},{8,0},{16,24},{24,16},{32,40},{40,32},{48,56},{56,48},{64,72... | collective-permute-start | bytes 1597448 | tf_op jit(solution)/shard_map/update/ppermute | solution.py:249
  77.1 2.3 %collective-permute-start.20 = (f32[512,256]{1,0:T(8,128)S(1)}, f32[512,256]{1,0:T(8,128)S(1)}, u32[]{:S(2)}, u32[]{:S(2)}) collective-permute-start(f32[512,256]{1,0:T(8,128)S(1)} %slice.82.refs_3_), channel_id=1, source_target_pairs={{0,8},{8,0},{16,24},{24,16},{32,40},{40,32},{48,56},{56,48},{64,72... | collective-permute-start | bytes 1572872 | tf_op jit(solution)/shard_map/update/ppermute | solution.py:249
